TPU v7x, 32 devices: a whole 2x2x4 slice. The times are simulated.
32 devices in a mesh: dp: 4 (over y, x), fsdp: 8 (over z, core).
Axes of the slice: x: 2, y: 2, z: 4, core: 2. Of those that a mesh axis runs over, the one named last changes fastest.
Arguments:
- latents: bfloat16 [32, 256, 768], P(('dp', 'fsdp')), may hold values from -6 to 6
- conditioning: bfloat16 [32, 768], P(('dp', 'fsdp')), may hold values from -6 to 6
- cotangent: bfloat16 [32, 256, 768], P(('dp', 'fsdp')), may hold values from -6 to 6
- latent_count: int32 [32], P(('dp', 'fsdp')), may hold values from 0 to 1, as said below
- ada_weight: bfloat16 [768, 4608], P('dp', 'fsdp'), may hold values from -0.21875 to 0.21875
- ada_bias: bfloat16 [4608], P('fsdp'), may hold values from -3 to 3
- qkv_weight: bfloat16 [768, 2304], P('dp', 'fsdp'), may hold values from -0.21875 to 0.21875
- qv_bias: bfloat16 [1536], P('fsdp'), may hold values from -3 to 3
- proj_weight: bfloat16 [768, 768], P('dp', 'fsdp'), may hold values from -0.875 to 0.875
- proj_bias: bfloat16 [768], P('fsdp'), may hold values from -3 to 3
- fc1_weight: bfloat16 [768, 3072], P('dp', 'fsdp'), may hold values from -0.21875 to 0.21875
- fc1_bias: bfloat16 [3072], P('fsdp'), may hold values from -3 to 3
- fc2_weight: bfloat16 [3072, 768], P('dp', 'fsdp'), may hold values from -0.109375 to 0.109375
- fc2_bias: bfloat16 [768], P('fsdp'), may hold values from -3 to 3
Outputs:
- block_out: bfloat16 [32, 256, 768], P(('dp', 'fsdp'))
- latents_grad: bfloat16 [32, 256, 768], P(('dp', 'fsdp'))
- conditioning_grad: float32 [32, 768], P(('dp', 'fsdp'))
- ada_weight_grad: float32 [768, 4608], P('dp', 'fsdp')
- ada_bias_grad: float32 [4608], P('fsdp')
- qkv_weight_grad: float32 [768, 2304], P('dp', 'fsdp')
- qv_bias_grad: float32 [1536], P('fsdp')
- proj_weight_grad: float32 [768, 768], P('dp', 'fsdp')
- proj_bias_grad: float32 [768], P('fsdp')
- fc1_weight_grad: float32 [768, 3072], P('dp', 'fsdp')
- fc1_bias_grad: float32 [3072], P('fsdp')
- fc2_weight_grad: float32 [3072, 768], P('dp', 'fsdp')
- fc2_bias_grad: float32 [768], P('fsdp')
Inputs may be any that keep to these rules, and one draw needn't show every extreme that they name: `latent_count`: exactly 8 slots hold no latent.
All inputs are finite; a program needn't handle non-finite values.
Results may differ from a plain program's by a relative error of at most 0.015.
The roundings to bfloat16 on the way count: a program that leaves them out, or rounds other values in their place, can miss the bound.
Values may be sent and summed in bfloat16 or wider, within the bound.
A program may use at most 128 MiB of HBM per device.

v0:
```python
import functools
import jax
import jax.numpy as jnp
from jax import lax
from jax.sharding import PartitionSpec as P
from jax.experimental import pallas as pl
from jax.experimental.pallas import tpu as pltpu

MESH_IDS = pl.DeviceIdType.MESH
D = 768
HEADS = 12
HEAD = 64
FF = 3072

highest = lax.Precision.HIGHEST
bfloat = jnp.bfloat16


def place(dp_index, z_index, core):
    return (dp_index, z_index * 2 + core)


def z_order(size):
    steps = [0]
    for distance in range(1, size // 2 + 1):
        steps.append(distance)
        if size - distance != distance:
            steps.append(size - distance)
    return steps


def enter_barrier(partners):
    barrier = pltpu.get_barrier_semaphore()
    for partner in partners:
        pl.semaphore_signal(barrier, inc=1, device_id=partner, device_id_type=MESH_IDS)
    pl.semaphore_wait(barrier, len(partners))


def positions(rows, depth):
    dp = lax.axis_index("dp")
    column = lax.axis_index("fsdp")
    z, core = column // 2, column % 2
    others = [(dp ^ 1), (dp ^ 2)] if rows == 4 else [(dp + step) % rows for step in range(1, rows)]
    partners = [place(dp, z, 1 - core)]
    partners += [place(other, z, core) for other in others]
    partners += [place(dp, (z + step) % depth, core) for step in z_order(depth)[1:]]
    return dp, z, core, others, partners


def block_of(array, line, row, shape, turned):
    if len(array.shape) == 4:
        return array.at[line, row]
    high, wide = (line, row) if turned else (row, line)
    height, width = shape
    return array.at[
        pl.ds(pl.multiple_of(high * height, height), height),
        pl.ds(pl.multiple_of(wide * width, width), width),
    ]


def whole_shape(shape, turned, rows, columns):
    height, width = shape
    if width % 128 == 0 and height % 32 == 0:
        return (columns * height, rows * width) if turned else (rows * height, columns * width)
    return (columns, rows, height, width)


def gather_kernel(rows, depth, *refs):
    shards, outs = refs[:3], refs[3:6]
    own_sems, send_sems, recv_sems = refs[6:]
    dp, z, core, others, partners = positions(rows, depth)
    sibling = place(dp, z, 1 - core)
    enter_barrier(partners)
    sends = []

    def slot_of(part, line, row):
        return block_of(outs[part], line, row, shards[part].shape, part == 2)

    def half_of(ref, part, which):
        half = shards[part].shape[0] // 2
        return ref.at[pl.ds(which * half, half)]

    def send(line, row, target, which=None, own=False):
        for part in range(3):
            destination = slot_of(part, line, row)
            source = shards[part] if own else destination
            if which is not None:
                source, destination = half_of(source, part, which), half_of(destination, part, which)
            copy = pltpu.make_async_remote_copy(
                src_ref=source,
                dst_ref=destination,
                send_sem=send_sems.at[len(sends)],
                recv_sem=recv_sems.at[which or 0, part, line, row],
                device_id=target,
                device_id_type=MESH_IDS,
            )
            copy.start()
            sends.append(copy)

    def arrive(line, row, which=None):
        for part in range(3):
            destination = slot_of(part, line, row)
            if which is not None:
                destination = half_of(destination, part, which)
            pltpu.make_async_remote_copy(
                src_ref=destination,
                dst_ref=destination,
                send_sem=send_sems.at[0],
                recv_sem=recv_sems.at[which or 0, part, line, row],
                device_id=sibling,
                device_id_type=MESH_IDS,
            ).wait_recv()

    own = z * 2 + core
    steps = z_order(depth)
    lines = [((z - step) % depth) * 2 + core for step in steps]
    for other in others:
        send(own, dp, place(other, z, core), own=True)
    for step in steps[1:]:
        send(own, dp, place(dp, (z + step) % depth, core), own=True)
    send(own, dp, sibling, own=True)
    keeps = [
        pltpu.make_async_copy(shards[part], slot_of(part, own, dp), own_sems.at[part])
        for part in range(3)
    ]
    for keep in keeps:
        keep.start()
    for turn in range(depth + 2):
        if 0 < turn < depth:
            line = lines[turn]
            arrive(line, dp)
            for other in others:
                send(line, dp, place(other, z, core))
            send(line, dp, sibling)
        if 1 <= turn <= depth:
            line = lines[turn - 1]
            for position, other in enumerate(others):
                arrive(line, other)
                if rows == 4:
                    send(line, other, place(others[1 - position], z, core), which=position)
                send(line, other, sibling)
        if turn >= 2 and rows == 4:
            line = lines[turn - 2]
            arrive(line, dp ^ 3, 0)
            arrive(line, dp ^ 3, 1)
            send(line, dp ^ 3, sibling)
    for line in lines:
        for row in range(rows):
            arrive(line + 1 - 2 * core, (dp + row) % rows)
    for keep in keeps:
        keep.wait()
    for copy in sends:
        copy.wait_send()


def gather_shards(shards, rows, columns):
    depth = columns // 2
    count = (depth - 1) + depth * rows + depth * (rows - 1) + (2 * depth if rows == 4 else 0)
    shapes = [
        whole_shape(shard.shape, part == 2, rows, columns) for part, shard in enumerate(shards)
    ]
    return pl.pallas_call(
        functools.partial(gather_kernel, rows, depth),
        out_shape=[jax.ShapeDtypeStruct(shape, bfloat) for shape in shapes],
        in_specs=[pl.BlockSpec(memory_space=pl.ANY)] * 3,
        out_specs=[pl.BlockSpec(memory_space=pl.ANY)] * 3,
        scratch_shapes=[
            pltpu.SemaphoreType.DMA((3,)),
            pltpu.SemaphoreType.DMA((3 * count,)),
            pltpu.SemaphoreType.DMA((2, 3, columns, rows)),
        ],
        compiler_params=pltpu.CompilerParams(collective_id=0, has_side_effects=True),
        name="gather_shards",
    )(*shards)


def scatter_kernel(rows, depth, *refs):
    grads, outs = refs[:3], refs[3:6]
    helds, pairs_in, planes_in, crosses_in, alongs_in = (
        refs[6 + 3 * kind : 9 + 3 * kind] for kind in range(5)
    )
    (
        load_sems, pair_send, pair_recv, plane_send, plane_recv,
        cross_send, cross_recv, along_send, along_recv,
    ) = refs[21:]
    dp, z, core, others, partners = positions(rows, depth)
    sibling = place(dp, z, 1 - core)
    targets = [dp ^ 3, dp ^ 1, dp ^ 2, dp] if rows == 4 else others + [dp]
    steps = z_order(depth)[::-1]
    enter_barrier(partners)
    waits = []

    def remote(source, destination, send_sem, recv_sem, target):
        copy = pltpu.make_async_remote_copy(
            src_ref=source, dst_ref=destination, send_sem=send_sem, recv_sem=recv_sem,
            device_id=target, device_id_type=MESH_IDS,
        )
        copy.start()
        waits.append(copy)
        return copy

    def add(first, others_in, length, target):
        chunk = 48 if length % 48 == 0 else 16

        @pl.loop(0, length // chunk)
        def _(index):
            piece = pl.ds(pl.multiple_of(index * chunk, chunk), chunk)
            total = first[piece, :].astype(jnp.float32)
            for other in others_in:
                total = total + other[piece, :].astype(jnp.float32)
            target[piece, :] = total.astype(target.dtype)

    lines = [(z + step) % depth for step in steps]
    pairs, loads, planes, crosses, alongs = {}, {}, {}, {}, {}
    for turn, line in enumerate(lines):
        for slot, target in enumerate(targets):
            for part in range(3):
                key = (part, turn, slot)
                shape = outs[part].shape
                pairs[key] = remote(
                    block_of(grads[part], line * 2 + 1 - core, target, shape, part == 2),
                    pairs_in[part].at[turn, slot], pair_send.at[key], pair_recv.at[key], sibling)
                loads[key] = pltpu.make_async_copy(
                    block_of(grads[part], line * 2 + core, target, shape, part == 2),
                    helds[part].at[turn, slot], load_sems.at[key])
                loads[key].start()
    last = len(targets) - 1
    for turn in range(depth + 2):
        if turn < depth:
            for slot in range(len(targets)):
                for part in range(3):
                    key = (part, turn, slot)
                    height = outs[part].shape[0]
                    half = height // 2
                    loads[key].wait()
                    pairs[key].wait_recv()
                    here = helds[part].at[turn, slot]
                    add(here, [pairs_in[part].at[turn, slot]], height, here)
                    if rows == 4 and slot == 0:
                        for position in range(2):
                            key = (part, turn, position)
                            crosses[key] = remote(
                                helds[part].at[turn, 0, pl.ds((1 - position) * half, half)],
                                crosses_in[part].at[turn, position],
                                cross_send.at[key], cross_recv.at[key],
                                place(others[position], z, core))
                    if rows != 4 and slot < last:
                        planes[key] = remote(
                            here, planes_in[part].at[turn, slot], plane_send.at[key],
                            plane_recv.at[key], place(targets[slot], z, core))
        if rows == 4 and 1 <= turn <= depth:
            now = turn - 1
            for position in range(2):
                for part in range(3):
                    half = outs[part].shape[0] // 2
                    crosses[part, now, 1 - position].wait_recv()
                    piece = helds[part].at[now, 1 + position, pl.ds(position * half, half)]
                    add(piece, [crosses_in[part].at[now, 1 - position]], half, piece)
                    key = (part, now, position)
                    planes[key] = remote(
                        helds[part].at[now, 1 + position], planes_in[part].at[now, position],
                        plane_send.at[key], plane_recv.at[key],
                        place(others[position], z, core))
        if turn >= 2:
            now = turn - 2
            for part in range(3):
                for slot in range(len(others)):
                    planes[part, now, slot].wait_recv()
                here = helds[part].at[now, last]
                arrived = [planes_in[part].at[now, slot] for slot in range(len(others))]
                add(here, arrived, outs[part].shape[0], here)
                if now < depth - 1:
                    key = (part, now)
                    alongs[key] = remote(
                        here, alongs_in[part].at[now], along_send.at[key], along_recv.at[key],
                        place(dp, lines[now], core))
    for part in range(3):
        for now in range(depth - 1):
            alongs[part, now].wait_recv()
        arrived = [alongs_in[part].at[now] for now in range(depth - 1)]
        add(helds[part].at[depth - 1, last], arrived, outs[part].shape[0], outs[part])
    for copy in waits:
        copy.wait_send()


def scatter_shards(grads, shapes, rows, columns):
    depth = columns // 2
    peers = 2 if rows == 4 else rows - 1
    dma = pltpu.SemaphoreType.DMA
    buffers = []
    for lead in ((depth, rows), (depth, rows), (depth, peers), (depth, 2), (depth - 1,)):
        for height, width in shapes:
            if lead == (depth, 2) and len(buffers) >= 9:
                height = height // 2 if rows == 4 else 16
            buffers.append(pltpu.VMEM(lead + (height, width), bfloat))
    return pl.pallas_call(
        functools.partial(scatter_kernel, rows, depth),
        out_shape=[jax.ShapeDtypeStruct(shape, jnp.float32) for shape in shapes],
        in_specs=[pl.BlockSpec(memory_space=pl.ANY)] * 3,
        out_specs=[pl.BlockSpec(memory_space=pltpu.VMEM)] * 3,
        scratch_shapes=buffers + [
            dma((3, depth, rows)), dma((3, depth, rows)), dma((3, depth, rows)),
            dma((3, depth, peers)), dma((3, depth, peers)),
            dma((3, depth, 2)), dma((3, depth, 2)),
            dma((3, depth - 1)), dma((3, depth - 1)),
        ],
        compiler_params=pltpu.CompilerParams(
            collective_id=1, has_side_effects=True, vmem_limit_bytes=50 * 2**20),
        name="scatter_shards",
    )(*grads)


def normalize_rows(values):
    center = jnp.mean(values, axis=-1, keepdims=True)
    spread = jnp.mean(jnp.square(values - center), axis=-1, keepdims=True)
    inverse = lax.rsqrt(spread + 1e-06)
    return ((values - center) * inverse, inverse)


def norm_backward(grad_normed, normed, inverse):
    centered = grad_normed - jnp.mean(grad_normed, axis=-1, keepdims=True)
    return inverse * (centered - normed * jnp.mean(grad_normed * normed, axis=-1, keepdims=True))


def contract_rows(left_rows, right_rows):
    return lax.dot_general(
        left_rows, right_rows, (((0,), (0,)), ((), ())), preferred_element_type=jnp.float32
    )


def contract_exact(left_rows, right_rows):
    return lax.dot_general(left_rows, right_rows, (((0,), (0,)), ((), ())), precision=highest)


def against_weight(grad_rows, weight):
    return lax.dot_general(
        grad_rows, weight, (((1,), (1,)), ((), ())), preferred_element_type=jnp.float32
    )


def pick(mixed, columns, kind):
    width = mixed.shape[1] // columns
    edge = 3 * width // 4
    low, high = (0, edge) if kind == 0 else (edge, width)
    return jnp.concatenate(
        [mixed[:, block * width + low : block * width + high] for block in range(columns)], axis=1
    )


def spread(rows_in, columns, kind):
    width = rows_in.shape[1] // columns
    rest = width // 3 if kind == 0 else 3 * width
    zeros = jnp.zeros((rows_in.shape[0], rest), rows_in.dtype)
    pieces = []
    for block in range(columns):
        piece = rows_in[:, block * width : (block + 1) * width]
        pieces += [piece, zeros] if kind == 0 else [zeros, piece]
    return jnp.concatenate(pieces, axis=1)


def layer(latent_rows, cond_act, live, cot_rows, modulation, weights, biases, columns):
    mixed_weight, fc1_weight, fc2_turned = weights
    qv_bias, proj_bias, fc1_bias, fc2_bias = biases
    length = latent_rows.shape[0]
    rows_wide = latent_rows.astype(jnp.float32)
    shift_one, scale_one, gate_one, shift_two, scale_two, gate_two = jnp.split(
        modulation, 6, axis=-1
    )
    normed_one, inverse_one = normalize_rows(rows_wide)
    hidden_one = (normed_one * (1.0 + scale_one) + shift_one).astype(bfloat)
    qkv_bias = jnp.concatenate([qv_bias[:D], jnp.zeros((D,), jnp.float32), qv_bias[D:]])
    projected = (
        pick(jnp.dot(hidden_one, mixed_weight, preferred_element_type=jnp.float32), columns, 0)
        + qkv_bias
    ).astype(bfloat)
    queries = projected[:, :D].reshape(length, HEADS, HEAD)
    key_rows = projected[:, D : 2 * D].reshape(length, HEADS, HEAD)
    values = projected[:, 2 * D :].reshape(length, HEADS, HEAD)
    scale_factor = HEAD ** (-0.5)
    scores = (
        jnp.einsum("qhe,khe->hqk", queries, key_rows, preferred_element_type=jnp.float32)
        * scale_factor
    )
    row_max = jnp.max(scores, axis=-1, keepdims=True)
    shifted = jnp.exp(scores - row_max)
    row_total = jnp.sum(shifted, axis=-1, keepdims=True)
    exact_probability = shifted / row_total
    probability = exact_probability.astype(bfloat)
    attended = jnp.einsum("hqk,khe->qhe", probability, values, preferred_element_type=jnp.float32)
    attended = attended.reshape(length, D).astype(bfloat)
    branch = pick(jnp.dot(attended, mixed_weight, preferred_element_type=jnp.float32), columns, 1)
    branch = branch + proj_bias
    middle = rows_wide + gate_one * branch
    normed_two, inverse_two = normalize_rows(middle)
    hidden_two = (normed_two * (1.0 + scale_two) + shift_two).astype(bfloat)
    pre_gelu = jnp.dot(hidden_two, fc1_weight, preferred_element_type=jnp.float32) + fc1_bias
    activated, gelu_pull = jax.vjp(
        lambda argument: jax.nn.gelu(argument, approximate=True), pre_gelu
    )
    activated = activated.astype(bfloat)
    mlp_out = against_weight(activated, fc2_turned) + fc2_bias
    block_out = (live * (middle + gate_two * mlp_out)).astype(bfloat)

    grad_out = live * cot_rows.astype(jnp.float32)
    gate_two_grad = jnp.sum(grad_out * mlp_out, axis=0, keepdims=True)
    grad_mlp = (gate_two * grad_out).astype(bfloat)
    fc2_bias_grad = jnp.sum(grad_mlp.astype(jnp.float32), axis=0)
    grad_act = jnp.dot(grad_mlp, fc2_turned, preferred_element_type=jnp.float32)
    grad_pre = gelu_pull(grad_act)[0].astype(bfloat)
    fc1_bias_grad = jnp.sum(grad_pre.astype(jnp.float32), axis=0)
    grad_hidden_two = against_weight(grad_pre, fc1_weight)
    shift_two_grad = jnp.sum(grad_hidden_two, axis=0, keepdims=True)
    scale_two_grad = jnp.sum(grad_hidden_two * normed_two, axis=0, keepdims=True)
    grad_middle = grad_out + norm_backward(
        grad_hidden_two * (1.0 + scale_two), normed_two, inverse_two
    )
    gate_one_grad = jnp.sum(grad_middle * branch, axis=0, keepdims=True)
    grad_branch = (gate_one * grad_middle).astype(bfloat)
    proj_bias_grad = jnp.sum(grad_branch.astype(jnp.float32), axis=0)
    spread_branch = spread(grad_branch, columns, 1)
    grad_attended = (
        against_weight(spread_branch, mixed_weight).astype(bfloat).reshape(length, HEADS, HEAD)
    )
    grad_prob = jnp.einsum(
        "qhe,khe->hqk", grad_attended, values, preferred_element_type=jnp.float32
    )
    inner_sum = jnp.sum(exact_probability * grad_prob, axis=-1, keepdims=True)
    grad_scores = (exact_probability * (grad_prob - inner_sum)).astype(bfloat)
    grad_queries = (
        jnp.einsum("hqk,khe->qhe", grad_scores, key_rows, preferred_element_type=jnp.float32)
        * scale_factor
    )
    grad_keys = (
        jnp.einsum("hqk,qhe->khe", grad_scores, queries, preferred_element_type=jnp.float32)
        * scale_factor
    )
    grad_values = jnp.einsum(
        "hqk,qhe->khe", probability, grad_attended, preferred_element_type=jnp.float32
    )
    grad_projected = jnp.concatenate(
        [
            grad_queries.reshape(length, D),
            grad_keys.reshape(length, D),
            grad_values.reshape(length, D),
        ],
        axis=1,
    ).astype(bfloat)
    summed = jnp.sum(grad_projected.astype(jnp.float32), axis=0)
    qv_bias_grad = jnp.concatenate([summed[:D], summed[2 * D :]])
    spread_projected = spread(grad_projected, columns, 0)
    grad_hidden_one = against_weight(spread_projected, mixed_weight)
    shift_one_grad = jnp.sum(grad_hidden_one, axis=0, keepdims=True)
    scale_one_grad = jnp.sum(grad_hidden_one * normed_one, axis=0, keepdims=True)
    latent_grad = (
        grad_middle + norm_backward(grad_hidden_one * (1.0 + scale_one), normed_one, inverse_one)
    ).astype(bfloat)
    mod_grad = jnp.concatenate(
        [
            shift_one_grad,
            scale_one_grad,
            gate_one_grad,
            shift_two_grad,
            scale_two_grad,
            gate_two_grad,
        ],
        axis=-1,
    )
    weight_grads = (
        contract_rows(
            jnp.concatenate([hidden_one, attended]),
            jnp.concatenate([spread_projected, spread_branch]),
        ).astype(bfloat),
        contract_rows(hidden_two, grad_pre).astype(bfloat),
        contract_rows(grad_mlp, activated).astype(bfloat),
    )
    bias_grads = (qv_bias_grad, proj_bias_grad, fc1_bias_grad, fc2_bias_grad)
    return block_out, latent_grad, mod_grad, weight_grads, bias_grads


def flatten_blocks(blocks, turned):
    if blocks.ndim == 2:
        return blocks
    columns, rows, height, width = blocks.shape
    if turned:
        return blocks.transpose(0, 2, 1, 3).reshape(columns * height, rows * width)
    return blocks.transpose(1, 2, 0, 3).reshape(rows * height, columns * width)


def cut_blocks(whole, shape, turned, rows, columns):
    if len(whole_shape(shape, turned, rows, columns)) == 2:
        return whole
    height, width = shape
    if turned:
        return whole.reshape(columns, height, rows, width).transpose(0, 2, 1, 3)
    return whole.reshape(rows, height, columns, width).transpose(2, 0, 1, 3)


def per_device(
    latents,
    conditioning,
    cotangent,
    latent_count,
    ada_weight,
    ada_bias,
    qkv_weight,
    qv_bias,
    proj_weight,
    proj_bias,
    fc1_weight,
    fc1_bias,
    fc2_weight,
    fc2_bias,
):
    rows, columns = lax.axis_size("dp"), lax.axis_size("fsdp")
    row_index = lax.axis_index("dp")
    live = latent_count[0].astype(jnp.float32)
    depth = ada_weight.shape[0]
    mod_width = ada_weight.shape[1]
    own_biases = (qv_bias, proj_bias, fc1_bias, fc2_bias)
    widths = [bias.shape[0] for bias in own_biases]
    cuts = [mod_width + sum(widths[:place]) for place in range(len(widths))]

    cond_row = conditioning.astype(jnp.float32)
    cond_act = jax.nn.silu(cond_row).astype(bfloat)
    cond_all = lax.all_gather(cond_act, ("dp", "fsdp"), axis=0, tiled=True)
    cond_owned = lax.dynamic_slice_in_dim(cond_all, row_index * depth, depth, 1)
    partial = jnp.dot(cond_owned, ada_weight, preferred_element_type=jnp.float32)
    mod_rows = lax.psum_scatter(partial, "dp", scatter_dimension=0, tiled=True)
    mod_rows = mod_rows + ada_bias.astype(jnp.float32)
    bias_row = jnp.concatenate(own_biases).astype(jnp.float32)
    payload = jnp.concatenate(
        [mod_rows, jnp.broadcast_to(bias_row, (columns, bias_row.shape[0]))], axis=1
    )
    arrived = lax.all_to_all(payload, "fsdp", split_axis=0, concat_axis=0, tiled=True)
    modulation = arrived[:, :mod_width].reshape(1, -1)
    biases = tuple(
        arrived[:, cut : cut + width].reshape(-1) for cut, width in zip(cuts, widths)
    )

    qkv_width = qkv_weight.shape[1]
    shards = (
        jnp.concatenate([qkv_weight, proj_weight], axis=1),
        fc1_weight,
        fc2_weight.T,
    )
    shapes = [shard.shape for shard in shards]
    blocks = gather_shards(shards, rows, columns)
    weights = [flatten_blocks(block, part == 2) for part, block in enumerate(blocks)]
    block_out, latent_grad, mod_grad, weight_grads, bias_grads = layer(
        latents[0], cond_act, live, cotangent[0], modulation, weights, biases, columns
    )
    grads = [
        cut_blocks(grad, shapes[part], part == 2, rows, columns)
        for part, grad in enumerate(weight_grads)
    ]
    mixed_grad, fc1_grad, fc2_turned_grad = scatter_shards(grads, shapes, rows, columns)
    qkv_grad, proj_grad = mixed_grad[:, :qkv_width], mixed_grad[:, qkv_width:]
    fc2_grad = fc2_turned_grad.T

    leaving = jnp.concatenate(
        [mod_grad.reshape(columns, -1)] + [grad.reshape(columns, -1) for grad in bias_grads], axis=1
    )
    group_rows = lax.all_to_all(leaving, "fsdp", split_axis=0, concat_axis=0, tiled=True)
    all_rows = lax.all_gather(group_rows, "dp", axis=0, tiled=True)
    mod_owned = all_rows[:, :mod_width]
    ada_grad = contract_exact(cond_owned.astype(jnp.float32), mod_owned)
    sums = jnp.sum(all_rows, axis=0)
    ada_bias_grad = sums[:mod_width]
    bias_sums = [sums[cut : cut + width] for cut, width in zip(cuts, widths)]
    back = lax.dot_general(
        mod_owned, ada_weight.astype(jnp.float32), (((1,), (1,)), ((), ())), precision=highest
    )
    back = lax.psum_scatter(
        back.reshape(rows, columns, depth), "fsdp", scatter_dimension=1, tiled=True
    )
    back = lax.all_to_all(
        back.reshape(rows, depth), "dp", split_axis=0, concat_axis=0, tiled=True
    ).reshape(1, -1)
    cond_grad = jax.vjp(jax.nn.silu, cond_row)[1](back)[0]
    return (
        block_out[None],
        latent_grad[None],
        cond_grad,
        ada_grad,
        ada_bias_grad,
        qkv_grad,
        bias_sums[0],
        proj_grad,
        bias_sums[1],
        fc1_grad,
        bias_sums[2],
        fc2_grad,
        bias_sums[3],
    )


def solution(mesh):
    in_specs = (
        P(("dp", "fsdp"), None, None),
        P(("dp", "fsdp"), None),
        P(("dp", "fsdp"), None, None),
        P(("dp", "fsdp")),
        P("dp", "fsdp"),
        P("fsdp"),
        P("dp", "fsdp"),
        P("fsdp"),
        P("dp", "fsdp"),
        P("fsdp"),
        P("dp", "fsdp"),
        P("fsdp"),
        P("dp", "fsdp"),
        P("fsdp"),
    )
    out_specs = (
        P(("dp", "fsdp"), None, None),
        P(("dp", "fsdp"), None, None),
        P(("dp", "fsdp"), None),
        P("dp", "fsdp"),
        P("fsdp"),
        P("dp", "fsdp"),
        P("fsdp"),
        P("dp", "fsdp"),
        P("fsdp"),
        P("dp", "fsdp"),
        P("fsdp"),
        P("dp", "fsdp"),
        P("fsdp"),
    )
    return jax.shard_map(
        per_device, mesh=mesh, in_specs=in_specs, out_specs=out_specs, check_vma=False
    )
```

profile of v0, /device:TPU:0, one launch (start us, length us, event | category | flops | bytes accessed | tf_op | source)
XLA Modules:
  0.0 363.2 jit_solution(4353695455945252596)
XLA Ops:
  7.3 1.4 convert_bitcast_fusion.1
  8.6 43.6 %all-gather.1 = bf16[32,1,768]{2,1,0:T(2,128)(2,1)S(1)} all-gather(bf16[1,1,768]{2,1,0:T(2,128)(2,1)S(1)} %get-tuple-element.46), channel_id=1, replica_groups=mesh['dp'=4,'fsdp'=8] {'dp','fsdp'}, dimensions={0}, use_global_device_ids=true | all-gather | bytes 50688 | tf_op jit(solution)/shard_map/all_gather | solution.py:525
  52.3 0.8 fusion.55
  53.8 0.7 convert_element_type.103
  54.5 1.1 convert_reduce_fusion.2
  55.7 1.2 fusion.33
  56.9 1.2 dynamic-slice.1
  58.2 1.3 dynamic-slice.3
  60.1 0.8 maximum_convert_fusion
  61.0 1.7 pad_maximum_fusion.2.refs_0_
  62.6 68.2 %gather_shards.1 = (bf16[768,3072]{1,0:T(8,128)(2,1)}, bf16[768,3072]{1,0:T(8,128)(2,1)}, bf16[768,3072]{1,0:T(8,128)(2,1)}) custom-call(bf16[192,384]{1,0:T(8,128)(2,1)} %pad_maximum_fusion.2.refs_0_, bf16[192,384]{1,0:T(8,128)(2,1)} %refs_1_.1, bf16[96,768]{1,0:T(8,128)(2,1)} %bitcast.159), custom_call_target="tpu_custom_call" | custom-call | tf_op jit(solution)/shard_map/gather_shards/pallas_call | solution.py:162
  130.9 0.7 dynamic-slice_add_fusion
  132.3 6.4 %all-to-all-start = ((f32[8,1,1344]{2,1,0:T(1,128)}), f32[8,1,1344]{2,1,0:T(1,128)S(1)}, u32[]{:S(2)}, u32[]{:S(2)}) async-start(f32[8,1,1344]{2,1,0:T(1,128)} %all_to_all.20), calls=%async_computation | async-start | bytes 90112 | tf_op jit(solution)/shard_map/all_to_all | solution.py:534
  139.3 5.1 %all-to-all-done = f32[8,1,1344]{2,1,0:T(1,128)S(1)} async-done(((f32[8,1,1344]{2,1,0:T(1,128)}), f32[8,1,1344]{2,1,0:T(1,128)S(1)}, u32[]{:S(2)}, u32[]{:S(2)}) %all-to-all-start) | async-done | bytes 43040 | tf_op jit(solution)/shard_map/all_to_all | solution.py:534
  147.6 3.8 %fusion.73 = f32[256,3072]{1,0:T(8,128)S(1)} fusion(bf16[256,768]{1,0:T(8,128)(2,1)S(1)} %fusion.26, bf16[768,3072]{1,0:T(8,128)(2,1)} %get-tuple-element.19), kind=kOutput, calls=%fused_computation.171 | convolution fusion | flops 1207959552 | bytes 8257536 | tf_op jit(solution)/shard_map/dot_general | solution.py:373
  151.4 1.6 fusion.65
  153.1 3.2 concatenate.57
  157.1 2.8 fusion.72
  160.0 2.4 convolution_convert_fusion.5
  163.1 1.4 fusion.74
  165.9 0.9 fusion.62
  167.1 0.7 add.142
  167.8 4.0 %convolution_add_fusion = f32[256,3072]{1,0:T(8,128)S(1)} fusion(bf16[768,3072]{1,0:T(8,128)(2,1)} %get-tuple-element.20, f32[3072]{0:T(1024)S(1)} %add.142, f32[256,768]{1,0:T(8,128)S(1)} %get-tuple-element.45, f32[768]{0:T(1024)} %get-tuple-element.36, f32[768]{0:T(1024)} %get-tuple-element.37, f32[256]{0:T(256)S(1)} %add_rsqrt_fusion, ...), kind=kOutput, calls=%fused_computation.6 | convolution fusion | flops 1209729024 | bytes 8671232 | tf_op jit(solution)/shard_map/dot_general | solution.py:396
  171.9 8.2 %convert_reduce_fusion = (f32[3072]{0:T(1024)}, bf16[256,3072]{1,0:T(8,128)(2,1)S(1)}) fusion(f32[256,3072]{1,0:T(8,128)S(1)} %convolution_add_fusion, bf16[768,3072]{1,0:T(8,128)(2,1)} %get-tuple-element.21, bf16[1,256,768]{2,1,0:T(8,128)(2,1)S(1)} %copy-done.45, f32[]{:T(128)} %bitcast, f32[768]{0:T(1024)S(1)} %copy-done.43), kind=kOutput, calls=%fused_computation.17 | convolution fusion | flops 1226044416 | bytes 9845764 | tf_op jit(solution)/shard_map/dot_general | solution.py:408
  180.0 1.2 copy-done.6
  181.3 3.0 multiply_reduce_fusion.2
  184.4 7.4 %convert_reduce_fusion.3 = (f32[768]{0:T(1024)}, f32[768]{0:T(1024)}, bf16[1,256,768]{2,1,0:T(8,128)(2,1)}, f32[768]{0:T(1024)}, bf16[256,768]{1,0:T(8,128)(2,1)S(1)}, /*index=5*/f32[256,768]{1,0:T(8,128)}) fusion(bf16[1,256,768]{2,1,0:T(8,128)(2,1)S(1)} %copy-done.45, f32[]{:T(128)} %bitcast, f32[768]{0:T(1024)S(1)} %copy-done.43, ...), kind=kOutput, calls=%fused_computation.64 | convolution fusion | flops 1219950336 | bytes 11428868 | tf_op jit(solution)/shard_map/dot_general | solution.py:336
  195.4 0.7 constant_dynamic-update-slice_fusion.9
  202.4 5.0 %convolution_convert_fusion.4 = bf16[256,768]{1,0:T(8,128)(2,1)} fusion(bf16[256,3072]{0,1:T(8,128)(2,1)} %constant_dynamic-update-slice_fusion, bf16[768,3072]{1,0:T(8,128)(2,1)} %get-tuple-element.19), kind=kOutput, calls=%fused_computation.32 | convolution fusion | flops 1208156160 | bytes 6684672 | tf_op jit(solution)/shard_map/dot_general | solution.py:336
  207.4 1.2 copy.97
  208.6 2.7 multiply_reduce_fusion
  214.3 1.9 copy.103
  216.2 5.3 %convolution_convert_fusion.1.refs_1_ = bf16[768,3072]{1,0:T(8,128)(2,1)} fusion(bf16[256,3072]{1,0:T(8,128)(2,1)} %copy-done.6, f32[256,768]{1,0:T(8,128)S(1)} %get-tuple-element.45, f32[768]{0:T(1024)S(1)} %copy-done.15, f32[768]{0:T(1024)S(1)} %copy-done.17, f32[256]{0:T(256)S(1)} %copy-done.37, f32[256]{0:T(256)S(1)} %copy-done.29), kind=kOutput, calls=%fused_computation.2 | convolution fusion | flops 1211301888 | bytes 7086080 | tf_op jit(solution)/shard_map/dot_general | solution.py:326
  221.6 3.9 %convolution_convert_fusion.refs_2_ = bf16[768,3072]{1,0:T(8,128)(2,1)} fusion(bf16[1,256,768]{2,1,0:T(8,128)(2,1)S(1)} %copy-done.46, f32[]{:T(128)} %bitcast, f32[768]{0:T(1024)S(1)} %copy-done.44, f32[256,3072]{1,0:T(8,128)S(1)} %copy-done.48), kind=kOutput, calls=%fused_computation.1 | convolution fusion | flops 1218183168 | bytes 8260612 | tf_op jit(solution)/shard_map/dot_general | solution.py:326
  226.5 1.7 fusion.32
  228.3 1.1 multiply_reduce_fusion.3
  230.7 3.3 all-to-all-start.1
  234.1 6.7 %convolution_convert_fusion.2.refs_0_ = bf16[768,3072]{1,0:T(8,128)(2,1)} fusion(bf16[256,3072]{0,1:T(8,128)(2,1)} %constant_dynamic-update-slice_fusion, bf16[256,3072]{0,1:T(8,128)(2,1)} %copy-done.30, bf16[256,768]{1,0:T(8,128)(2,1)S(1)} %copy-done.12, bf16[256,768]{1,0:T(8,128)(2,1)S(1)} %copy-done.9), kind=kOutput, calls=%fused_computation.3 | convolution fusion | flops 2426142720 | bytes 8650752 | tf_op jit(solution)/shard_map/dot_general | solution.py:326
  240.8 66.5 %scatter_shards.1 = (f32[192,384]{1,0:T(8,128)S(1)}, f32[192,384]{1,0:T(8,128)S(1)}, f32[96,768]{1,0:T(8,128)S(1)}) custom-call(bf16[768,3072]{1,0:T(8,128)(2,1)} %convolution_convert_fusion.2.refs_0_, bf16[768,3072]{1,0:T(8,128)(2,1)} %convolution_convert_fusion.1.refs_1_, bf16[768,3072]{1,0:T(8,128)(2,1)} %convolution_convert_fusion.refs_2_), custom_call_target="tpu_custom_call" | custom-call | tf_op jit(solution)/shard_map/scatter_shards/pallas_call | solution.py:296
  307.2 0.7 slice.233
  308.0 8.7 %all-gather = f32[32,1,1344]{2,1,0:T(1,128)S(1)} all-gather(f32[8,1,1344]{2,1,0:T(1,128)S(1)} %all-to-all-done.1), channel_id=2, replica_groups=mesh['dp'=4,'fsdp'=8] {'dp'}, dimensions={0}, use_global_device_ids=true | all-gather | bytes 215040 | tf_op jit(solution)/shard_map/all_gather | solution.py:564
  317.1 1.2 fusion.52
  318.4 25.9 %all-reduce.1 = f32[4,8,192]{2,0,1:T(4,128)S(1)} all-reduce(f32[4,8,192]{2,0,1:T(4,128)S(1)} %copy.101), channel_id=4, replica_groups=mesh['dp'=4,'fsdp'=8] {'fsdp'}, use_global_device_ids=true, to_apply=%region_22.23.clone | all-reduce | flops 6144 | bytes 49152
  345.6 3.2 all-to-all-start.2
  351.4 2.2 all-to-all-done.2
  354.2 0.7 copy.158
  354.9 0.7 copy.159
  355.7 0.7 copy.160
  (224 shorter events, 27.8 us)
Async XLA Ops:
  7.2 45.1 %copy-start = (bf16[192,576]{1,0:T(8,128)(2,1)S(1)}, bf16[192,576]{1,0:T(8,128)(2,1)}, u32[]{:S(2)}) copy-start(bf16[192,576]{1,0:T(8,128)(2,1)} %param.18) | copy-start | bytes 663556
  7.2 139.4 %copy-start.1 = (bf16[1,256,768]{2,1,0:T(8,128)(2,1)S(1)}, bf16[1,256,768]{2,1,0:T(8,128)(2,1)}, u32[]{:S(2)}) copy-start(bf16[1,256,768]{2,1,0:T(8,128)(2,1)} %param.14) | copy-start | bytes 1179652
  7.2 123.7 %all-reduce.4.cloned.1.call-start = ((), (), s32[]{:S(2)}) async-start(), calls=%async_computation.3 | async-start | bytes 163840
  55.6 91.2 %copy-start.23 = (f32[256]{0:T(256)}, f32[256]{0:T(256)S(1)}, u32[]{:S(2)}) copy-start(f32[256]{0:T(256)S(1)} %broadcast_multiply_fusion.5) | copy-start | bytes 3076
  56.9 94.5 %copy-start.34 = (f32[256]{0:T(256)}, f32[256]{0:T(256)S(1)}, u32[]{:S(2)}) copy-start(f32[256]{0:T(256)S(1)} %add_rsqrt_fusion.1) | copy-start | bytes 3076
  132.3 12.2 %all-to-all-start = ((f32[8,1,1344]{2,1,0:T(1,128)}), f32[8,1,1344]{2,1,0:T(1,128)S(1)}, u32[]{:S(2)}, u32[]{:S(2)}) async-start(f32[8,1,1344]{2,1,0:T(1,128)} %all_to_all.20), calls=%async_computation | async-start | bytes 90112 | tf_op jit(solution)/shard_map/all_to_all | solution.py:534
  156.8 3.2 copy-start.10
  157.1 5.3 %copy-start.4 = (bf16[256,768]{0,1:T(8,128)(2,1)}, bf16[256,768]{0,1:T(8,128)(2,1)S(1)}, u32[]{:S(2)}) copy-start(bf16[256,768]{0,1:T(8,128)(2,1)S(1)} %copy.87) | copy-start | bytes 1179652
  157.1 5.3 %slice-start = ((s8[4718592]{0:T(1024)(128)(4,1)}), s8[524288]{0:T(1024)(128)(4,1)S(1)}, s32[]{:S(2)}) async-start(s8[4718592]{0:T(1024)(128)(4,1)} %bitcast.126), calls=%async_computation.4 | async-start | bytes 1048576
  160.0 2.5 copy-start.21
  160.0 3.1 slice-start.1
  162.4 2.5 copy-start.3
  163.1 1.8 copy-start.27
  166.8 17.5 %copy-start.28 = (f32[256]{0:T(256)}, f32[256]{0:T(256)S(1)}, u32[]{:S(2)}) copy-start(f32[256]{0:T(256)S(1)} %broadcast_multiply_fusion.4) | copy-start | bytes 3076
  167.1 17.3 %copy-start.36 = (f32[256]{0:T(256)}, f32[256]{0:T(256)S(1)}, u32[]{:S(2)}) copy-start(f32[256]{0:T(256)S(1)} %add_rsqrt_fusion) | copy-start | bytes 3076
  167.8 4.0 %copy-start.43 = (f32[768]{0:T(1024)S(1)}, f32[768]{0:T(1024)}, u32[]{:S(2)}) copy-start(f32[768]{0:T(1024)} %get-tuple-element.35) | copy-start | bytes 9220
  167.8 4.0 %copy-start.45 = (bf16[1,256,768]{2,1,0:T(8,128)(2,1)S(1)}, bf16[1,256,768]{2,1,0:T(8,128)(2,1)}, u32[]{:S(2)}) copy-start(bf16[1,256,768]{2,1,0:T(8,128)(2,1)} %param.16) | copy-start | bytes 1179652
  167.8 13.4 %slice-start.4 = ((s8[4718592]{0:T(1024)(128)(4,1)}), s8[4194304]{0:T(1024)(128)(4,1)S(1)}, s32[]{:S(2)}) async-start(s8[4718592]{0:T(1024)(128)(4,1)} %bitcast.160), calls=%async_computation.8 | async-start | bytes 8388608
  171.8 8.2 %copy-start.47 = (f32[256,3072]{1,0:T(8,128)}, f32[256,3072]{1,0:T(8,128)S(1)}, u32[]{:S(2)}) copy-start(f32[256,3072]{1,0:T(8,128)S(1)} %convolution_add_fusion) | copy-start | bytes 9437188
  171.8 9.4 %copy-start.16 = (f32[768]{0:T(1024)S(1)}, f32[768]{0:T(1024)}, u32[]{:S(2)}) copy-start(f32[768]{0:T(1024)} %get-tuple-element.37) | copy-start | bytes 9220
  171.8 9.4 %slice-start.5 = ((s8[4718592]{0:T(1024)(128)(4,1)}), s8[524288]{0:T(1024)(128)(4,1)S(1)}, s32[]{:S(2)}) async-start(s8[4718592]{0:T(1024)(128)(4,1)} %bitcast.160), calls=%async_computation.9 | async-start | bytes 1048576
  181.2 3.0 copy-start.26
  181.2 3.1 copy-start.25
  202.4 6.2 %copy-start.11 = (bf16[256,768]{0,1:T(8,128)(2,1)S(1)}, bf16[256,768]{0,1:T(8,128)(2,1)}, u32[]{:S(2)}) copy-start(bf16[256,768]{0,1:T(8,128)(2,1)} %copy-done.10) | copy-start | bytes 1179652
  202.4 6.2 %copy-start.22 = (f32[12,256]{1,0:T(8,128)S(1)}, f32[12,256]{1,0:T(8,128)}, u32[]{:S(2)}) copy-start(f32[12,256]{1,0:T(8,128)} %copy-done.21) | copy-start | bytes 36868
  208.6 2.8 copy-start.13
  208.6 3.0 copy-start.2
  213.6 2.6 copy-start.15
  213.6 2.6 copy-start.17
  213.6 2.6 copy-start.29
  213.6 2.5 copy-start.37
  216.2 5.4 %copy-start.44 = (f32[768]{0:T(1024)S(1)}, f32[768]{0:T(1024)}, u32[]{:S(2)}) copy-start(f32[768]{0:T(1024)} %get-tuple-element.35) | copy-start | bytes 9220
  216.2 5.3 %copy-start.46 = (bf16[1,256,768]{2,1,0:T(8,128)(2,1)S(1)}, bf16[1,256,768]{2,1,0:T(8,128)(2,1)}, u32[]{:S(2)}) copy-start(bf16[1,256,768]{2,1,0:T(8,128)(2,1)} %param.16) | copy-start | bytes 1179652
  216.2 5.3 %copy-start.48 = (f32[256,3072]{1,0:T(8,128)S(1)}, f32[256,3072]{1,0:T(8,128)}, u32[]{:S(2)}) copy-start(f32[256,3072]{1,0:T(8,128)} %copy-done.47) | copy-start | bytes 9437188
  216.2 10.2 %slice-start.2 = ((s8[4718592]{0:T(1024)(128)(4,1)}), s8[4194304]{0:T(1024)(128)(4,1)S(1)}, s32[]{:S(2)}) async-start(s8[4718592]{0:T(1024)(128)(4,1)} %bitcast.128), calls=%async_computation.6 | async-start | bytes 8388608
  221.6 4.8 %slice-start.3 = ((s8[4718592]{0:T(1024)(128)(4,1)}), s8[524288]{0:T(1024)(128)(4,1)S(1)}, s32[]{:S(2)}) async-start(s8[4718592]{0:T(1024)(128)(4,1)} %bitcast.128), calls=%async_computation.7 | async-start | bytes 1048576
  226.4 1.7 copy-start.30
  226.4 1.8 copy-start.7
  226.5 1.8 copy-start.18
  228.2 1.6 copy-start.42
  228.2 1.7 copy-start.31
  228.2 1.7 copy-start.41
  228.2 5.8 %copy-start.9 = (bf16[256,768]{1,0:T(8,128)(2,1)S(1)}, bf16[256,768]{1,0:T(8,128)(2,1)}, u32[]{:S(2)}) copy-start(bf16[256,768]{1,0:T(8,128)(2,1)} %copy-done.8) | copy-start | bytes 1179652
  228.2 5.8 %copy-start.12 = (bf16[256,768]{1,0:T(8,128)(2,1)S(1)}, bf16[256,768]{1,0:T(8,128)(2,1)}, u32[]{:S(2)}) copy-start(bf16[256,768]{1,0:T(8,128)(2,1)} %copy.103) | copy-start | bytes 1179652
  230.7 77.3 %all-to-all-start.1 = ((f32[8,1,1344]{2,1,0:T(1,128)}), f32[8,1,1344]{2,1,0:T(1,128)S(1)}, u32[]{:S(2)}, u32[]{:S(2)}) async-start(f32[8,1,1344]{2,1,0:T(1,128)} %all_to_all.23), calls=%async_computation.1 | async-start | bytes 90112 | tf_op jit(solution)/shard_map/all_to_all | solution.py:563
  240.8 112.9 %copy-start.32 = (bf16[1,768]{1,0:T(2,128)(2,1)S(1)}, bf16[1,768]{1,0:T(2,128)(2,1)}, u32[]{:S(2)}) copy-start(bf16[1,768]{1,0:T(2,128)(2,1)} %param.15) | copy-start | bytes 4612
  240.8 112.9 %copy-start.33 = (f32[1,768]{1,0:T(1,128)S(1)}, f32[1,768]{1,0:T(1,128)}, u32[]{:S(2)}) copy-start(f32[1,768]{1,0:T(1,128)} %get-tuple-element.47) | copy-start | bytes 9220
  345.6 7.9 %all-to-all-start.2 = ((f32[4,1,192]{2,1,0:T(1,128)}), f32[4,1,192]{2,1,0:T(1,128)S(1)}, u32[]{:S(2)}, u32[]{:S(2)}) async-start(f32[4,1,192]{2,1,0:T(1,128)} %copy.102), calls=%async_computation.2 | async-start | bytes 8192 | tf_op jit(solution)/shard_map/all_to_all | solution.py:576
  (11 other events, 11.1 us)
Sparse Core Ops, SparseCore 0:
  53.3 37.8 all-reduce.3
where the time goes:
time: 364 us; the launch traced here: 363 us
  Pallas kernels  135 us (37%)
  blocking collectives  78.3 us (22%)
  matrix products  62.3 us (17%)
  local copies, waits for them, and re-layouts  38.2 us (10%)
  between operations  16.4 us (5%)
  starting transfers between devices  13 us (4%)
  other arithmetic  13 us (4%)
  waiting for transfers between devices  7.37 us (2%)
    pallas_call x1, Pallas kernels, gather_shards(): pl.pallas_call(functools.partial(gather_kernel, rows, depth), out_shape=[...  68.2 us
    pallas_call x1, Pallas kernels, scatter_shards(): pl.pallas_call(functools.partial(scatter_kernel, rows, depth), out_shape=...  66.5 us
    all_gather x1, blocking collectives, per_device(): cond_all = lax.all_gather(cond_act, ('dp', 'fsdp'), axis=0, tiled=True)  43.6 us
    unnamed x1, blocking collectives  25.9 us
    unnamed x151, local copies, waits for them, and re-layouts  18.5 us
    dot_general x4, matrix products, against_weight(): lax.dot_general(grad_rows, weight, (((1,), (1,)), ((), ())), preferred_el...  17.1 us
    dot_general x3, matrix products, contract_rows(): lax.dot_general(left_rows, right_rows, (((0,), (0,)), ((), ())), preferre...  15.9 us
    all_gather x1, blocking collectives, per_device(): all_rows = lax.all_gather(group_rows, 'dp', axis=0, tiled=True)  8.71 us
  transfers between devices with their start and end apart: 4, of which 2 were waited for; matrix products, arithmetic and copies ran while one was open for 5% of the time, Pallas kernels for 37%

commit v1 on v0

--- a/solution.py
+++ b/solution.py
@@ -29,11 +29,62 @@
     return steps
 
 
-def enter_barrier(partners):
+def device_of(index, columns):
+    return (index // columns, lax.rem(index, columns))
+
+
+def enter_barrier(me, rows, columns):
     barrier = pltpu.get_barrier_semaphore()
-    for partner in partners:
-        pl.semaphore_signal(barrier, inc=1, device_id=partner, device_id_type=MESH_IDS)
-    pl.semaphore_wait(barrier, len(partners))
+    count = rows * columns
+
+    @pl.loop(1, count)
+    def _(step):
+        target = device_of(lax.rem(me + step, count), columns)
+        pl.semaphore_signal(barrier, inc=1, device_id=target, device_id_type=MESH_IDS)
+
+    pl.semaphore_wait(barrier, count - 1)
+
+
+class Exchange:
+    def __init__(self, me, rows, columns, row_for, landing, send_sems, recv_sems):
+        self.me, self.columns, self.count = me, columns, rows * columns
+        self.row_for, self.landing = row_for, landing
+        self.send_sems, self.recv_sems = send_sems, recv_sems
+
+    def start(self):
+        @pl.loop(1, self.count)
+        def _(step):
+            target = lax.rem(self.me + step, self.count)
+            pltpu.make_async_remote_copy(
+                src_ref=self.row_for(target),
+                dst_ref=self.landing.at[self.me],
+                send_sem=self.send_sems.at[target],
+                recv_sem=self.recv_sems.at[self.me],
+                device_id=device_of(target, self.columns),
+                device_id_type=MESH_IDS,
+            ).start()
+
+        self.landing[self.me] = self.row_for(self.me)[...]
+
+    def pair(self, other):
+        return pltpu.make_async_remote_copy(
+            src_ref=self.row_for(other),
+            dst_ref=self.landing.at[other],
+            send_sem=self.send_sems.at[other],
+            recv_sem=self.recv_sems.at[other],
+            device_id=device_of(other, self.columns),
+            device_id_type=MESH_IDS,
+        )
+
+    def wait_arrivals(self):
+        @pl.loop(1, self.count)
+        def _(step):
+            self.pair(lax.rem(self.me + step, self.count)).wait_recv()
+
+    def wait_sends(self):
+        @pl.loop(1, self.count)
+        def _(step):
+            self.pair(lax.rem(self.me + step, self.count)).wait_send()
 
 
 def positions(rows, depth):
@@ -41,10 +92,7 @@
     column = lax.axis_index("fsdp")
     z, core = column // 2, column % 2
     others = [(dp ^ 1), (dp ^ 2)] if rows == 4 else [(dp + step) % rows for step in range(1, rows)]
-    partners = [place(dp, z, 1 - core)]
-    partners += [place(other, z, core) for other in others]
-    partners += [place(dp, (z + step) % depth, core) for step in z_order(depth)[1:]]
-    return dp, z, core, others, partners
+    return dp, z, core, others
 
 
 def block_of(array, line, row, shape, turned):
@@ -66,12 +114,38 @@
 
 
 def gather_kernel(rows, depth, *refs):
-    shards, outs = refs[:3], refs[3:6]
-    own_sems, send_sems, recv_sems = refs[6:]
-    dp, z, core, others, partners = positions(rows, depth)
+    shards = refs[:3]
+    cond_rows, ada_ref, ada_bias, bias_row = refs[3:7]
+    outs, mod_out, bias_out, cond_in = refs[7:10], refs[10], refs[11], refs[12]
+    (
+        own_sems, send_sems, recv_sems, bias_in, part_out, part_in,
+        cond_send, cond_recv, part_send, part_recv, bias_send, bias_recv,
+    ) = refs[13:]
+    dp, z, core, others = positions(rows, depth)
+    columns = 2 * depth
+    column = lax.axis_index("fsdp")
+    me = dp * columns + column
     sibling = place(dp, z, 1 - core)
-    enter_barrier(partners)
+    enter_barrier(me, rows, columns)
     sends = []
+
+    cond_swap = Exchange(
+        me, rows, columns, lambda target: cond_rows.at[target // columns], cond_in,
+        cond_send, cond_recv)
+    part_swap = Exchange(
+        me, rows, columns, lambda target: part_out.at[target], part_in, part_send, part_recv)
+    cond_swap.start()
+
+    def bias_copy(target, slot):
+        return pltpu.make_async_remote_copy(
+            src_ref=bias_row, dst_ref=bias_in.at[slot], send_sem=bias_send.at[target],
+            recv_sem=bias_recv.at[slot], device_id=(dp, target), device_id_type=MESH_IDS)
+
+    @pl.loop(1, columns)
+    def _(step):
+        bias_copy(lax.rem(column + step, columns), column).start()
+
+    bias_in[column] = bias_row[...]
 
     def slot_of(part, line, row):
         return block_of(outs[part], line, row, shards[part].shape, part == 2)
@@ -125,6 +199,12 @@
     ]
     for keep in keeps:
         keep.start()
+    cond_swap.wait_arrivals()
+    high, wide = ada_ref.shape
+    part = jnp.dot(
+        cond_in[:, 0, :high].astype(bfloat), ada_ref[...], preferred_element_type=jnp.float32)
+    part_out[:, 0, :wide] = part + jnp.where(dp == 0, ada_bias[...], 0.0)
+    part_swap.start()
     for turn in range(depth + 2):
         if 0 < turn < depth:
             line = lines[turn]
@@ -147,47 +227,93 @@
     for line in lines:
         for row in range(rows):
             arrive(line + 1 - 2 * core, (dp + row) % rows)
+    part_swap.wait_arrivals()
+    for block in range(columns):
+        total = part_in[block]
+        for row in range(1, rows):
+            total = total + part_in[row * columns + block]
+        mod_out[block] = total
+
+    @pl.loop(1, columns)
+    def _(step):
+        other = lax.rem(column + step, columns)
+        bias_copy(other, other).wait_recv()
+        bias_copy(other, other).wait_send()
+
+    bias_out[...] = bias_in[...]
     for keep in keeps:
         keep.wait()
     for copy in sends:
         copy.wait_send()
-
-
-def gather_shards(shards, rows, columns):
+    cond_swap.wait_sends()
+    part_swap.wait_sends()
+
+
+def round_up(width):
+    return -(-width // 128) * 128
+
+
+def gather_shards(shards, cond_rows, ada_weight, ada_bias, bias_row, rows, columns):
     depth = columns // 2
+    total = rows * columns
+    mod_pad = round_up(ada_weight.shape[1])
+    vmem = pl.BlockSpec(memory_space=pltpu.VMEM)
+    dma = pltpu.SemaphoreType.DMA
+    row_shape = lambda count, width: jax.ShapeDtypeStruct((count, 1, width), jnp.float32)
+    row_buffer = lambda count, width: pltpu.VMEM((count, 1, width), jnp.float32)
     count = (depth - 1) + depth * rows + depth * (rows - 1) + (2 * depth if rows == 4 else 0)
     shapes = [
         whole_shape(shard.shape, part == 2, rows, columns) for part, shard in enumerate(shards)
     ]
     return pl.pallas_call(
         functools.partial(gather_kernel, rows, depth),
-        out_shape=[jax.ShapeDtypeStruct(shape, bfloat) for shape in shapes],
-        in_specs=[pl.BlockSpec(memory_space=pl.ANY)] * 3,
-        out_specs=[pl.BlockSpec(memory_space=pl.ANY)] * 3,
+        out_shape=[jax.ShapeDtypeStruct(shape, bfloat) for shape in shapes]
+        + [row_shape(columns, mod_pad), row_shape(columns, bias_row.shape[-1]),
+           row_shape(total, cond_rows.shape[-1])],
+        in_specs=[pl.BlockSpec(memory_space=pl.ANY)] * 3 + [vmem] * 4,
+        out_specs=[pl.BlockSpec(memory_space=pl.ANY)] * 3 + [vmem] * 3,
         scratch_shapes=[
-            pltpu.SemaphoreType.DMA((3,)),
-            pltpu.SemaphoreType.DMA((3 * count,)),
-            pltpu.SemaphoreType.DMA((2, 3, columns, rows)),
+            dma((3,)),
+            dma((3 * count,)),
+            dma((2, 3, columns, rows)),
+            row_buffer(columns, bias_row.shape[-1]),
+            row_buffer(total, mod_pad),
+            row_buffer(total, mod_pad),
+            dma((total,)), dma((total,)), dma((total,)), dma((total,)),
+            dma((columns,)), dma((columns,)),
         ],
-        compiler_params=pltpu.CompilerParams(collective_id=0, has_side_effects=True),
+        compiler_params=pltpu.CompilerParams(
+            collective_id=0, has_side_effects=True, vmem_limit_bytes=32 * 2**20),
         name="gather_shards",
-    )(*shards)
+    )(*shards, cond_rows, ada_weight, ada_bias, bias_row)
 
 
 def scatter_kernel(rows, depth, *refs):
-    grads, outs = refs[:3], refs[3:6]
+    grads = refs[:3]
+    leaving, cond_in, ada_ref, slope = refs[3:7]
+    outs, ada_grad, sums_out, cond_grad = refs[7:10], refs[10], refs[11], refs[12]
+    refs = refs[13:]
     helds, pairs_in, planes_in, crosses_in, alongs_in = (
-        refs[6 + 3 * kind : 9 + 3 * kind] for kind in range(5)
+        refs[3 * kind : 3 + 3 * kind] for kind in range(5)
     )
     (
         load_sems, pair_send, pair_recv, plane_send, plane_recv,
         cross_send, cross_recv, along_send, along_recv,
-    ) = refs[21:]
-    dp, z, core, others, partners = positions(rows, depth)
+        all_rows, back_out, back_in, row_send, row_recv, back_send, back_recv,
+    ) = refs[15:]
+    dp, z, core, others = positions(rows, depth)
+    columns = 2 * depth
+    me = dp * columns + lax.axis_index("fsdp")
+    row_swap = Exchange(
+        me, rows, columns, lambda target: leaving.at[lax.rem(target, columns)], all_rows,
+        row_send, row_recv)
+    back_swap = Exchange(
+        me, rows, columns, lambda target: back_out.at[target], back_in, back_send, back_recv)
     sibling = place(dp, z, 1 - core)
     targets = [dp ^ 3, dp ^ 1, dp ^ 2, dp] if rows == 4 else others + [dp]
     steps = z_order(depth)[::-1]
-    enter_barrier(partners)
+    enter_barrier(me, rows, columns)
+    row_swap.start()
     waits = []
 
     def remote(source, destination, send_sem, recv_sem, target):
@@ -226,6 +352,16 @@
                 loads[key].start()
     last = len(targets) - 1
     for turn in range(depth + 2):
+        if turn == depth - 1:
+            row_swap.wait_arrivals()
+            high, wide = ada_ref.shape
+            arrived = all_rows[:, 0, :]
+            sums_out[...] = jnp.sum(arrived, axis=0, keepdims=True)
+            ada_grad[...] = contract_exact(cond_in[:, 0, :high], arrived[:, :wide])
+            back_out[:, 0, :high] = lax.dot_general(
+                arrived[:, :wide], ada_ref[...].astype(jnp.float32), (((1,), (1,)), ((), ())),
+                precision=highest)
+            back_swap.start()
         if turn < depth:
             for slot in range(len(targets)):
                 for part in range(3):
@@ -279,12 +415,23 @@
             alongs[part, now].wait_recv()
         arrived = [alongs_in[part].at[now] for now in range(depth - 1)]
         add(helds[part].at[depth - 1, last], arrived, outs[part].shape[0], outs[part])
+    back_swap.wait_arrivals()
+    for row in range(rows):
+        total = back_in[row * columns]
+        for block in range(1, columns):
+            total = total + back_in[row * columns + block]
+        cond_grad[row] = total * slope[row]
     for copy in waits:
         copy.wait_send()
-
-
-def scatter_shards(grads, shapes, rows, columns):
+    row_swap.wait_sends()
+    back_swap.wait_sends()
+
+
+def scatter_shards(grads, leaving, cond_in, ada_weight, slope, shapes, rows, columns):
     depth = columns // 2
+    total = rows * columns
+    vmem = pl.BlockSpec(memory_space=pltpu.VMEM)
+    row_buffer = lambda count, width: pltpu.VMEM((count, 1, width), jnp.float32)
     peers = 2 if rows == 4 else rows - 1
     dma = pltpu.SemaphoreType.DMA
     buffers = []
@@ -295,19 +442,25 @@
             buffers.append(pltpu.VMEM(lead + (height, width), bfloat))
     return pl.pallas_call(
         functools.partial(scatter_kernel, rows, depth),
-        out_shape=[jax.ShapeDtypeStruct(shape, jnp.float32) for shape in shapes],
-        in_specs=[pl.BlockSpec(memory_space=pl.ANY)] * 3,
-        out_specs=[pl.BlockSpec(memory_space=pltpu.VMEM)] * 3,
+        out_shape=[jax.ShapeDtypeStruct(shape, jnp.float32) for shape in shapes]
+        + [jax.ShapeDtypeStruct(ada_weight.shape, jnp.float32),
+           jax.ShapeDtypeStruct((1, leaving.shape[-1]), jnp.float32),
+           jax.ShapeDtypeStruct(slope.shape, jnp.float32)],
+        in_specs=[pl.BlockSpec(memory_space=pl.ANY)] * 3 + [vmem] * 4,
+        out_specs=[vmem] * 6,
         scratch_shapes=buffers + [
             dma((3, depth, rows)), dma((3, depth, rows)), dma((3, depth, rows)),
             dma((3, depth, peers)), dma((3, depth, peers)),
             dma((3, depth, 2)), dma((3, depth, 2)),
             dma((3, depth - 1)), dma((3, depth - 1)),
+            row_buffer(total, leaving.shape[-1]),
+            row_buffer(total, slope.shape[-1]), row_buffer(total, slope.shape[-1]),
+            dma((total,)), dma((total,)), dma((total,)), dma((total,)),
         ],
         compiler_params=pltpu.CompilerParams(
             collective_id=1, has_side_effects=True, vmem_limit_bytes=50 * 2**20),
         name="scatter_shards",
-    )(*grads)
+    )(*grads, leaving, cond_in, ada_weight, slope)
 
 
 def normalize_rows(values):
@@ -358,7 +511,7 @@
     return jnp.concatenate(pieces, axis=1)
 
 
-def layer(latent_rows, cond_act, live, cot_rows, modulation, weights, biases, columns):
+def layer(latent_rows, live, cot_rows, modulation, weights, biases, columns):
     mixed_weight, fc1_weight, fc2_turned = weights
     qv_bias, proj_bias, fc1_bias, fc2_bias = biases
     length = latent_rows.shape[0]
@@ -512,30 +665,23 @@
     fc2_bias,
 ):
     rows, columns = lax.axis_size("dp"), lax.axis_size("fsdp")
-    row_index = lax.axis_index("dp")
     live = latent_count[0].astype(jnp.float32)
     depth = ada_weight.shape[0]
     mod_width = ada_weight.shape[1]
+    mod_pad = round_up(mod_width)
     own_biases = (qv_bias, proj_bias, fc1_bias, fc2_bias)
     widths = [bias.shape[0] for bias in own_biases]
-    cuts = [mod_width + sum(widths[:place]) for place in range(len(widths))]
+    cuts = [sum(widths[:place]) for place in range(len(widths))]
+
+    def split_cond(row):
+        pad = round_up(depth) - depth
+        return jnp.pad(row.reshape(rows, 1, depth), ((0, 0), (0, 0), (0, pad)))
 
     cond_row = conditioning.astype(jnp.float32)
-    cond_act = jax.nn.silu(cond_row).astype(bfloat)
-    cond_all = lax.all_gather(cond_act, ("dp", "fsdp"), axis=0, tiled=True)
-    cond_owned = lax.dynamic_slice_in_dim(cond_all, row_index * depth, depth, 1)
-    partial = jnp.dot(cond_owned, ada_weight, preferred_element_type=jnp.float32)
-    mod_rows = lax.psum_scatter(partial, "dp", scatter_dimension=0, tiled=True)
-    mod_rows = mod_rows + ada_bias.astype(jnp.float32)
-    bias_row = jnp.concatenate(own_biases).astype(jnp.float32)
-    payload = jnp.concatenate(
-        [mod_rows, jnp.broadcast_to(bias_row, (columns, bias_row.shape[0]))], axis=1
-    )
-    arrived = lax.all_to_all(payload, "fsdp", split_axis=0, concat_axis=0, tiled=True)
-    modulation = arrived[:, :mod_width].reshape(1, -1)
-    biases = tuple(
-        arrived[:, cut : cut + width].reshape(-1) for cut, width in zip(cuts, widths)
-    )
+    cond_act, silu_pull = jax.vjp(jax.nn.silu, cond_row)
+    slope = split_cond(silu_pull(jnp.ones_like(cond_row))[0])
+    cond_rows = split_cond(cond_act.astype(bfloat).astype(jnp.float32))
+    bias_row = jnp.concatenate(own_biases).astype(jnp.float32).reshape(1, -1)
 
     qkv_width = qkv_weight.shape[1]
     shards = (
@@ -544,39 +690,33 @@
         fc2_weight.T,
     )
     shapes = [shard.shape for shard in shards]
-    blocks = gather_shards(shards, rows, columns)
+    *blocks, mod_blocks, bias_blocks, cond_in = gather_shards(
+        shards, cond_rows, ada_weight, ada_bias.astype(jnp.float32).reshape(1, -1), bias_row,
+        rows, columns)
+    modulation = mod_blocks[:, :, :mod_width].reshape(1, -1)
+    biases = tuple(
+        bias_blocks[:, :, cut : cut + width].reshape(-1) for cut, width in zip(cuts, widths)
+    )
     weights = [flatten_blocks(block, part == 2) for part, block in enumerate(blocks)]
     block_out, latent_grad, mod_grad, weight_grads, bias_grads = layer(
-        latents[0], cond_act, live, cotangent[0], modulation, weights, biases, columns
+        latents[0], live, cotangent[0], modulation, weights, biases, columns
     )
     grads = [
         cut_blocks(grad, shapes[part], part == 2, rows, columns)
         for part, grad in enumerate(weight_grads)
     ]
-    mixed_grad, fc1_grad, fc2_turned_grad = scatter_shards(grads, shapes, rows, columns)
+    leaving = jnp.concatenate(
+        [jnp.pad(mod_grad.reshape(columns, -1), ((0, 0), (0, mod_pad - mod_width)))]
+        + [grad.reshape(columns, -1) for grad in bias_grads], axis=1
+    ).reshape(columns, 1, -1)
+    mixed_grad, fc1_grad, fc2_turned_grad, ada_grad, sums, cond_grad = scatter_shards(
+        grads, leaving, cond_in, ada_weight, slope, shapes, rows, columns)
     qkv_grad, proj_grad = mixed_grad[:, :qkv_width], mixed_grad[:, qkv_width:]
     fc2_grad = fc2_turned_grad.T
-
-    leaving = jnp.concatenate(
-        [mod_grad.reshape(columns, -1)] + [grad.reshape(columns, -1) for grad in bias_grads], axis=1
-    )
-    group_rows = lax.all_to_all(leaving, "fsdp", split_axis=0, concat_axis=0, tiled=True)
-    all_rows = lax.all_gather(group_rows, "dp", axis=0, tiled=True)
-    mod_owned = all_rows[:, :mod_width]
-    ada_grad = contract_exact(cond_owned.astype(jnp.float32), mod_owned)
-    sums = jnp.sum(all_rows, axis=0)
-    ada_bias_grad = sums[:mod_width]
-    bias_sums = [sums[cut : cut + width] for cut, width in zip(cuts, widths)]
-    back = lax.dot_general(
-        mod_owned, ada_weight.astype(jnp.float32), (((1,), (1,)), ((), ())), precision=highest
-    )
-    back = lax.psum_scatter(
-        back.reshape(rows, columns, depth), "fsdp", scatter_dimension=1, tiled=True
-    )
-    back = lax.all_to_all(
-        back.reshape(rows, depth), "dp", split_axis=0, concat_axis=0, tiled=True
-    ).reshape(1, -1)
-    cond_grad = jax.vjp(jax.nn.silu, cond_row)[1](back)[0]
+    ada_bias_grad = sums[0, :mod_width]
+    bias_sums = [
+        sums[0, mod_pad + cut : mod_pad + cut + width] for cut, width in zip(cuts, widths)]
+    cond_grad = cond_grad[:, :, :depth].reshape(1, -1)
     return (
         block_out[None],
         latent_grad[None],

time: 364 us -> 259 us (0.71)
  blocking collectives: 78.3 us -> 0 us
  between operations: 16.4 us -> 2.07 us
  Pallas kernels: 135 us -> 149 us
  starting transfers between devices: 13 us -> 0 us
  waiting for transfers between devices: 7.37 us -> 0 us
  matrix products: 62.3 us -> 56.4 us
    all_gather x2 -> x0, blocking collectives: 52.3 us -> none  [the longest x1 43.6 us: per_device(): cond_all = lax.all_gather(cond_act, ('dp', 'fsdp'), axis=0, tiled=True)]
    unnamed x1 -> x0, blocking collectives: 25.9 us -> none
    all_to_all x3 -> x0, starting transfers between devices: 12.9 us -> none  [the longest x1 6.35 us: per_device(): lax.all_to_all(payload, 'fsdp', split_axis=0, concat_axis=0, tiled=True)]
    pallas_call x1, Pallas kernels: 68.2 us -> 76.6 us  [gather_shards(): pl.pallas_call(functools.partial(gather_kernel, rows, depth), out_shape=[...]
    all_to_all x3 -> x0, waiting for transfers between devices: 7.33 us -> none  [the longest x1 5.15 us: per_device(): lax.all_to_all(payload, 'fsdp', split_axis=0, concat_axis=0, tiled=True)]
    unnamed x151 -> x101, local copies, waits for them, and re-layouts: 18.5 us -> 24.5 us
    pallas_call x1, Pallas kernels: 66.5 us -> 72.3 us  [scatter_shards(): pl.pallas_call(functools.partial(scatter_kernel, rows, depth), out_shape=...]
    dot_general x1, matrix products: 8.19 us -> 3.5 us  [layer(): grad_act = jnp.dot(grad_mlp, fc2_turned, preferred_element_type=jnp.float32)]
  transfers between devices with their start and end apart: 4 -> 0, of which waited for: 2 -> 0; matrix products, arithmetic and copies ran while one was open for 5% -> 0% of each run, Pallas kernels for 37% -> 0%
where the time goes in v1:
time: 259 us
  Pallas kernels  149 us (58%)
  matrix products  56.4 us (22%)
  local copies, waits for them, and re-layouts  40.1 us (15%)
  other arithmetic  11.4 us (4%)
    pallas_call x1, Pallas kernels, gather_shards(): pl.pallas_call(functools.partial(gather_kernel, rows, depth), out_shape=[...  76.6 us
    pallas_call x1, Pallas kernels, scatter_shards(): pl.pallas_call(functools.partial(scatter_kernel, rows, depth), out_shape=...  72.3 us
    unnamed x101, local copies, waits for them, and re-layouts  24.5 us
    dot_general x4, matrix products, against_weight(): lax.dot_general(grad_rows, weight, (((1,), (1,)), ((), ())), preferred_el...  18.1 us
    dot_general x3, matrix products, contract_rows(): lax.dot_general(left_rows, right_rows, (((0,), (0,)), ((), ())), preferre...  15.8 us

profile of v1, /device:TPU:0, one launch (start us, length us, event | category | flops | bytes accessed | tf_op | source)
XLA Modules:
  0.0 258.8 jit_solution(3021104556554224694)
XLA Ops:
  0.6 0.7 fusion.56
  1.4 0.7 convert_reduce_fusion.5
  2.2 1.0 pad_maximum_fusion.2.refs_0_
  3.2 0.7 concatenate.69
  4.5 0.7 maximum_convert_fusion.refs_6_
  5.3 0.7 reshape.232.refs_5_
  6.0 0.9 copy-done.1
  6.9 0.9 copy-done.3
  7.8 0.9 copy-done.4
  8.7 76.6 %gather_shards.1 = (bf16[768,3072]{1,0:T(8,128)(2,1)S(1)}, bf16[768,3072]{1,0:T(8,128)(2,1)S(1)}, bf16[768,3072]{1,0:T(8,128)(2,1)S(1)}, f32[8,1,640]{2,1,0:T(1,...) custom-call(bf16[192,384]{1,0:T(8,128)(2,1)S(1)} %pad_maximum_fusion.2.refs_0_, ...), custom_call_target="tpu_custom_call" | custom-call | tf_op jit(solution)/shard_map/gather_shards/pallas_call | solution.py:268
  85.4 2.1 copy-done
  87.5 2.2 copy-done.5
  89.7 2.2 copy-done.6
  92.1 1.1 convert_reduce_fusion.2
  93.2 1.2 fusion.33
  94.5 1.3 fusion.26
  95.8 0.7 copy-done.15
  96.5 3.8 %fusion.67 = f32[256,3072]{1,0:T(8,128)S(1)} fusion(bf16[256,768]{1,0:T(8,128)(2,1)S(1)} %fusion.26, bf16[768,3072]{1,0:T(8,128)(2,1)} %copy-done), kind=kOutput, calls=%fused_computation.168 | convolution fusion | flops 1207959552 | bytes 8257536 | tf_op jit(solution)/shard_map/dot_general | solution.py:526
  100.3 1.0 fusion.62
  101.2 3.4 %concatenate.72 = f32[256,2304]{1,0:T(8,128)} concatenate(f32[256,288]{1,0:T(8,128)} %get-tuple-element.79, f32[256,288]{1,0:T(8,128)S(1)} %get-tuple-element.78, f32[256,288]{1,0:T(8,128)S(1)} %get-tuple-element.77, f32[256,288]{1,0:T(8,128)S(1)} %get-tuple-element.76, f32[256,288]{1,0:T(8,128)S(1)} %get-tuple-element.75, f32[256,288]{1,0:T(8,128)S(1)} %get-tuple-element.74, ...), dimensions={1} | concatenate | bytes 4718592 | tf_op jit(solution)/shard_map/concatenate | solution.py:498
  104.9 1.8 add_convert_fusion
  107.1 2.8 %fusion.66 = (f32[12,256]{1,0:T(8,128)S(1)}, f32[12,256,256]{1,2,0:T(8,128)}) fusion(bf16[256,12,64]{0,2,1:T(8,128)(2,1)S(1)} %bitcast.138, bf16[256,12,64]{0,2,1:T(8,128)(2,1)S(1)} %bitcast.140), kind=kOutput, calls=%fused_computation.167 | convolution fusion | flops 103022848 | bytes 3944448 | tf_op jit(solution)/shard_map/sub | solution.py:538
  110.1 2.5 convolution_convert_fusion.5
  112.6 0.8 slice-done.1
  113.4 1.4 fusion.68
  116.5 4.0 %convolution_add_fusion = f32[256,3072]{1,0:T(8,128)S(1)} fusion(bf16[768,3072]{1,0:T(8,128)(2,1)} %copy-done.6, f32[3072]{0:T(1024)S(1)} %bitcast.146, f32[256,768]{1,0:T(8,128)S(1)} %get-tuple-element.63, f32[768]{0:T(1024)S(1)} %get-tuple-element.52, f32[768]{0:T(1024)S(1)} %get-tuple-element.53, f32[256]{0:T(256)S(1)} %add_rsqrt_fusion, ...), kind=kOutput, calls=%fused_computation.6 | convolution fusion | flops 1209729024 | bytes 8671232 | tf_op jit(solution)/shard_map/dot_general | solution.py:549
  121.2 3.5 %convert_reduce_fusion = (f32[3072]{0:T(1024)S(1)}, bf16[256,3072]{1,0:T(8,128)(2,1)S(1)}) fusion(f32[256,3072]{1,0:T(8,128)S(1)} %convolution_add_fusion, bf16[768,3072]{1,0:T(8,128)(2,1)S(1)} %bitcast.120, bf16[1,256,768]{2,1,0:T(8,128)(2,1)S(1)} %copy-done.22, f32[]{:T(128)} %bitcast, f32[768]{0:T(1024)S(1)} %get-tuple-element.51), kind=kOutput, calls=%fused_computation.17 | convolution fusion | flops 1226044416 | bytes 9845764 | tf_op jit(solution)/shard_map/dot_general | solution.py:561
  124.8 2.5 multiply_reduce_fusion.2
  127.3 6.8 %convert_reduce_fusion.3 = (f32[768]{0:T(1024)S(1)}, f32[768]{0:T(1024)S(1)}, bf16[1,256,768]{2,1,0:T(8,128)(2,1)}, f32[768]{0:T(1024)S(1)}, bf16[256,768]{1,0:T(8,128)(2,1)S(1)}, /*index=5*/f32[256,768]{1,0:T(8,128)}) fusion(bf16[1,256,768]{2,1,0:T(8,128)(2,1)S(1)} %copy-done.22, f32[]{:T(128)} %bitcast, f32[768]{0:T(1024)S(1)} %get-tuple-element.51, ...), kind=kOutput, calls=%fused_computation.63 | convolution fusion | flops 1219950336 | bytes 11428868 | tf_op jit(solution)/shard_map/dot_general | solution.py:489
  134.4 0.7 constant_dynamic-update-slice_fusion.15
  135.7 0.7 constant_dynamic-update-slice_fusion.13
  139.8 0.7 constant_dynamic-update-slice_fusion.7
  144.1 0.7 constant_dynamic-update-slice_fusion.1
  145.5 4.3 %convolution_convert_fusion.4 = bf16[256,768]{1,0:T(8,128)(2,1)S(1)} fusion(bf16[256,3072]{0,1:T(8,128)(2,1)} %constant_dynamic-update-slice_fusion, bf16[768,3072]{1,0:T(8,128)(2,1)} %copy-done), kind=kOutput, calls=%fused_computation.32 | convolution fusion | flops 1208156160 | bytes 6684672 | tf_op jit(solution)/shard_map/dot_general | solution.py:489
  149.7 0.9 copy.61
  150.7 2.8 %convolution_convert_fusion.3 = bf16[12,64,256]{2,1,0:T(8,128)(2,1)S(1)} fusion(bf16[256,12,64]{0,2,1:T(8,128)(2,1)} %bitcast.144, f32[12,256,256]{1,2,0:T(8,128)} %get-tuple-element.102, f32[12,256]{1,0:T(8,128)S(1)} %get-tuple-element.101), kind=kOutput, calls=%fused_computation.31 | convolution fusion | flops 102432768 | bytes 3944448 | tf_op jit(solution)/shard_map/hqk,qhe->khe/dot_general | solution.py:590
  153.8 0.7 multiply_reduce_fusion
  157.3 4.6 %fusion.32 = (f32[768]{0:T(1024)S(1)}, f32[256]{0:T(256)S(1)}, f32[256]{0:T(256)S(1)}, f32[768]{0:T(1024)S(1)}, f32[256,768]{1,0:T(8,128)S(1)}) fusion(bf16[1,256,768]{2,1,0:T(8,128)(2,1)S(1)} %copy-done.7, f32[256]{0:T(256)S(1)} %add_rsqrt_fusion.1, f32[256]{0:T(256)S(1)} %broadcast_multiply_fusion.5, f32[768]{0:T(1024)S(1)} %get-tuple-element.55, ...), kind=kOutput, calls=%fused_computation.53 | convolution fusion | flops 1209923584 | bytes 7484416 | tf_op jit(solution)/shard_map/dot_general | solution.py:489
  162.0 1.2 multiply_reduce_fusion.3
  163.6 5.5 %convolution_convert_fusion.1.refs_1_ = bf16[768,3072]{1,0:T(8,128)(2,1)} fusion(bf16[256,3072]{1,0:T(8,128)(2,1)} %copy-done.13, f32[256,768]{1,0:T(8,128)S(1)} %get-tuple-element.63, f32[768]{0:T(1024)S(1)} %get-tuple-element.52, f32[768]{0:T(1024)S(1)} %get-tuple-element.53, f32[256]{0:T(256)S(1)} %add_rsqrt_fusion, f32[256]{0:T(256)S(1)} %broadcast_multiply_fusion.4), kind=kOutput, calls=%fused_computation.2 | convolution fusion | flops 1211301888 | bytes 7086080 | tf_op jit(solution)/shard_map/dot_general | solution.py:479
  169.4 6.4 %convolution_convert_fusion.2.refs_0_ = bf16[768,3072]{1,0:T(8,128)(2,1)} fusion(bf16[256,3072]{0,1:T(8,128)(2,1)S(1)} %copy-done.20, bf16[256,3072]{0,1:T(8,128)(2,1)} %copy-done.21, bf16[256,768]{1,0:T(8,128)(2,1)S(1)} %copy.65, bf16[256,768]{1,0:T(8,128)(2,1)S(1)} %copy-done.16), kind=kOutput, calls=%fused_computation.3 | convolution fusion | flops 2426142720 | bytes 8650752 | tf_op jit(solution)/shard_map/dot_general | solution.py:479
  175.8 3.9 %convolution_convert_fusion.refs_2_ = bf16[768,3072]{1,0:T(8,128)(2,1)} fusion(bf16[1,256,768]{2,1,0:T(8,128)(2,1)S(1)} %copy-done.23, f32[]{:T(128)} %bitcast, f32[768]{0:T(1024)S(1)} %get-tuple-element.51, f32[256,3072]{1,0:T(8,128)S(1)} %copy-done.25), kind=kOutput, calls=%fused_computation.1 | convolution fusion | flops 1218183168 | bytes 8260612 | tf_op jit(solution)/shard_map/dot_general | solution.py:479
  179.7 72.3 %scatter_shards.1 = (f32[192,384]{1,0:T(8,128)S(1)}, f32[192,384]{1,0:T(8,128)S(1)}, f32[96,768]{1,0:T(8,128)S(1)}, f32[192,576]{1,0:T(8,128)S(1)}, f32[1,1408]{1,0:T(1,128)S(1)}, /*index=5*/f32[4,1,256]{2,1,0:T(1,128)S(1)}) custom-call(bf16[768,3072]{1,0:T(8,128)(2,1)} %convolution_convert_fusion.2.refs_0_, ...), custom_call_target="tpu_custom_call" | custom-call | tf_op jit(solution)/shard_map/scatter_shards/pallas_call | solution.py:443
  252.0 0.7 slice.233
  255.8 0.8 copy.110
  256.6 0.7 copy.111
  257.3 0.7 copy.112
  258.0 0.7 copy.113
  (157 shorter events, 18.8 us)
Async XLA Ops:
  6.0 0.9 copy-start.1
  6.9 0.9 copy-start.3
  7.8 0.9 copy-start.4
  85.4 2.1 copy-start
  87.5 2.2 copy-start.5
  89.7 2.2 copy-start.6
  95.8 0.7 copy-start.15
  107.1 2.8 %copy-start.11 = (bf16[256,768]{0,1:T(8,128)(2,1)}, bf16[256,768]{0,1:T(8,128)(2,1)S(1)}, u32[]{:S(2)}) copy-start(bf16[256,768]{0,1:T(8,128)(2,1)S(1)} %copy.51) | copy-start | bytes 1179652
  109.9 2.7 %slice-start = ((s8[4718592]{0:T(1024)(128)(4,1)}), s8[524288]{0:T(1024)(128)(4,1)S(1)}, s32[]{:S(2)}) async-start(s8[4718592]{0:T(1024)(128)(4,1)} %bitcast.114), calls=%async_computation | async-start | bytes 1048576
  110.1 2.5 copy-start.17
  110.1 3.3 %slice-start.1 = ((s8[4718592]{0:T(1024)(128)(4,1)}), s8[4194304]{0:T(1024)(128)(4,1)S(1)}, s32[]{:S(2)}) async-start(s8[4718592]{0:T(1024)(128)(4,1)} %bitcast.114), calls=%async_computation.1 | async-start | bytes 8388608
  112.6 2.3 copy-start.9
  114.9 1.0 copy-start.7
  116.1 5.0 %slice-start.2 = ((s8[4718592]{0:T(1024)(128)(4,1)}), s8[4194304]{0:T(1024)(128)(4,1)S(1)}, s32[]{:S(2)}) async-start(s8[4718592]{0:T(1024)(128)(4,1)} %bitcast.119), calls=%async_computation.2 | async-start | bytes 8388608
  116.5 4.7 %slice-start.3 = ((s8[4718592]{0:T(1024)(128)(4,1)}), s8[524288]{0:T(1024)(128)(4,1)S(1)}, s32[]{:S(2)}) async-start(s8[4718592]{0:T(1024)(128)(4,1)} %bitcast.119), calls=%async_computation.3 | async-start | bytes 1048576
  116.5 4.7 %copy-start.22 = (bf16[1,256,768]{2,1,0:T(8,128)(2,1)S(1)}, bf16[1,256,768]{2,1,0:T(8,128)(2,1)}, u32[]{:S(2)}) copy-start(bf16[1,256,768]{2,1,0:T(8,128)(2,1)} %param.16) | copy-start | bytes 1179652
  116.5 8.2 %slice-start.4 = ((s8[4718592]{0:T(1024)(128)(4,1)}), s8[4194304]{0:T(1024)(128)(4,1)S(1)}, s32[]{:S(2)}) async-start(s8[4718592]{0:T(1024)(128)(4,1)} %bitcast.121), calls=%async_computation.4 | async-start | bytes 8388608
  120.5 4.2 %copy-start.24 = (f32[256,3072]{1,0:T(8,128)}, f32[256,3072]{1,0:T(8,128)S(1)}, u32[]{:S(2)}) copy-start(f32[256,3072]{1,0:T(8,128)S(1)} %convolution_add_fusion) | copy-start | bytes 9437188
  121.2 3.5 %slice-start.5 = ((s8[4718592]{0:T(1024)(128)(4,1)}), s8[524288]{0:T(1024)(128)(4,1)S(1)}, s32[]{:S(2)}) async-start(s8[4718592]{0:T(1024)(128)(4,1)} %bitcast.121), calls=%async_computation.5 | async-start | bytes 1048576
  124.7 2.5 copy-start.13
  150.6 3.0 %copy-start.8 = (f32[12,256,256]{1,2,0:T(8,128)S(1)}, f32[12,256,256]{1,2,0:T(8,128)}, u32[]{:S(2)}) copy-start(f32[12,256,256]{1,2,0:T(8,128)} %get-tuple-element.102) | copy-start | bytes 9437188
  150.7 3.0 %copy-start.18 = (bf16[256,768]{0,1:T(8,128)(2,1)S(1)}, bf16[256,768]{0,1:T(8,128)(2,1)}, u32[]{:S(2)}) copy-start(bf16[256,768]{0,1:T(8,128)(2,1)} %copy-done.17) | copy-start | bytes 1179652
  150.7 3.1 %copy-start.19 = (bf16[256,768]{0,1:T(8,128)(2,1)S(1)}, bf16[256,768]{0,1:T(8,128)(2,1)}, u32[]{:S(2)}) copy-start(bf16[256,768]{0,1:T(8,128)(2,1)} %copy.61) | copy-start | bytes 1179652
  155.1 1.0 copy-start.12
  157.3 4.6 %copy-start.21 = (bf16[256,3072]{0,1:T(8,128)(2,1)}, bf16[256,3072]{0,1:T(8,128)(2,1)S(1)}, u32[]{:S(2)}) copy-start(bf16[256,3072]{0,1:T(8,128)(2,1)S(1)} %constant_dynamic-update-slice_fusion.16) | copy-start | bytes 4718596
  157.3 4.7 %copy-start.14 = (f32[256,768]{1,0:T(8,128)S(1)}, f32[256,768]{1,0:T(8,128)}, u32[]{:S(2)}) copy-start(f32[256,768]{1,0:T(8,128)} %get-tuple-element.86) | copy-start | bytes 2359300
  163.6 5.5 %copy-start.10 = (bf16[12,64,256]{2,1,0:T(8,128)(2,1)S(1)}, bf16[12,64,256]{2,1,0:T(8,128)(2,1)}, u32[]{:S(2)}) copy-start(bf16[12,64,256]{2,1,0:T(8,128)(2,1)} %copy-done.9) | copy-start | bytes 1179652
  163.6 5.7 %copy-start.16 = (bf16[256,768]{1,0:T(8,128)(2,1)S(1)}, bf16[256,768]{1,0:T(8,128)(2,1)}, u32[]{:S(2)}) copy-start(bf16[256,768]{1,0:T(8,128)(2,1)} %copy-done.15) | copy-start | bytes 1179652
  163.6 5.7 %copy-start.20 = (bf16[256,3072]{0,1:T(8,128)(2,1)S(1)}, bf16[256,3072]{0,1:T(8,128)(2,1)}, u32[]{:S(2)}) copy-start(bf16[256,3072]{0,1:T(8,128)(2,1)} %constant_dynamic-update-slice_fusion) | copy-start | bytes 4718596
  169.3 6.4 %copy-start.23 = (bf16[1,256,768]{2,1,0:T(8,128)(2,1)S(1)}, bf16[1,256,768]{2,1,0:T(8,128)(2,1)}, u32[]{:S(2)}) copy-start(bf16[1,256,768]{2,1,0:T(8,128)(2,1)} %param.16) | copy-start | bytes 1179652
  169.4 6.4 %copy-start.25 = (f32[256,3072]{1,0:T(8,128)S(1)}, f32[256,3072]{1,0:T(8,128)}, u32[]{:S(2)}) copy-start(f32[256,3072]{1,0:T(8,128)} %copy-done.24) | copy-start | bytes 9437188
  175.8 4.0 %copy-start.2 = (bf16[192,576]{1,0:T(8,128)(2,1)S(1)}, bf16[192,576]{1,0:T(8,128)(2,1)}, u32[]{:S(2)}) copy-start(bf16[192,576]{1,0:T(8,128)(2,1)} %refs_5_.1) | copy-start | bytes 663556

commit v2 on v1

--- a/solution.py
+++ b/solution.py
@@ -491,6 +491,495 @@
     )
 
 
+def dot_plain(left, right):
+    return jnp.dot(left, right, preferred_element_type=jnp.float32)
+
+
+def columns_sum(values):
+    return jnp.sum(values, axis=0, keepdims=True)
+
+
+class Gather:
+    def __init__(self, rows, depth, where, shards, outs, own_sems, send_sems, recv_sems):
+        self.rows, self.depth = rows, depth
+        self.dp, self.z, self.core, self.others = where
+        self.shards, self.outs = shards, outs
+        self.own_sems, self.send_sems, self.recv_sems = own_sems, send_sems, recv_sems
+        self.sibling = place(self.dp, self.z, 1 - self.core)
+        self.sends = []
+        self.keeps = []
+        self.own = self.z * 2 + self.core
+        self.steps = z_order(depth)
+        self.lines = [((self.z - step) % depth) * 2 + self.core for step in self.steps]
+        self.units = [(part, turn) for part in range(3) for turn in range(depth)]
+
+    def slot_of(self, part, line, row):
+        return block_of(self.outs[part], line, row, self.shards[part].shape, part == 2)
+
+    def half_of(self, ref, part, which):
+        half = self.shards[part].shape[0] // 2
+        return ref.at[pl.ds(which * half, half)]
+
+    def send(self, part, line, row, target, which=None, own=False):
+        destination = self.slot_of(part, line, row)
+        source = self.shards[part] if own else destination
+        if which is not None:
+            source, destination = (
+                self.half_of(source, part, which), self.half_of(destination, part, which))
+        copy = pltpu.make_async_remote_copy(
+            src_ref=source,
+            dst_ref=destination,
+            send_sem=self.send_sems.at[len(self.sends)],
+            recv_sem=self.recv_sems.at[which or 0, part, line, row],
+            device_id=target,
+            device_id_type=MESH_IDS,
+        )
+        copy.start()
+        self.sends.append(copy)
+
+    def arrive(self, part, line, row, which=None):
+        destination = self.slot_of(part, line, row)
+        if which is not None:
+            destination = self.half_of(destination, part, which)
+        pltpu.make_async_remote_copy(
+            src_ref=destination,
+            dst_ref=destination,
+            send_sem=self.send_sems.at[0],
+            recv_sem=self.recv_sems.at[which or 0, part, line, row],
+            device_id=self.sibling,
+            device_id_type=MESH_IDS,
+        ).wait_recv()
+
+    def send_own(self, part):
+        dp, z, core = self.dp, self.z, self.core
+        for other in self.others:
+            self.send(part, self.own, dp, place(other, z, core), own=True)
+        for step in self.steps[1:]:
+            self.send(part, self.own, dp, place(dp, (z + step) % self.depth, core), own=True)
+        self.send(part, self.own, dp, self.sibling, own=True)
+        keep = pltpu.make_async_copy(
+            self.shards[part], self.slot_of(part, self.own, dp), self.own_sems.at[part])
+        keep.start()
+        self.keeps.append(keep)
+
+    def turn(self, index):
+        dp, z, core = self.dp, self.z, self.core
+        count = len(self.units)
+        if index < count:
+            part, turn = self.units[index]
+            line = self.lines[turn]
+            if turn:
+                self.arrive(part, line, dp)
+                for other in self.others:
+                    self.send(part, line, dp, place(other, z, core))
+                self.send(part, line, dp, self.sibling)
+        if 1 <= index <= count:
+            part, turn = self.units[index - 1]
+            line = self.lines[turn]
+            for position, other in enumerate(self.others):
+                self.arrive(part, line, other)
+                self.send(
+                    part, line, other, place(self.others[1 - position], z, core), which=position)
+                self.send(part, line, other, self.sibling)
+        if 2 <= index:
+            part, turn = self.units[index - 2]
+            line = self.lines[turn]
+            self.arrive(part, line, dp ^ 3, 0)
+            self.arrive(part, line, dp ^ 3, 1)
+            self.send(part, line, dp ^ 3, self.sibling)
+
+    def finish_part(self, part):
+        for line in self.lines:
+            for row in range(self.rows):
+                self.arrive(part, line + 1 - 2 * self.core, (self.dp + row) % self.rows)
+        self.keeps[part].wait()
+
+    def wait_sends(self):
+        for copy in self.sends:
+            copy.wait_send()
+
+
+def layer_kernel(rows, depth, *refs):
+    shards = refs[:3]
+    cond_rows, ada_ref, ada_bias, bias_row, latents, cotangent, live_ref = refs[3:10]
+    block_out, latent_grad, leaving, cond_in = refs[10:14]
+    grads_out = refs[14:17]
+    weights, grads = refs[17:20], refs[20:23]
+    (
+        own_sems, send_sems, recv_sems, out_sems, bias_in, part_out, part_in,
+        cond_send, cond_recv, part_send, part_recv, bias_send, bias_recv,
+        mod, qkv_bias, proj_bias, fc1_bias, fc2_bias, mod_grad, qkv_sums, proj_sums, fc1_sums,
+        fc2_sums, inverse_one, inverse_two, normed_one, normed_two, middle, branch, wide,
+        hidden_one, hidden_one_t, hidden_two, hidden_two_t, attended, attended_t,
+        grad_mlp, grad_mlp_t, grad_attended, projected, grad_natural, grad_mixed,
+        grad_proj_mixed, activated, grad_pre, probability,
+    ) = refs[23:]
+    mixed, fc1, fc2_turned = weights
+    where = positions(rows, depth)
+    dp = where[0]
+    columns = 2 * depth
+    column = lax.axis_index("fsdp")
+    me = dp * columns + column
+    length = latents.shape[0]
+    qkv_part, proj_part = 3 * D // columns, D // columns
+    block = qkv_part + proj_part
+    edge = qkv_part // 128 * 128
+    rest = block - edge
+    lead = qkv_part - edge
+    scale_factor = HEAD ** (-0.5)
+    enter_barrier(me, rows, columns)
+    gather = Gather(rows, depth, where, shards, weights, own_sems, send_sems, recv_sems)
+
+    cond_swap = Exchange(
+        me, rows, columns, lambda target: cond_rows.at[target // columns], cond_in,
+        cond_send, cond_recv)
+    part_swap = Exchange(
+        me, rows, columns, lambda target: part_out.at[target], part_in, part_send, part_recv)
+    cond_swap.start()
+    gather.send_own(0)
+
+    def bias_copy(target, slot):
+        return pltpu.make_async_remote_copy(
+            src_ref=bias_row, dst_ref=bias_in.at[slot], send_sem=bias_send.at[target],
+            recv_sem=bias_recv.at[slot], device_id=(dp, target), device_id_type=MESH_IDS)
+
+    @pl.loop(1, columns)
+    def _(step):
+        bias_copy(lax.rem(column + step, columns), column).start()
+
+    bias_in[column] = bias_row[...]
+    gather.send_own(1)
+    gather.send_own(2)
+
+    def piece(kind):
+        return mod[:, kind * D : (kind + 1) * D]
+
+    def start_modulation():
+        cond_swap.wait_arrivals()
+        high, width = ada_ref.shape
+        part = dot_plain(cond_in[:, 0, :high].astype(bfloat), ada_ref[...])
+        part_out[:, 0, :width] = part + jnp.where(dp == 0, ada_bias[...], 0.0)
+        part_swap.start()
+
+    def normalize_first():
+        normed, inverse = normalize_rows(latents[...].astype(jnp.float32))
+        normed_one[...] = normed
+        inverse_one[...] = inverse
+
+    def finish_modulation():
+        part_swap.wait_arrivals()
+        width = ada_ref.shape[1]
+        pieces = []
+        for source in range(columns):
+            total = part_in[source]
+            for row in range(1, rows):
+                total = total + part_in[row * columns + source]
+            pieces.append(total[:, :width])
+        mod[...] = jnp.concatenate(pieces, axis=1)
+
+        @pl.loop(1, columns)
+        def _(step):
+            other = lax.rem(column + step, columns)
+            bias_copy(other, other).wait_recv()
+            bias_copy(other, other).wait_send()
+
+        low = 0
+        naturals = []
+        for width in (2 * D // columns, D // columns, FF // columns, D // columns):
+            naturals.append(jnp.concatenate(
+                [bias_in[source][:, low : low + width] for source in range(columns)], axis=1))
+            low += width
+        qkv_bias[:, :D] = naturals[0][:, :D]
+        qkv_bias[:, D : 2 * D] = jnp.zeros((1, D), jnp.float32)
+        qkv_bias[:, 2 * D :] = naturals[0][:, D:]
+        proj_bias[...] = naturals[1]
+        fc1_bias[...] = naturals[2]
+        fc2_bias[...] = naturals[3]
+        hidden = (normed_one[...] * (1.0 + piece(1)) + piece(0)).astype(bfloat)
+        hidden_one[...] = hidden
+        hidden_one_t[...] = hidden.T
+        grad = (piece(5) * (live_ref[...] * cotangent[...].astype(jnp.float32))).astype(bfloat)
+        grad_mlp[...] = grad
+        grad_mlp_t[...] = grad.T
+        fc2_sums[...] = columns_sum(grad.astype(jnp.float32))
+
+    def span(index, width):
+        return pl.ds(pl.multiple_of(index * width, width), width)
+
+    def project():
+        @pl.loop(0, columns)
+        def _(index):
+            wide[:, span(index, block)] = dot_plain(hidden_one[...], mixed[:, span(index, block)])
+
+        for index in range(columns):
+            natural = slice(index * qkv_part, (index + 1) * qkv_part)
+            projected[:, natural] = (
+                wide[:, index * block : index * block + qkv_part] + qkv_bias[:, natural]
+            ).astype(bfloat)
+
+    def head_slabs(source, pair):
+        return [
+            source[:, pl.ds(pl.multiple_of(kind * D + pair * 128, 128), 128)] for kind in range(3)]
+
+    def own_lanes(which):
+        lane = lax.broadcasted_iota(jnp.int32, (length, 128), 1)
+        return lane < HEAD if which == 0 else lane >= HEAD
+
+    def attend(low, high):
+        @pl.loop(low, high)
+        def _(pair):
+            queries, keys, values = head_slabs(projected, pair)
+            zero = jnp.zeros_like(queries)
+            results = []
+            for which in range(2):
+                scores = against_weight(
+                    jnp.where(own_lanes(which), queries, zero), keys) * scale_factor
+                shifted = jnp.exp(scores - jnp.max(scores, axis=-1, keepdims=True))
+                exact = shifted / jnp.sum(shifted, axis=-1, keepdims=True)
+                probability[2 * pair + which] = exact
+                results.append(dot_plain(exact.astype(bfloat), values))
+            attended[:, span(pair, 128)] = jnp.where(
+                own_lanes(0), results[0], results[1]).astype(bfloat)
+
+    def finish_attention():
+        attended_t[...] = attended[...].T
+
+        @pl.loop(0, columns)
+        def _(index):
+            tail = pl.ds(pl.multiple_of(index * block + edge, 128), rest)
+            wide[:, span(index, rest)] = dot_plain(attended[...], mixed[:, tail])
+
+        for index in range(columns):
+            natural = slice(index * proj_part, (index + 1) * proj_part)
+            branch[:, natural] = (
+                wide[:, index * rest + lead : (index + 1) * rest] + proj_bias[:, natural])
+        total = latents[...].astype(jnp.float32) + piece(2) * branch[...]
+        middle[...] = total
+        normed, inverse = normalize_rows(total)
+        normed_two[...] = normed
+        inverse_two[...] = inverse
+        hidden = (normed * (1.0 + piece(4)) + piece(3)).astype(bfloat)
+        hidden_two[...] = hidden
+        hidden_two_t[...] = hidden.T
+
+    chunk = 384
+    chunks = FF // chunk
+
+    def expand(low, high):
+        @pl.loop(low, high)
+        def _(index):
+            part = span(index, chunk)
+            value = dot_plain(hidden_two[...], fc1[:, part]) + fc1_bias[:, part]
+            root = 0.7978845608028654
+            square = value * value
+            bend = jnp.tanh(root * (value + 0.044715 * (square * value)))
+            activated[:, part] = (0.5 * value * (1.0 + bend)).astype(bfloat)
+            wide[:, part] = 0.5 * (1.0 + bend) + 0.5 * value * (1.0 - bend * bend) * (
+                root * (1.0 + 3 * 0.044715 * square))
+
+    def fc2_weight_grad(low, high):
+        @pl.loop(low, high)
+        def _(index):
+            part = span(index, chunk)
+            grads[2][:, part] = dot_plain(grad_mlp_t[...], activated[:, part]).astype(bfloat)
+
+    def leave(part):
+        copy = pltpu.make_async_copy(grads[part], grads_out[part], out_sems.at[part])
+        copy.start()
+        return copy
+
+    hooks = {
+        0: start_modulation,
+        1: normalize_first,
+        2: finish_modulation,
+    }
+
+    def after_part_zero():
+        gather.finish_part(0)
+        project()
+
+    def after_part_one():
+        gather.finish_part(1)
+        expand(0, 4)
+
+    hooks[depth + 2] = after_part_zero
+    hooks[depth + 3] = lambda: attend(0, 3)
+    hooks[depth + 4] = lambda: attend(3, 6)
+    hooks[depth + 5] = finish_attention
+    hooks[2 * depth + 2] = after_part_one
+    hooks[2 * depth + 3] = lambda: expand(4, 8)
+    hooks[2 * depth + 4] = lambda: fc2_weight_grad(0, 4)
+    hooks[2 * depth + 5] = lambda: fc2_weight_grad(4, 8)
+    for index in range(3 * depth + 2):
+        gather.turn(index)
+        if index in hooks:
+            hooks[index]()
+    copies = [leave(2)]
+    gather.finish_part(2)
+
+    third = 256
+
+    @pl.loop(0, D // third)
+    def _(index):
+        part = span(index, third)
+        branch_part = against_weight(activated[...], fc2_turned[part, :]) + fc2_bias[:, part]
+        live_grad = live_ref[:, part] * cotangent[:, part].astype(jnp.float32)
+        gate = mod[:, pl.ds(pl.multiple_of(5 * D + index * third, third), third)]
+        block_out[:, part] = (
+            live_ref[:, part] * (middle[:, part] + gate * branch_part)).astype(bfloat)
+        mod_grad[:, pl.ds(pl.multiple_of(5 * D + index * third, third), third)] = columns_sum(
+            live_grad * branch_part)
+
+    @pl.loop(0, chunks)
+    def _(index):
+        part = span(index, chunk)
+        grad = (dot_plain(grad_mlp[...], fc2_turned[:, part]) * wide[:, part]).astype(bfloat)
+        grad_pre[:, part] = grad
+        fc1_sums[:, part] = columns_sum(grad.astype(jnp.float32))
+        grads[1][:, part] = dot_plain(hidden_two_t[...], grad).astype(bfloat)
+
+    copies.append(leave(1))
+
+    @pl.loop(0, D // third)
+    def _(index):
+        part = span(index, third)
+        middle[:, part] = against_weight(grad_pre[...], fc1[part, :])
+
+    grad_hidden = middle[...]
+    mod_grad[:, 3 * D : 4 * D] = columns_sum(grad_hidden)
+    mod_grad[:, 4 * D : 5 * D] = columns_sum(grad_hidden * normed_two[...])
+    grad_middle = live_ref[...] * cotangent[...].astype(jnp.float32) + norm_backward(
+        grad_hidden * (1.0 + piece(4)), normed_two[...], inverse_two[...])
+    mod_grad[:, 2 * D : 3 * D] = columns_sum(grad_middle * branch[...])
+    middle[...] = grad_middle
+    grad_branch = (piece(2) * grad_middle).astype(bfloat)
+    proj_sums[...] = columns_sum(grad_branch.astype(jnp.float32))
+    for index in range(columns):
+        grad_proj_mixed[:, index * rest : index * rest + lead] = jnp.zeros((length, lead), bfloat)
+        grad_proj_mixed[:, index * rest + lead : (index + 1) * rest] = (
+            grad_branch[:, index * proj_part : (index + 1) * proj_part])
+    total = None
+    for index in range(columns):
+        term = against_weight(
+            grad_proj_mixed[:, index * rest : (index + 1) * rest],
+            mixed[:, index * block + edge : (index + 1) * block])
+        total = term if total is None else total + term
+    grad_attended[...] = total.astype(bfloat)
+
+    @pl.loop(0, HEADS // 2)
+    def _(pair):
+        queries, keys, values = head_slabs(projected, pair)
+        grad_out = grad_attended[:, span(pair, 128)]
+        zero = jnp.zeros_like(grad_out)
+        results = []
+        for which in range(2):
+            exact = probability[2 * pair + which]
+            grad_prob = against_weight(jnp.where(own_lanes(which), grad_out, zero), values)
+            inner = jnp.sum(exact * grad_prob, axis=-1, keepdims=True)
+            grad_scores = (exact * (grad_prob - inner)).astype(bfloat)
+            results.append((
+                dot_plain(grad_scores, keys) * scale_factor,
+                contract_rows(grad_scores, queries) * scale_factor,
+                contract_rows(exact.astype(bfloat), grad_out)))
+        for kind in range(3):
+            grad_natural[:, pl.ds(pl.multiple_of(kind * D + pair * 128, 128), 128)] = jnp.where(
+                own_lanes(0), results[0][kind], results[1][kind]).astype(bfloat)
+
+    qkv_sums[...] = columns_sum(grad_natural[...].astype(jnp.float32))
+    for index in range(columns):
+        grad_mixed[:, index * block : index * block + qkv_part] = (
+            grad_natural[:, index * qkv_part : (index + 1) * qkv_part])
+        grad_mixed[:, index * block + qkv_part : (index + 1) * block] = jnp.zeros(
+            (length, proj_part), bfloat)
+
+    @pl.loop(0, columns)
+    def _(index):
+        low = pl.multiple_of(index * block, 128)
+        grads[0][:, pl.ds(low, edge)] = dot_plain(
+            hidden_one_t[...], grad_mixed[:, pl.ds(low, edge)]).astype(bfloat)
+        tail = pl.ds(pl.multiple_of(index * block + edge, 128), rest)
+        grads[0][:, tail] = (
+            dot_plain(hidden_one_t[...], grad_mixed[:, tail])
+            + dot_plain(attended_t[...], grad_proj_mixed[:, span(index, rest)])).astype(bfloat)
+
+    copies.append(leave(0))
+
+    @pl.loop(0, D // third)
+    def _(index):
+        part = span(index, third)
+        branch[:, part] = against_weight(grad_mixed[...], mixed[part, :])
+
+    grad_hidden = branch[...]
+    mod_grad[:, :D] = columns_sum(grad_hidden)
+    mod_grad[:, D : 2 * D] = columns_sum(grad_hidden * normed_one[...])
+    latent_grad[...] = (middle[...] + norm_backward(
+        grad_hidden * (1.0 + piece(1)), normed_one[...], inverse_one[...])).astype(bfloat)
+    width = ada_ref.shape[1]
+    pad = jnp.zeros((1, round_up(width) - width), jnp.float32)
+    qv_sums = jnp.concatenate([qkv_sums[:, :D], qkv_sums[:, 2 * D :]], axis=1)
+    rows_of = (qv_sums, proj_sums[...], fc1_sums[...], fc2_sums[...])
+    every = mod_grad[...]
+    for index in range(columns):
+        pieces = [every[:, index * width : (index + 1) * width], pad]
+        for row in rows_of:
+            share = row.shape[1] // columns
+            pieces.append(row[:, index * share : (index + 1) * share])
+        leaving[index] = jnp.concatenate(pieces, axis=1)
+    for copy in copies:
+        copy.wait()
+    gather.wait_sends()
+    cond_swap.wait_sends()
+    part_swap.wait_sends()
+
+
+def run_layer(shards, cond_rows, ada_weight, ada_bias, bias_row, latents, cotangent, live,
+              rows, columns):
+    depth = columns // 2
+    count = (depth - 1) + depth * rows + depth * (rows - 1) + 2 * depth
+    total = rows * columns
+    mod_pad = round_up(ada_weight.shape[1])
+    bias_width = bias_row.shape[-1]
+    length = latents.shape[0]
+    vmem = pl.BlockSpec(memory_space=pltpu.VMEM)
+    anywhere = pl.BlockSpec(memory_space=pl.ANY)
+    dma = pltpu.SemaphoreType.DMA
+    shapes = [
+        whole_shape(shard.shape, part == 2, rows, columns) for part, shard in enumerate(shards)]
+    row_buffer = lambda count, width: pltpu.VMEM((count, 1, width), jnp.float32)
+    wide_row = lambda width: pltpu.VMEM((1, width), jnp.float32)
+    single = lambda width: pltpu.VMEM((length, width), jnp.float32)
+    half = lambda width: pltpu.VMEM((length, width), bfloat)
+    turned = pltpu.VMEM((D, length), bfloat)
+    rest = 128 * columns
+    row_out = lambda count, width: jax.ShapeDtypeStruct((count, 1, width), jnp.float32)
+    return pl.pallas_call(
+        functools.partial(layer_kernel, rows, depth),
+        out_shape=[
+            jax.ShapeDtypeStruct((length, D), bfloat),
+            jax.ShapeDtypeStruct((length, D), bfloat),
+            row_out(columns, mod_pad + bias_width),
+            row_out(total, cond_rows.shape[-1]),
+        ] + [jax.ShapeDtypeStruct(shape, bfloat) for shape in shapes],
+        in_specs=[anywhere] * 3 + [vmem] * 7,
+        out_specs=[vmem] * 4 + [anywhere] * 3,
+        scratch_shapes=[pltpu.VMEM(shape, bfloat) for shape in shapes] * 2 + [
+            dma((3,)), dma((3 * count,)), dma((2, 3, columns, rows)), dma((3,)),
+            row_buffer(columns, bias_width), row_buffer(total, mod_pad), row_buffer(total, mod_pad),
+            dma((total,)), dma((total,)), dma((total,)), dma((total,)),
+            dma((columns,)), dma((columns,)),
+            wide_row(6 * D), wide_row(3 * D), wide_row(D), wide_row(FF), wide_row(D),
+            wide_row(6 * D), wide_row(3 * D), wide_row(D), wide_row(FF), wide_row(D),
+            single(1), single(1), single(D), single(D), single(D), single(D), single(FF),
+            half(D), turned, half(D), turned, half(D), turned,
+            half(D), turned, half(D), half(3 * D), half(3 * D), half(4 * D),
+            half(rest), half(FF), half(FF), pltpu.VMEM((HEADS, length, length), jnp.float32),
+        ],
+        compiler_params=pltpu.CompilerParams(
+            collective_id=2, has_side_effects=True, vmem_limit_bytes=60 * 2**20),
+        name="run_layer",
+    )(*shards, cond_rows, ada_weight, ada_bias, bias_row, latents, cotangent, live)
+
+
 def pick(mixed, columns, kind):
     width = mixed.shape[1] // columns
     edge = 3 * width // 4
@@ -690,25 +1179,32 @@
         fc2_weight.T,
     )
     shapes = [shard.shape for shard in shards]
-    *blocks, mod_blocks, bias_blocks, cond_in = gather_shards(
-        shards, cond_rows, ada_weight, ada_bias.astype(jnp.float32).reshape(1, -1), bias_row,
-        rows, columns)
-    modulation = mod_blocks[:, :, :mod_width].reshape(1, -1)
-    biases = tuple(
-        bias_blocks[:, :, cut : cut + width].reshape(-1) for cut, width in zip(cuts, widths)
-    )
-    weights = [flatten_blocks(block, part == 2) for part, block in enumerate(blocks)]
-    block_out, latent_grad, mod_grad, weight_grads, bias_grads = layer(
-        latents[0], live, cotangent[0], modulation, weights, biases, columns
-    )
-    grads = [
-        cut_blocks(grad, shapes[part], part == 2, rows, columns)
-        for part, grad in enumerate(weight_grads)
-    ]
-    leaving = jnp.concatenate(
-        [jnp.pad(mod_grad.reshape(columns, -1), ((0, 0), (0, mod_pad - mod_width)))]
-        + [grad.reshape(columns, -1) for grad in bias_grads], axis=1
-    ).reshape(columns, 1, -1)
+    ada_row = ada_bias.astype(jnp.float32).reshape(1, -1)
+    fused = rows == 4 and columns == 8
+    if fused:
+        block_out, latent_grad, leaving, cond_in, *grads = run_layer(
+            shards, cond_rows, ada_weight, ada_row, bias_row, latents[0], cotangent[0],
+            jnp.full((1, D), live), rows, columns)
+    else:
+        *blocks, mod_blocks, bias_blocks, cond_in = gather_shards(
+            shards, cond_rows, ada_weight, ada_row, bias_row,
+            rows, columns)
+        modulation = mod_blocks[:, :, :mod_width].reshape(1, -1)
+        biases = tuple(
+            bias_blocks[:, :, cut : cut + width].reshape(-1) for cut, width in zip(cuts, widths)
+        )
+        weights = [flatten_blocks(block, part == 2) for part, block in enumerate(blocks)]
+        block_out, latent_grad, mod_grad, weight_grads, bias_grads = layer(
+            latents[0], live, cotangent[0], modulation, weights, biases, columns
+        )
+        grads = [
+            cut_blocks(grad, shapes[part], part == 2, rows, columns)
+            for part, grad in enumerate(weight_grads)
+        ]
+        leaving = jnp.concatenate(
+            [jnp.pad(mod_grad.reshape(columns, -1), ((0, 0), (0, mod_pad - mod_width)))]
+            + [grad.reshape(columns, -1) for grad in bias_grads], axis=1
+        ).reshape(columns, 1, -1)
     mixed_grad, fc1_grad, fc2_turned_grad, ada_grad, sums, cond_grad = scatter_shards(
         grads, leaving, cond_in, ada_weight, slope, shapes, rows, columns)
     qkv_grad, proj_grad = mixed_grad[:, :qkv_width], mixed_grad[:, qkv_width:]

time: 259 us -> 220 us (0.85)
  matrix products: 56.4 us -> 0 us
  Pallas kernels: 149 us -> 199 us
  local copies, waits for them, and re-layouts: 40.1 us -> 14.1 us
  other arithmetic: 11.4 us -> 5.03 us
    dot_general x16 -> x0, matrix products: 53.5 us -> none  [the longest x4 18.1 us: against_weight(): lax.dot_general(grad_rows, weight, (((1,), (1,)), ((), ())), preferred_el...]
    pallas_call x1, Pallas kernels: 76.6 us -> 128 us  [run_layer(): pl.pallas_call(functools.partial(layer_kernel, rows, depth), out_shape=[j...]
    unnamed x101 -> x16, local copies, waits for them, and re-layouts: 24.5 us -> 6.9 us
    concatenate x8 -> x0, local copies, waits for them, and re-layouts: 4.65 us -> none  [the longest x2 3.77 us: pick(): jnp.concatenate([mixed[:, block * width + low:block * width + high] for b...]
    reduce_sum x6 -> x0, other arithmetic: 4.35 us -> none  [the longest x2 1.46 us: normalize_rows(): spread = jnp.mean(jnp.square(values - center), axis=-1, keepdims=True)]
    convert_element_type x3 -> x0, other arithmetic: 3.66 us -> none  [the longest x1 1.8 us: layer(): projected = (pick(jnp.dot(hidden_one, mixed_weight, preferred_element_typ...]
    slice x22 -> x0, local copies, waits for them, and re-layouts: 3.25 us -> none  [the longest x2 1.29 us: pick(): mixed[:, block * width + low:block * width + high]]
    sub x1 -> x0, matrix products: 2.81 us -> none  [layer(): shifted = jnp.exp(scores - row_max)]
where the time goes in v2:
time: 220 us; the launch traced here: 219 us
  Pallas kernels  199 us (90%)
  local copies, waits for them, and re-layouts  14.1 us (6%)
  other arithmetic  5.03 us (2%)
    pallas_call x1, Pallas kernels, run_layer(): pl.pallas_call(functools.partial(layer_kernel, rows, depth), out_shape=[j...  128 us
    pallas_call x1, Pallas kernels, scatter_shards(): pl.pallas_call(functools.partial(scatter_kernel, rows, depth), out_shape=...  70.3 us
    unnamed x16, local copies, waits for them, and re-layouts  6.9 us

profile of v2, /device:TPU:0, one launch (start us, length us, event | category | flops | bytes accessed | tf_op | source)
XLA Modules:
  0.0 219.2 jit_solution(17407764692540543795)
XLA Ops:
  1.3 0.7 concatenate.22
  1.9 0.7 concatenate.24
  2.6 1.3 maximum_convert_fusion.refs_6_
  4.0 1.3 reshape.104.refs_5_
  5.2 0.6 broadcast_in_dim.10.refs_9_
  5.8 0.7 fusion.2
  6.5 0.1 reshape.101
  6.6 0.7 convert_reduce_fusion
  7.3 0.1 reshape.105
  7.4 0.6 pad_convert_fusion.refs_3_
  8.0 1.7 pad_maximum_fusion.refs_0_
  9.7 128.5 %run_layer.1 = (bf16[256,768]{1,0:T(8,128)(2,1)}, bf16[256,768]{1,0:T(8,128)(2,1)}, f32[8,1,1408]{2,1,0:T(1,128)}, f32[32,1,256]{2,1,0:T(1,128)}, bf16[768,3072]...) custom-call(bf16[192,384]{1,0:T(8,128)(2,1)} %pad_maximum_fusion.refs_0_, ...), custom_call_target="tpu_custom_call" | custom-call | tf_op jit(solution)/shard_map/run_layer/pallas_call | solution.py:955
  138.2 0.0 copy-start
  138.2 0.9 copy-done
  139.1 0.0 copy-start.1
  139.1 0.8 copy-done.1
  139.9 0.0 copy-start.2
  139.9 0.8 copy-done.2
  140.7 0.0 copy-start.4
  140.7 0.0 copy-start.3
  140.7 70.3 %scatter_shards.1 = (f32[192,384]{1,0:T(8,128)S(1)}, f32[192,384]{1,0:T(8,128)S(1)}, f32[96,768]{1,0:T(8,128)S(1)}, f32[192,576]{1,0:T(8,128)S(1)}, f32[1,1408]{1,0:T(1,128)S(1)}, /*index=5*/f32[4,1,256]{2,1,0:T(1,128)S(1)}) custom-call(bf16[768,3072]{1,0:T(8,128)(2,1)} %get-tuple-element.28.refs_0_, bf16[768,3072]{1,0:T(8,128)(2,1)} %get-tuple-element.29.refs_1_, ...), custom_call_target="tpu_custom_call" | custom-call | tf_op jit(solution)/shard_map/scatter_shards/pallas_call | solution.py:443
  211.0 0.7 reshape.102
  211.7 0.6 slice.27
  212.2 0.6 slice_bitcast_fusion
  212.8 0.7 slice_reduce_fusion.2
  213.5 0.6 slice_reduce_fusion.1
  214.1 0.7 slice.28
  214.8 0.0 copy-done.4
  214.8 0.7 copy.35
  215.6 0.0 copy-done.3
  215.6 0.7 copy.36
  216.3 0.8 copy.37
  217.1 0.7 copy.38
  217.8 0.7 copy.39
  218.5 0.7 copy.40
  (2 shorter events, 0.0 us)
Async XLA Ops:
  138.2 0.9 copy-start
  139.1 0.8 copy-start.1
  139.9 0.8 copy-start.2
  140.7 74.1 %copy-start.4 = (bf16[256,768]{1,0:T(8,128)(2,1)S(1)}, bf16[256,768]{1,0:T(8,128)(2,1)}, u32[]{:S(2)}) copy-start(bf16[256,768]{1,0:T(8,128)(2,1)} %get-tuple-element.26) | copy-start | bytes 1179652
  140.7 74.9 %copy-start.3 = (bf16[256,768]{1,0:T(8,128)(2,1)S(1)}, bf16[256,768]{1,0:T(8,128)(2,1)}, u32[]{:S(2)}) copy-start(bf16[256,768]{1,0:T(8,128)(2,1)} %get-tuple-element.27) | copy-start | bytes 1179652

commit v3 on v2

--- a/solution.py
+++ b/solution.py
@@ -599,21 +599,136 @@
             copy.wait_send()
 
 
+class Scatter:
+    def __init__(self, rows, depth, where, shapes, grads, buffers, sems):
+        self.rows, self.depth, self.shapes, self.grads = rows, depth, shapes, grads
+        self.dp, self.z, self.core, self.others = where
+        self.held, self.planes_in, self.crosses_in, self.alongs_in = (
+            buffers[3 * kind : 3 * kind + 3] for kind in range(4))
+        (
+            self.pair_send, self.pair_recv, self.plane_send, self.plane_recv,
+            self.cross_send, self.cross_recv, self.along_send, self.along_recv,
+        ) = sems
+        self.sibling = place(self.dp, self.z, 1 - self.core)
+        self.targets = [self.dp ^ 3, self.dp ^ 1, self.dp ^ 2, self.dp]
+        self.lines = [(self.z + step) % depth for step in z_order(depth)[::-1]]
+        self.units = [(part, turn) for part in (2, 1, 0) for turn in range(depth)]
+        self.pairs, self.planes, self.crosses, self.alongs = {}, {}, {}, {}
+
+    def remote(self, source, destination, send_sem, recv_sem, target):
+        copy = pltpu.make_async_remote_copy(
+            src_ref=source, dst_ref=destination, send_sem=send_sem, recv_sem=recv_sem,
+            device_id=target, device_id_type=MESH_IDS)
+        copy.start()
+        return copy
+
+    def block(self, part, line, target):
+        return block_of(self.grads[part], line, target, self.shapes[part], part == 2)
+
+    def add(self, first, others_in, length, target):
+        chunk = 48
+
+        @pl.loop(0, length // chunk)
+        def _(index):
+            piece = pl.ds(pl.multiple_of(index * chunk, chunk), chunk)
+            total = first[piece, :].astype(jnp.float32)
+            for other in others_in:
+                total = total + other[piece, :].astype(jnp.float32)
+            target[piece, :] = total.astype(target.dtype)
+
+    def start_pairs(self, part):
+        for turn, line in enumerate(self.lines):
+            for slot, target in enumerate(self.targets):
+                key = (part, turn, slot)
+                self.pairs[key] = self.remote(
+                    self.block(part, line * 2 + 1 - self.core, target),
+                    self.held[part].at[turn, slot], self.pair_send.at[key],
+                    self.pair_recv.at[key], self.sibling)
+
+    def wait_pairs_sent(self, part):
+        for turn in range(self.depth):
+            for slot in range(self.rows):
+                self.pairs[part, turn, slot].wait_send()
+
+    def turn(self, index):
+        last = self.rows - 1
+        count = len(self.units)
+        if index < count:
+            part, turn = self.units[index]
+            height = self.shapes[part][0]
+            half = height // 2
+            for slot, target in enumerate(self.targets):
+                self.pairs[part, turn, slot].wait_recv()
+                here = self.held[part].at[turn, slot]
+                own = self.block(part, self.lines[turn] * 2 + self.core, target)
+                self.add(own, [here], height, here)
+                if slot == 0:
+                    for position in range(2):
+                        key = (part, turn, position)
+                        self.crosses[key] = self.remote(
+                            self.held[part].at[turn, 0, pl.ds((1 - position) * half, half)],
+                            self.crosses_in[part].at[turn, position],
+                            self.cross_send.at[key], self.cross_recv.at[key],
+                            place(self.others[position], self.z, self.core))
+        if 1 <= index <= count:
+            part, turn = self.units[index - 1]
+            half = self.shapes[part][0] // 2
+            for position in range(2):
+                self.crosses[part, turn, 1 - position].wait_recv()
+                piece = self.held[part].at[turn, 1 + position, pl.ds(position * half, half)]
+                self.add(piece, [self.crosses_in[part].at[turn, 1 - position]], half, piece)
+                key = (part, turn, position)
+                self.planes[key] = self.remote(
+                    self.held[part].at[turn, 1 + position], self.planes_in[part].at[turn, position],
+                    self.plane_send.at[key], self.plane_recv.at[key],
+                    place(self.others[position], self.z, self.core))
+        if 2 <= index:
+            part, turn = self.units[index - 2]
+            for position in range(2):
+                self.planes[part, turn, position].wait_recv()
+            here = self.held[part].at[turn, last]
+            arrived = [self.planes_in[part].at[turn, position] for position in range(2)]
+            self.add(here, arrived, self.shapes[part][0], here)
+            if turn < self.depth - 1:
+                key = (part, turn)
+                self.alongs[key] = self.remote(
+                    here, self.alongs_in[part].at[turn], self.along_send.at[key],
+                    self.along_recv.at[key], place(self.dp, self.lines[turn], self.core))
+
+    def finish_part(self, part):
+        total = self.held[part][self.depth - 1, self.rows - 1].astype(jnp.float32)
+        for turn in range(self.depth - 1):
+            self.alongs[part, turn].wait_recv()
+            total = total + self.alongs_in[part][turn].astype(jnp.float32)
+        return total
+
+    def wait_sends(self):
+        for copies in (self.planes, self.crosses, self.alongs):
+            for copy in copies.values():
+                copy.wait_send()
+
+
 def layer_kernel(rows, depth, *refs):
     shards = refs[:3]
-    cond_rows, ada_ref, ada_bias, bias_row, latents, cotangent, live_ref = refs[3:10]
-    block_out, latent_grad, leaving, cond_in = refs[10:14]
-    grads_out = refs[14:17]
-    weights, grads = refs[17:20], refs[20:23]
+    cond_rows, slope, ada_ref, ada_bias, bias_row, latents, cotangent, live_ref = refs[3:11]
     (
-        own_sems, send_sems, recv_sems, out_sems, bias_in, part_out, part_in,
+        block_out, latent_grad, cond_grad, ada_grad, ada_bias_grad, qkv_grad, qv_bias_grad,
+        proj_grad, proj_bias_grad, fc1_grad, fc1_bias_grad, fc2_grad, fc2_bias_grad,
+    ) = refs[11:24]
+    refs = refs[24:]
+    weights, grads = refs[:3], (refs[3], refs[4], refs[3])
+    scatter_buffers, scatter_sems = refs[5:17], refs[17:25]
+    (
+        own_sems, send_sems, recv_sems, bias_in, part_out, part_in,
         cond_send, cond_recv, part_send, part_recv, bias_send, bias_recv,
+        leaving, cond_in, all_rows, back_out, back_in, row_send, row_recv, back_send, back_recv,
         mod, qkv_bias, proj_bias, fc1_bias, fc2_bias, mod_grad, qkv_sums, proj_sums, fc1_sums,
         fc2_sums, inverse_one, inverse_two, normed_one, normed_two, middle, branch, wide,
         hidden_one, hidden_one_t, hidden_two, hidden_two_t, attended, attended_t,
-        grad_mlp, grad_mlp_t, grad_attended, projected, grad_natural, grad_mixed,
+        grad_mlp, grad_mlp_t, grad_attended, projected,
         grad_proj_mixed, activated, grad_pre, probability,
-    ) = refs[23:]
+    ) = refs[25:]
+    grad_natural, grad_mixed = activated, grad_pre
     mixed, fc1, fc2_turned = weights
     where = positions(rows, depth)
     dp = where[0]
@@ -627,8 +742,17 @@
     rest = block - edge
     lead = qkv_part - edge
     scale_factor = HEAD ** (-0.5)
+    ada_rows, mod_width = ada_ref.shape
+    mod_pad = round_up(mod_width)
     enter_barrier(me, rows, columns)
     gather = Gather(rows, depth, where, shards, weights, own_sems, send_sems, recv_sems)
+    scatter = Scatter(
+        rows, depth, where, [shard.shape for shard in shards], grads, scatter_buffers, scatter_sems)
+    row_swap = Exchange(
+        me, rows, columns, lambda target: leaving.at[lax.rem(target, columns)], all_rows,
+        row_send, row_recv)
+    back_swap = Exchange(
+        me, rows, columns, lambda target: back_out.at[target], back_in, back_send, back_recv)
 
     cond_swap = Exchange(
         me, rows, columns, lambda target: cond_rows.at[target // columns], cond_in,
@@ -783,11 +907,6 @@
             part = span(index, chunk)
             grads[2][:, part] = dot_plain(grad_mlp_t[...], activated[:, part]).astype(bfloat)
 
-    def leave(part):
-        copy = pltpu.make_async_copy(grads[part], grads_out[part], out_sems.at[part])
-        copy.start()
-        return copy
-
     hooks = {
         0: start_modulation,
         1: normalize_first,
@@ -814,130 +933,191 @@
         gather.turn(index)
         if index in hooks:
             hooks[index]()
-    copies = [leave(2)]
+    scatter.start_pairs(2)
     gather.finish_part(2)
-
     third = 256
 
-    @pl.loop(0, D // third)
-    def _(index):
-        part = span(index, third)
-        branch_part = against_weight(activated[...], fc2_turned[part, :]) + fc2_bias[:, part]
-        live_grad = live_ref[:, part] * cotangent[:, part].astype(jnp.float32)
-        gate = mod[:, pl.ds(pl.multiple_of(5 * D + index * third, third), third)]
-        block_out[:, part] = (
-            live_ref[:, part] * (middle[:, part] + gate * branch_part)).astype(bfloat)
-        mod_grad[:, pl.ds(pl.multiple_of(5 * D + index * third, third), third)] = columns_sum(
-            live_grad * branch_part)
-
-    @pl.loop(0, chunks)
-    def _(index):
-        part = span(index, chunk)
-        grad = (dot_plain(grad_mlp[...], fc2_turned[:, part]) * wide[:, part]).astype(bfloat)
-        grad_pre[:, part] = grad
-        fc1_sums[:, part] = columns_sum(grad.astype(jnp.float32))
-        grads[1][:, part] = dot_plain(hidden_two_t[...], grad).astype(bfloat)
-
-    copies.append(leave(1))
-
-    @pl.loop(0, D // third)
-    def _(index):
-        part = span(index, third)
-        middle[:, part] = against_weight(grad_pre[...], fc1[part, :])
-
-    grad_hidden = middle[...]
-    mod_grad[:, 3 * D : 4 * D] = columns_sum(grad_hidden)
-    mod_grad[:, 4 * D : 5 * D] = columns_sum(grad_hidden * normed_two[...])
-    grad_middle = live_ref[...] * cotangent[...].astype(jnp.float32) + norm_backward(
-        grad_hidden * (1.0 + piece(4)), normed_two[...], inverse_two[...])
-    mod_grad[:, 2 * D : 3 * D] = columns_sum(grad_middle * branch[...])
-    middle[...] = grad_middle
-    grad_branch = (piece(2) * grad_middle).astype(bfloat)
-    proj_sums[...] = columns_sum(grad_branch.astype(jnp.float32))
-    for index in range(columns):
-        grad_proj_mixed[:, index * rest : index * rest + lead] = jnp.zeros((length, lead), bfloat)
-        grad_proj_mixed[:, index * rest + lead : (index + 1) * rest] = (
-            grad_branch[:, index * proj_part : (index + 1) * proj_part])
-    total = None
-    for index in range(columns):
-        term = against_weight(
-            grad_proj_mixed[:, index * rest : (index + 1) * rest],
-            mixed[:, index * block + edge : (index + 1) * block])
-        total = term if total is None else total + term
-    grad_attended[...] = total.astype(bfloat)
-
-    @pl.loop(0, HEADS // 2)
-    def _(pair):
-        queries, keys, values = head_slabs(projected, pair)
-        grad_out = grad_attended[:, span(pair, 128)]
-        zero = jnp.zeros_like(grad_out)
-        results = []
-        for which in range(2):
-            exact = probability[2 * pair + which]
-            grad_prob = against_weight(jnp.where(own_lanes(which), grad_out, zero), values)
-            inner = jnp.sum(exact * grad_prob, axis=-1, keepdims=True)
-            grad_scores = (exact * (grad_prob - inner)).astype(bfloat)
-            results.append((
-                dot_plain(grad_scores, keys) * scale_factor,
-                contract_rows(grad_scores, queries) * scale_factor,
-                contract_rows(exact.astype(bfloat), grad_out)))
-        for kind in range(3):
-            grad_natural[:, pl.ds(pl.multiple_of(kind * D + pair * 128, 128), 128)] = jnp.where(
-                own_lanes(0), results[0][kind], results[1][kind]).astype(bfloat)
-
-    qkv_sums[...] = columns_sum(grad_natural[...].astype(jnp.float32))
-    for index in range(columns):
-        grad_mixed[:, index * block : index * block + qkv_part] = (
-            grad_natural[:, index * qkv_part : (index + 1) * qkv_part])
-        grad_mixed[:, index * block + qkv_part : (index + 1) * block] = jnp.zeros(
-            (length, proj_part), bfloat)
-
-    @pl.loop(0, columns)
-    def _(index):
-        low = pl.multiple_of(index * block, 128)
-        grads[0][:, pl.ds(low, edge)] = dot_plain(
-            hidden_one_t[...], grad_mixed[:, pl.ds(low, edge)]).astype(bfloat)
-        tail = pl.ds(pl.multiple_of(index * block + edge, 128), rest)
-        grads[0][:, tail] = (
-            dot_plain(hidden_one_t[...], grad_mixed[:, tail])
-            + dot_plain(attended_t[...], grad_proj_mixed[:, span(index, rest)])).astype(bfloat)
-
-    copies.append(leave(0))
-
-    @pl.loop(0, D // third)
-    def _(index):
-        part = span(index, third)
-        branch[:, part] = against_weight(grad_mixed[...], mixed[part, :])
-
-    grad_hidden = branch[...]
-    mod_grad[:, :D] = columns_sum(grad_hidden)
-    mod_grad[:, D : 2 * D] = columns_sum(grad_hidden * normed_one[...])
-    latent_grad[...] = (middle[...] + norm_backward(
-        grad_hidden * (1.0 + piece(1)), normed_one[...], inverse_one[...])).astype(bfloat)
-    width = ada_ref.shape[1]
-    pad = jnp.zeros((1, round_up(width) - width), jnp.float32)
-    qv_sums = jnp.concatenate([qkv_sums[:, :D], qkv_sums[:, 2 * D :]], axis=1)
-    rows_of = (qv_sums, proj_sums[...], fc1_sums[...], fc2_sums[...])
-    every = mod_grad[...]
-    for index in range(columns):
-        pieces = [every[:, index * width : (index + 1) * width], pad]
-        for row in rows_of:
-            share = row.shape[1] // columns
-            pieces.append(row[:, index * share : (index + 1) * share])
-        leaving[index] = jnp.concatenate(pieces, axis=1)
-    for copy in copies:
-        copy.wait()
+    def finish_forward():
+        @pl.loop(0, D // third)
+        def _(index):
+            part = span(index, third)
+            branch_part = against_weight(activated[...], fc2_turned[part, :]) + fc2_bias[:, part]
+            live_grad = live_ref[:, part] * cotangent[:, part].astype(jnp.float32)
+            last = pl.ds(pl.multiple_of(5 * D + index * third, third), third)
+            block_out[:, part] = (
+                live_ref[:, part] * (middle[:, part] + mod[:, last] * branch_part)).astype(bfloat)
+            mod_grad[:, last] = columns_sum(live_grad * branch_part)
+
+    def fc1_weight_grad(low, high):
+        @pl.loop(low, high)
+        def _(index):
+            part = span(index, chunk)
+            grad = (dot_plain(grad_mlp[...], fc2_turned[:, part]) * wide[:, part]).astype(bfloat)
+            grad_pre[:, part] = grad
+            fc1_sums[:, part] = columns_sum(grad.astype(jnp.float32))
+            grads[1][:, part] = dot_plain(hidden_two_t[...], grad).astype(bfloat)
+
+    def hidden_two_back():
+        @pl.loop(0, D // third)
+        def _(index):
+            part = span(index, third)
+            middle[:, part] = against_weight(grad_pre[...], fc1[part, :])
+
+    def middle_back():
+        grad_hidden = middle[...]
+        mod_grad[:, 3 * D : 4 * D] = columns_sum(grad_hidden)
+        mod_grad[:, 4 * D : 5 * D] = columns_sum(grad_hidden * normed_two[...])
+        grad_middle = live_ref[...] * cotangent[...].astype(jnp.float32) + norm_backward(
+            grad_hidden * (1.0 + piece(4)), normed_two[...], inverse_two[...])
+        mod_grad[:, 2 * D : 3 * D] = columns_sum(grad_middle * branch[...])
+        middle[...] = grad_middle
+        grad_branch = (piece(2) * grad_middle).astype(bfloat)
+        proj_sums[...] = columns_sum(grad_branch.astype(jnp.float32))
+        for index in range(columns):
+            grad_proj_mixed[:, index * rest : index * rest + lead] = jnp.zeros(
+                (length, lead), bfloat)
+            grad_proj_mixed[:, index * rest + lead : (index + 1) * rest] = (
+                grad_branch[:, index * proj_part : (index + 1) * proj_part])
+        total = None
+        for index in range(columns):
+            term = against_weight(
+                grad_proj_mixed[:, index * rest : (index + 1) * rest],
+                mixed[:, index * block + edge : (index + 1) * block])
+            total = term if total is None else total + term
+        grad_attended[...] = total.astype(bfloat)
+
+    def attend_back(low, high):
+        @pl.loop(low, high)
+        def _(pair):
+            queries, keys, values = head_slabs(projected, pair)
+            grad_out = grad_attended[:, span(pair, 128)]
+            zero = jnp.zeros_like(grad_out)
+            results = []
+            for which in range(2):
+                exact = probability[2 * pair + which]
+                grad_prob = against_weight(jnp.where(own_lanes(which), grad_out, zero), values)
+                inner = jnp.sum(exact * grad_prob, axis=-1, keepdims=True)
+                grad_scores = (exact * (grad_prob - inner)).astype(bfloat)
+                results.append((
+                    dot_plain(grad_scores, keys) * scale_factor,
+                    contract_rows(grad_scores, queries) * scale_factor,
+                    contract_rows(exact.astype(bfloat), grad_out)))
+            for kind in range(3):
+                grad_natural[:, pl.ds(pl.multiple_of(kind * D + pair * 128, 128), 128)] = jnp.where(
+                    own_lanes(0), results[0][kind], results[1][kind]).astype(bfloat)
+
+    def mixed_weight_grad():
+        qkv_sums[...] = columns_sum(grad_natural[:, : 3 * D].astype(jnp.float32))
+        for index in range(columns):
+            grad_mixed[:, index * block : index * block + qkv_part] = (
+                grad_natural[:, index * qkv_part : (index + 1) * qkv_part])
+            grad_mixed[:, index * block + qkv_part : (index + 1) * block] = jnp.zeros(
+                (length, proj_part), bfloat)
+        scatter.wait_pairs_sent(2)
+
+        @pl.loop(0, columns)
+        def _(index):
+            low = pl.multiple_of(index * block, 128)
+            grads[0][:, pl.ds(low, edge)] = dot_plain(
+                hidden_one_t[...], grad_mixed[:, pl.ds(low, edge)]).astype(bfloat)
+            tail = pl.ds(pl.multiple_of(index * block + edge, 128), rest)
+            grads[0][:, tail] = (
+                dot_plain(hidden_one_t[...], grad_mixed[:, tail])
+                + dot_plain(attended_t[...], grad_proj_mixed[:, span(index, rest)])).astype(bfloat)
+
+    def finish_backward():
+        @pl.loop(0, D // third)
+        def _(index):
+            part = span(index, third)
+            branch[:, part] = against_weight(grad_mixed[...], mixed[part, :])
+
+        grad_hidden = branch[...]
+        mod_grad[:, :D] = columns_sum(grad_hidden)
+        mod_grad[:, D : 2 * D] = columns_sum(grad_hidden * normed_one[...])
+        latent_grad[...] = (middle[...] + norm_backward(
+            grad_hidden * (1.0 + piece(1)), normed_one[...], inverse_one[...])).astype(bfloat)
+        pad = jnp.zeros((1, mod_pad - mod_width), jnp.float32)
+        qv_sums = jnp.concatenate([qkv_sums[:, :D], qkv_sums[:, 2 * D :]], axis=1)
+        rows_of = (qv_sums, proj_sums[...], fc1_sums[...], fc2_sums[...])
+        every = mod_grad[...]
+        for index in range(columns):
+            pieces = [every[:, index * mod_width : (index + 1) * mod_width], pad]
+            for row in rows_of:
+                share = row.shape[1] // columns
+                pieces.append(row[:, index * share : (index + 1) * share])
+            leaving[index] = jnp.concatenate(pieces, axis=1)
+        row_swap.start()
+
+    def own_sums():
+        row_swap.wait_arrivals()
+        arrived = all_rows[:, 0, :]
+        sums = columns_sum(arrived)
+        ada_bias_grad[...] = sums[:, :mod_width]
+        low = mod_pad
+        for out in (qv_bias_grad, proj_bias_grad, fc1_bias_grad, fc2_bias_grad):
+            out[...] = sums[:, low : low + out.shape[1]]
+            low += out.shape[1]
+        ada_grad[...] = contract_exact(cond_in[:, 0, :ada_rows], arrived[:, :mod_width])
+        back_out[:, 0, :ada_rows] = lax.dot_general(
+            arrived[:, :mod_width], ada_ref[...].astype(jnp.float32), (((1,), (1,)), ((), ())),
+            precision=highest)
+        back_swap.start()
+
+    fc1_weight_grad(0, 4)
+    scatter.turn(0)
+    fc1_weight_grad(4, 8)
+    scatter.start_pairs(1)
+    scatter.turn(1)
+    finish_forward()
+    hidden_two_back()
+    scatter.turn(2)
+    middle_back()
+    scatter.turn(3)
+    attend_back(0, 2)
+    scatter.turn(4)
+    attend_back(2, 4)
+    scatter.turn(5)
+    attend_back(4, 6)
+    scatter.turn(6)
+    mixed_weight_grad()
+    scatter.start_pairs(0)
+    scatter.turn(7)
+    finish_backward()
+    fc2_grad[...] = scatter.finish_part(2).T
+    scatter.turn(8)
+    scatter.turn(9)
+    own_sums()
+    scatter.turn(10)
+    fc1_grad[...] = scatter.finish_part(1)
+    scatter.turn(11)
+    scatter.turn(12)
+    back_swap.wait_arrivals()
+    terms = []
+    for row in range(rows):
+        total = back_in[row * columns]
+        for source in range(1, columns):
+            total = total + back_in[row * columns + source]
+        terms.append(total[:, :ada_rows])
+    cond_grad[...] = jnp.concatenate(terms, axis=1) * slope[...]
+    scatter.turn(13)
+    total = scatter.finish_part(0)
+    qkv_grad[...] = total[:, :qkv_part]
+    proj_grad[...] = total[:, qkv_part:]
+    scatter.wait_pairs_sent(1)
+    scatter.wait_pairs_sent(0)
+    scatter.wait_sends()
     gather.wait_sends()
-    cond_swap.wait_sends()
-    part_swap.wait_sends()
-
-
-def run_layer(shards, cond_rows, ada_weight, ada_bias, bias_row, latents, cotangent, live,
-              rows, columns):
+    for swap in (cond_swap, part_swap, row_swap, back_swap):
+        swap.wait_sends()
+
+
+def run_layer(shards, cond_rows, slope, ada_weight, ada_bias, bias_row, latents, cotangent, live,
+              widths, rows, columns):
     depth = columns // 2
     count = (depth - 1) + depth * rows + depth * (rows - 1) + 2 * depth
     total = rows * columns
-    mod_pad = round_up(ada_weight.shape[1])
+    ada_rows, mod_width = ada_weight.shape
+    mod_pad = round_up(mod_width)
     bias_width = bias_row.shape[-1]
     length = latents.shape[0]
     vmem = pl.BlockSpec(memory_space=pltpu.VMEM)
@@ -951,33 +1131,53 @@
     half = lambda width: pltpu.VMEM((length, width), bfloat)
     turned = pltpu.VMEM((D, length), bfloat)
     rest = 128 * columns
-    row_out = lambda count, width: jax.ShapeDtypeStruct((count, 1, width), jnp.float32)
+    buffers = []
+    for lead in ((depth, rows), (depth, 2), (depth, 2), (depth - 1,)):
+        for shard in shards:
+            height, width = shard.shape
+            height = height // 2 if 6 <= len(buffers) < 9 else height
+            buffers.append(pltpu.VMEM(lead + (height, width), bfloat))
+    float_out = lambda *shape: jax.ShapeDtypeStruct(shape, jnp.float32)
+    qkv_part, proj_part = 3 * D // columns, D // columns
+    height = shards[0].shape[0]
     return pl.pallas_call(
         functools.partial(layer_kernel, rows, depth),
         out_shape=[
             jax.ShapeDtypeStruct((length, D), bfloat),
             jax.ShapeDtypeStruct((length, D), bfloat),
-            row_out(columns, mod_pad + bias_width),
-            row_out(total, cond_rows.shape[-1]),
-        ] + [jax.ShapeDtypeStruct(shape, bfloat) for shape in shapes],
-        in_specs=[anywhere] * 3 + [vmem] * 7,
-        out_specs=[vmem] * 4 + [anywhere] * 3,
-        scratch_shapes=[pltpu.VMEM(shape, bfloat) for shape in shapes] * 2 + [
-            dma((3,)), dma((3 * count,)), dma((2, 3, columns, rows)), dma((3,)),
+            float_out(1, D),
+            float_out(ada_rows, mod_width), float_out(1, mod_width),
+            float_out(height, qkv_part), float_out(1, widths[0]),
+            float_out(height, proj_part), float_out(1, widths[1]),
+            float_out(*shards[1].shape), float_out(1, widths[2]),
+            float_out(*shards[2].shape[::-1]), float_out(1, widths[3]),
+        ],
+        in_specs=[anywhere] * 3 + [vmem] * 8,
+        out_specs=[vmem] * 13,
+        scratch_shapes=[pltpu.VMEM(shape, bfloat) for shape in shapes + shapes[:2]]
+        + buffers + [
+            dma((3, depth, rows)), dma((3, depth, rows)),
+            dma((3, depth, 2)), dma((3, depth, 2)), dma((3, depth, 2)), dma((3, depth, 2)),
+            dma((3, depth - 1)), dma((3, depth - 1)),
+            dma((3,)), dma((3 * count,)), dma((2, 3, columns, rows)),
             row_buffer(columns, bias_width), row_buffer(total, mod_pad), row_buffer(total, mod_pad),
             dma((total,)), dma((total,)), dma((total,)), dma((total,)),
             dma((columns,)), dma((columns,)),
+            row_buffer(columns, mod_pad + bias_width), row_buffer(total, cond_rows.shape[-1]),
+            row_buffer(total, mod_pad + bias_width),
+            row_buffer(total, round_up(ada_rows)), row_buffer(total, round_up(ada_rows)),
+            dma((total,)), dma((total,)), dma((total,)), dma((total,)),
             wide_row(6 * D), wide_row(3 * D), wide_row(D), wide_row(FF), wide_row(D),
             wide_row(6 * D), wide_row(3 * D), wide_row(D), wide_row(FF), wide_row(D),
             single(1), single(1), single(D), single(D), single(D), single(D), single(FF),
             half(D), turned, half(D), turned, half(D), turned,
-            half(D), turned, half(D), half(3 * D), half(3 * D), half(4 * D),
+            half(D), turned, half(D), half(3 * D),
             half(rest), half(FF), half(FF), pltpu.VMEM((HEADS, length, length), jnp.float32),
         ],
         compiler_params=pltpu.CompilerParams(
-            collective_id=2, has_side_effects=True, vmem_limit_bytes=60 * 2**20),
+            collective_id=2, has_side_effects=True, vmem_limit_bytes=62 * 2**20),
         name="run_layer",
-    )(*shards, cond_rows, ada_weight, ada_bias, bias_row, latents, cotangent, live)
+    )(*shards, cond_rows, slope, ada_weight, ada_bias, bias_row, latents, cotangent, live)
 
 
 def pick(mixed, columns, kind):
@@ -1168,7 +1368,7 @@
 
     cond_row = conditioning.astype(jnp.float32)
     cond_act, silu_pull = jax.vjp(jax.nn.silu, cond_row)
-    slope = split_cond(silu_pull(jnp.ones_like(cond_row))[0])
+    slope = silu_pull(jnp.ones_like(cond_row))[0]
     cond_rows = split_cond(cond_act.astype(bfloat).astype(jnp.float32))
     bias_row = jnp.concatenate(own_biases).astype(jnp.float32).reshape(1, -1)
 
@@ -1182,31 +1382,34 @@
     ada_row = ada_bias.astype(jnp.float32).reshape(1, -1)
     fused = rows == 4 and columns == 8
     if fused:
-        block_out, latent_grad, leaving, cond_in, *grads = run_layer(
-            shards, cond_rows, ada_weight, ada_row, bias_row, latents[0], cotangent[0],
-            jnp.full((1, D), live), rows, columns)
-    else:
-        *blocks, mod_blocks, bias_blocks, cond_in = gather_shards(
-            shards, cond_rows, ada_weight, ada_row, bias_row,
-            rows, columns)
-        modulation = mod_blocks[:, :, :mod_width].reshape(1, -1)
-        biases = tuple(
-            bias_blocks[:, :, cut : cut + width].reshape(-1) for cut, width in zip(cuts, widths)
-        )
-        weights = [flatten_blocks(block, part == 2) for part, block in enumerate(blocks)]
-        block_out, latent_grad, mod_grad, weight_grads, bias_grads = layer(
-            latents[0], live, cotangent[0], modulation, weights, biases, columns
-        )
-        grads = [
-            cut_blocks(grad, shapes[part], part == 2, rows, columns)
-            for part, grad in enumerate(weight_grads)
-        ]
-        leaving = jnp.concatenate(
-            [jnp.pad(mod_grad.reshape(columns, -1), ((0, 0), (0, mod_pad - mod_width)))]
-            + [grad.reshape(columns, -1) for grad in bias_grads], axis=1
-        ).reshape(columns, 1, -1)
+        block_out, latent_grad, *param_grads = run_layer(
+            shards, cond_rows, slope, ada_weight, ada_row, bias_row, latents[0], cotangent[0],
+            jnp.full((1, D), live), widths, rows, columns)
+        param_grads = [
+            grad.reshape(-1) if 0 < place < 11 and place % 2 == 0 else grad
+            for place, grad in enumerate(param_grads)]
+        return (block_out[None], latent_grad[None], *param_grads)
+    *blocks, mod_blocks, bias_blocks, cond_in = gather_shards(
+        shards, cond_rows, ada_weight, ada_row, bias_row,
+        rows, columns)
+    modulation = mod_blocks[:, :, :mod_width].reshape(1, -1)
+    biases = tuple(
+        bias_blocks[:, :, cut : cut + width].reshape(-1) for cut, width in zip(cuts, widths)
+    )
+    weights = [flatten_blocks(block, part == 2) for part, block in enumerate(blocks)]
+    block_out, latent_grad, mod_grad, weight_grads, bias_grads = layer(
+        latents[0], live, cotangent[0], modulation, weights, biases, columns
+    )
+    grads = [
+        cut_blocks(grad, shapes[part], part == 2, rows, columns)
+        for part, grad in enumerate(weight_grads)
+    ]
+    leaving = jnp.concatenate(
+        [jnp.pad(mod_grad.reshape(columns, -1), ((0, 0), (0, mod_pad - mod_width)))]
+        + [grad.reshape(columns, -1) for grad in bias_grads], axis=1
+    ).reshape(columns, 1, -1)
     mixed_grad, fc1_grad, fc2_turned_grad, ada_grad, sums, cond_grad = scatter_shards(
-        grads, leaving, cond_in, ada_weight, slope, shapes, rows, columns)
+        grads, leaving, cond_in, ada_weight, split_cond(slope), shapes, rows, columns)
     qkv_grad, proj_grad = mixed_grad[:, :qkv_width], mixed_grad[:, qkv_width:]
     fc2_grad = fc2_turned_grad.T
     ada_bias_grad = sums[0, :mod_width]

time: 220 us -> 203 us (0.923)
  Pallas kernels: 199 us -> 180 us
  other arithmetic: 5.03 us -> 8.15 us
    pallas_call x1 -> x0, Pallas kernels: 70.3 us -> none  [scatter_shards(): pl.pallas_call(functools.partial(scatter_kernel, rows, depth), out_shape=...]
    pallas_call x1, Pallas kernels: 128 us -> 180 us  [run_layer(): pl.pallas_call(functools.partial(layer_kernel, rows, depth), out_shape=[j...]
    slice x5 -> x0, local copies, waits for them, and re-layouts: 2.59 us -> none  [the longest x2 1.23 us: per_device(): sums[0, mod_pad + cut:mod_pad + cut + width]]
    pallas_call x0 -> x2, other arithmetic: none -> 2.57 us  [run_layer(): pl.pallas_call(functools.partial(layer_kernel, rows, depth), out_shape=[j...]
    unnamed x16 -> x33, local copies, waits for them, and re-layouts: 6.9 us -> 9.18 us
where the time goes in v3:
time: 203 us; the launch traced here: 202 us
  Pallas kernels  180 us (89%)
  local copies, waits for them, and re-layouts  12.4 us (6%)
  other arithmetic  8.15 us (4%)
    pallas_call x1, Pallas kernels, run_layer(): pl.pallas_call(functools.partial(layer_kernel, rows, depth), out_shape=[j...  180 us
    unnamed x33, local copies, waits for them, and re-layouts  9.18 us

profile of v3, /device:TPU:0, one launch (start us, length us, event | category | flops | bytes accessed | tf_op | source)
XLA Modules:
  0.0 202.2 jit_solution(13689585152410206875)
XLA Ops:
  0.6 0.0 copy-start.6
  1.3 0.7 concatenate.22
  2.0 0.7 concatenate.24
  2.6 1.3 maximum_convert_fusion.refs_7_
  4.0 1.3 reshape.116.refs_6_
  5.2 0.6 broadcast_in_dim.10.refs_10_
  5.8 1.3 fusion.1
  7.1 0.7 convert_reduce_fusion
  7.8 0.1 reshape.117
  7.9 0.6 pad_convert_fusion.refs_3_
  8.5 0.0 copy-done.6
  8.5 1.7 pad_maximum_fusion.refs_0_
  10.2 180.3 %run_layer.1 = (bf16[256,768]{1,0:T(8,128)(2,1)}, bf16[256,768]{1,0:T(8,128)(2,1)}, f32[1,768]{1,0:T(1,128)}, f32[192,576]{1,0:T(8,128)}, f32[1,576]{1,0:T(1,128...) custom-call(bf16[192,384]{1,0:T(8,128)(2,1)} %pad_maximum_fusion.ref, ...), custom_call_target="tpu_custom_call" | custom-call | tf_op jit(solution)/shard_map/run_layer/pallas_call | solution.py:1143
  190.5 0.0 copy-start.2
  190.5 1.3 reduce.2
  191.8 1.3 reduce.1
  193.0 1.9 copy.28
  194.9 0.0 copy-done.2
  194.9 0.0 copy-start.1
  194.9 0.7 copy.40
  195.7 0.4 copy-done.1
  196.0 0.0 copy-start.7
  196.1 0.0 copy-start
  196.1 0.7 copy.41
  196.8 0.0 copy-done.7
  196.8 0.6 copy.42
  197.4 0.0 copy-done
  197.4 0.0 copy-start.4
  197.4 0.8 copy.43
  198.2 0.3 copy-done.4
  198.5 0.0 copy-start.8
  198.5 0.0 copy-start.5
  198.5 0.0 copy-start.3
  198.5 0.7 copy.44
  199.2 0.0 copy-done.8
  199.2 0.6 copy.45
  199.8 0.0 copy-done.5
  199.8 0.0 copy-start.10
  199.8 0.6 copy.46
  200.4 0.0 copy-done.10
  200.5 0.5 copy.47
  201.0 0.0 copy-done.3
  201.0 0.0 copy-start.9
  201.0 0.7 copy.48
  201.7 0.0 copy-done.9
  201.7 0.5 copy.49
Async XLA Ops:
  0.6 7.9 %copy-start.6 = (bf16[192,96]{1,0:T(8,128)(2,1)S(1)}, bf16[192,96]{1,0:T(8,128)(2,1)}, u32[]{:S(2)}) copy-start(bf16[192,96]{1,0:T(8,128)(2,1)} %param.22) | copy-start | bytes 110596
  190.5 4.5 %copy-start.2 = (bf16[256,768]{1,0:T(8,128)(2,1)S(1)}, bf16[256,768]{1,0:T(8,128)(2,1)}, u32[]{:S(2)}) copy-start(bf16[256,768]{1,0:T(8,128)(2,1)} %get-tuple-element.26) | copy-start | bytes 1179652
  194.9 1.1 copy-start.1
  196.0 0.8 copy-start.7
  196.1 1.3 copy-start
  197.4 1.1 copy-start.4
  198.5 0.7 copy-start.8
  198.5 1.3 copy-start.5
  198.5 2.5 %copy-start.3 = (f32[192,384]{1,0:T(8,128)S(1)}, f32[192,384]{1,0:T(8,128)}, u32[]{:S(2)}) copy-start(f32[192,384]{1,0:T(8,128)} %get-tuple-element.76) | copy-start | bytes 884740
  199.8 0.7 copy-start.10
  201.0 0.7 copy-start.9

commit v4 on v3

--- a/solution.py
+++ b/solution.py
@@ -14,6 +14,8 @@
 
 highest = lax.Precision.HIGHEST
 bfloat = jnp.bfloat16
+LAG = 2
+AHEAD = 3
 
 
 def place(dp_index, z_index, core):
@@ -499,6 +501,37 @@
     return jnp.sum(values, axis=0, keepdims=True)
 
 
+class Swap:
+    def __init__(self, me, size, device, row_for, landing, send_sems, recv_sems):
+        self.me, self.size, self.device = me, size, device
+        self.row_for, self.landing = row_for, landing
+        self.send_sems, self.recv_sems = send_sems, recv_sems
+        self.copies = []
+
+    def start(self):
+        for step in range(1, self.size):
+            other = lax.rem(self.me + step, self.size)
+            copy = pltpu.make_async_remote_copy(
+                src_ref=self.row_for(other),
+                dst_ref=self.landing.at[self.me],
+                send_sem=self.send_sems.at[step],
+                recv_sem=self.recv_sems.at[step],
+                device_id=self.device(other),
+                device_id_type=MESH_IDS,
+            )
+            copy.start()
+            self.copies.append(copy)
+        self.landing[self.me] = self.row_for(self.me)[...]
+
+    def wait_arrivals(self):
+        for copy in self.copies:
+            copy.wait_recv()
+
+    def wait_sends(self):
+        for copy in self.copies:
+            copy.wait_send()
+
+
 class Gather:
     def __init__(self, rows, depth, where, shards, outs, own_sems, send_sems, recv_sems):
         self.rows, self.depth = rows, depth
@@ -509,8 +542,7 @@
         self.sends = []
         self.keeps = []
         self.own = self.z * 2 + self.core
-        self.steps = z_order(depth)
-        self.lines = [((self.z - step) % depth) * 2 + self.core for step in self.steps]
+        self.lines = [(self.z ^ step) * 2 + self.core for step in range(depth)]
         self.units = [(part, turn) for part in range(3) for turn in range(depth)]
 
     def slot_of(self, part, line, row):
@@ -551,20 +583,27 @@
         ).wait_recv()
 
     def send_own(self, part):
-        dp, z, core = self.dp, self.z, self.core
         for other in self.others:
-            self.send(part, self.own, dp, place(other, z, core), own=True)
-        for step in self.steps[1:]:
-            self.send(part, self.own, dp, place(dp, (z + step) % self.depth, core), own=True)
-        self.send(part, self.own, dp, self.sibling, own=True)
+            self.send(part, self.own, self.dp, place(other, self.z, self.core), own=True)
+        self.send(part, self.own, self.dp, self.sibling, own=True)
         keep = pltpu.make_async_copy(
-            self.shards[part], self.slot_of(part, self.own, dp), self.own_sems.at[part])
+            self.shards[part], self.slot_of(part, self.own, self.dp), self.own_sems.at[part])
         keep.start()
         self.keeps.append(keep)
+
+    def send_deep(self, index):
+        if index < len(self.units):
+            part, step = self.units[index]
+            if step:
+                target = place(self.dp, self.z ^ step, self.core)
+                self.send(part, self.own, self.dp, target, own=True)
 
     def turn(self, index):
         dp, z, core = self.dp, self.z, self.core
         count = len(self.units)
+        self.send_deep(index + AHEAD)
+        if index in (1, 2):
+            self.send_own(index)
         if index < count:
             part, turn = self.units[index]
             line = self.lines[turn]
@@ -573,16 +612,16 @@
                 for other in self.others:
                     self.send(part, line, dp, place(other, z, core))
                 self.send(part, line, dp, self.sibling)
-        if 1 <= index <= count:
-            part, turn = self.units[index - 1]
+        if LAG <= index < count + LAG:
+            part, turn = self.units[index - LAG]
             line = self.lines[turn]
             for position, other in enumerate(self.others):
                 self.arrive(part, line, other)
                 self.send(
                     part, line, other, place(self.others[1 - position], z, core), which=position)
                 self.send(part, line, other, self.sibling)
-        if 2 <= index:
-            part, turn = self.units[index - 2]
+        if 2 * LAG <= index:
+            part, turn = self.units[index - 2 * LAG]
             line = self.lines[turn]
             self.arrive(part, line, dp ^ 3, 0)
             self.arrive(part, line, dp ^ 3, 1)
@@ -611,7 +650,7 @@
         ) = sems
         self.sibling = place(self.dp, self.z, 1 - self.core)
         self.targets = [self.dp ^ 3, self.dp ^ 1, self.dp ^ 2, self.dp]
-        self.lines = [(self.z + step) % depth for step in z_order(depth)[::-1]]
+        self.lines = [self.z ^ step for step in reversed(range(depth))]
         self.units = [(part, turn) for part in (2, 1, 0) for turn in range(depth)]
         self.pairs, self.planes, self.crosses, self.alongs = {}, {}, {}, {}
 
@@ -670,8 +709,8 @@
                             self.crosses_in[part].at[turn, position],
                             self.cross_send.at[key], self.cross_recv.at[key],
                             place(self.others[position], self.z, self.core))
-        if 1 <= index <= count:
-            part, turn = self.units[index - 1]
+        if LAG <= index < count + LAG:
+            part, turn = self.units[index - LAG]
             half = self.shapes[part][0] // 2
             for position in range(2):
                 self.crosses[part, turn, 1 - position].wait_recv()
@@ -682,8 +721,8 @@
                     self.held[part].at[turn, 1 + position], self.planes_in[part].at[turn, position],
                     self.plane_send.at[key], self.plane_recv.at[key],
                     place(self.others[position], self.z, self.core))
-        if 2 <= index:
-            part, turn = self.units[index - 2]
+        if 2 * LAG <= index:
+            part, turn = self.units[index - 2 * LAG]
             for position in range(2):
                 self.planes[part, turn, position].wait_recv()
             here = self.held[part].at[turn, last]
@@ -710,7 +749,7 @@
 
 def layer_kernel(rows, depth, *refs):
     shards = refs[:3]
-    cond_rows, slope, ada_ref, ada_bias, bias_row, latents, cotangent, live_ref = refs[3:11]
+    cond_rows, slope, ada_ref, ada_bias, bias_rows, latents, cotangent, live_ref = refs[3:11]
     (
         block_out, latent_grad, cond_grad, ada_grad, ada_bias_grad, qkv_grad, qv_bias_grad,
         proj_grad, proj_bias_grad, fc1_grad, fc1_bias_grad, fc2_grad, fc2_bias_grad,
@@ -719,22 +758,21 @@
     weights, grads = refs[:3], (refs[3], refs[4], refs[3])
     scatter_buffers, scatter_sems = refs[5:17], refs[17:25]
     (
-        own_sems, send_sems, recv_sems, bias_in, part_out, part_in,
-        cond_send, cond_recv, part_send, part_recv, bias_send, bias_recv,
-        leaving, cond_in, all_rows, back_out, back_in, row_send, row_recv, back_send, back_recv,
+        own_sems, send_sems, recv_sems, swap_send, swap_recv,
+        cond_across, cond_own, cond_along, cond_in, part_out, part_across, part_row, part_along,
+        leaving, rows_along, rows_across, back_out, back_across, back_row, back_along,
         mod, qkv_bias, proj_bias, fc1_bias, fc2_bias, mod_grad, qkv_sums, proj_sums, fc1_sums,
         fc2_sums, inverse_one, inverse_two, normed_one, normed_two, middle, branch, wide,
         hidden_one, hidden_one_t, hidden_two, hidden_two_t, attended, attended_t,
         grad_mlp, grad_mlp_t, grad_attended, projected,
-        grad_proj_mixed, activated, grad_pre, probability,
+        grad_proj_mixed, activated, grad_pre, grad_natural, grad_state, probability,
     ) = refs[25:]
-    grad_natural, grad_mixed = activated, grad_pre
+    grad_mixed = grad_pre
     mixed, fc1, fc2_turned = weights
     where = positions(rows, depth)
     dp = where[0]
     columns = 2 * depth
     column = lax.axis_index("fsdp")
-    me = dp * columns + column
     length = latents.shape[0]
     qkv_part, proj_part = 3 * D // columns, D // columns
     block = qkv_part + proj_part
@@ -744,46 +782,71 @@
     scale_factor = HEAD ** (-0.5)
     ada_rows, mod_width = ada_ref.shape
     mod_pad = round_up(mod_width)
-    enter_barrier(me, rows, columns)
+    barrier = pltpu.get_barrier_semaphore()
+    partners = [(lax.rem(dp + step, rows), column) for step in range(1, rows)]
+    partners += [(dp, lax.rem(column + step, columns)) for step in range(1, columns)]
+    for partner in partners:
+        pl.semaphore_signal(barrier, inc=1, device_id=partner, device_id_type=MESH_IDS)
+    pl.semaphore_wait(barrier, len(partners))
     gather = Gather(rows, depth, where, shards, weights, own_sems, send_sems, recv_sems)
     scatter = Scatter(
         rows, depth, where, [shard.shape for shard in shards], grads, scatter_buffers, scatter_sems)
-    row_swap = Exchange(
-        me, rows, columns, lambda target: leaving.at[lax.rem(target, columns)], all_rows,
-        row_send, row_recv)
-    back_swap = Exchange(
-        me, rows, columns, lambda target: back_out.at[target], back_in, back_send, back_recv)
-
-    cond_swap = Exchange(
-        me, rows, columns, lambda target: cond_rows.at[target // columns], cond_in,
-        cond_send, cond_recv)
-    part_swap = Exchange(
-        me, rows, columns, lambda target: part_out.at[target], part_in, part_send, part_recv)
-    cond_swap.start()
+    swaps = []
+
+    def swap_across(row_for, landing):
+        at = len(swaps)
+        swaps.append(Swap(
+            dp, rows, lambda other: (other, column), row_for, landing,
+            swap_send.at[at], swap_recv.at[at]))
+        return swaps[-1]
+
+    def swap_along(row_for, landing):
+        at = len(swaps)
+        swaps.append(Swap(
+            column, columns, lambda other: (dp, other), row_for, landing,
+            swap_send.at[at], swap_recv.at[at]))
+        return swaps[-1]
+
+    cond_first = swap_across(
+        lambda other: cond_rows.at[other], cond_across)
+    cond_second = swap_along(lambda other: cond_own, cond_along)
+    part_first = swap_across(lambda other: part_out.at[other], part_across)
+    part_second = swap_along(lambda other: part_row.at[other], part_along)
+    rows_first = swap_along(lambda other: leaving.at[other], rows_along)
+    rows_second = swap_across(lambda other: rows_along, rows_across)
+    back_first = swap_across(lambda other: back_out.at[other], back_across)
+    back_second = swap_along(lambda other: back_row.at[other], back_along)
+    cond_first.start()
+    for index in range(AHEAD):
+        gather.send_deep(index)
     gather.send_own(0)
-
-    def bias_copy(target, slot):
-        return pltpu.make_async_remote_copy(
-            src_ref=bias_row, dst_ref=bias_in.at[slot], send_sem=bias_send.at[target],
-            recv_sem=bias_recv.at[slot], device_id=(dp, target), device_id_type=MESH_IDS)
-
-    @pl.loop(1, columns)
-    def _(step):
-        bias_copy(lax.rem(column + step, columns), column).start()
-
-    bias_in[column] = bias_row[...]
-    gather.send_own(1)
-    gather.send_own(2)
 
     def piece(kind):
         return mod[:, kind * D : (kind + 1) * D]
 
+    def share_condition():
+        cond_first.wait_arrivals()
+        cond_own[:rows] = cond_across[...]
+        cond_own[rows:] = bias_rows[...]
+        cond_second.start()
+
     def start_modulation():
-        cond_swap.wait_arrivals()
-        high, width = ada_ref.shape
-        part = dot_plain(cond_in[:, 0, :high].astype(bfloat), ada_ref[...])
-        part_out[:, 0, :width] = part + jnp.where(dp == 0, ada_bias[...], 0.0)
-        part_swap.start()
+        cond_second.wait_arrivals()
+        cond_in[...] = jnp.concatenate(
+            [cond_along[source, row] for row in range(rows) for source in range(columns)], axis=0)
+        part = dot_plain(cond_in[:, :ada_rows].astype(bfloat), ada_ref[...])
+        part = part + jnp.where(dp == 0, ada_bias[...], 0.0)
+        for row in range(rows):
+            part_out[row, :, :mod_width] = part[row * columns : (row + 1) * columns]
+        part_first.start()
+
+    def sum_modulation():
+        part_first.wait_arrivals()
+        total = part_across[0]
+        for row in range(1, rows):
+            total = total + part_across[row]
+        part_row[:, 0, :] = total
+        part_second.start()
 
     def normalize_first():
         normed, inverse = normalize_rows(latents[...].astype(jnp.float32))
@@ -791,27 +854,18 @@
         inverse_one[...] = inverse
 
     def finish_modulation():
-        part_swap.wait_arrivals()
-        width = ada_ref.shape[1]
-        pieces = []
-        for source in range(columns):
-            total = part_in[source]
-            for row in range(1, rows):
-                total = total + part_in[row * columns + source]
-            pieces.append(total[:, :width])
-        mod[...] = jnp.concatenate(pieces, axis=1)
-
-        @pl.loop(1, columns)
-        def _(step):
-            other = lax.rem(column + step, columns)
-            bias_copy(other, other).wait_recv()
-            bias_copy(other, other).wait_send()
-
+        part_second.wait_arrivals()
+        mod[...] = jnp.concatenate(
+            [part_along[source][:, :mod_width] for source in range(columns)], axis=1)
+        bias_parts = [
+            jnp.concatenate(
+                [cond_along[source, row] for row in range(rows, cond_along.shape[1])], axis=1)
+            for source in range(columns)]
         low = 0
         naturals = []
         for width in (2 * D // columns, D // columns, FF // columns, D // columns):
             naturals.append(jnp.concatenate(
-                [bias_in[source][:, low : low + width] for source in range(columns)], axis=1))
+                [part[:, low : low + width] for part in bias_parts], axis=1))
             low += width
         qkv_bias[:, :D] = naturals[0][:, :D]
         qkv_bias[:, D : 2 * D] = jnp.zeros((1, D), jnp.float32)
@@ -822,6 +876,8 @@
         hidden = (normed_one[...] * (1.0 + piece(1)) + piece(0)).astype(bfloat)
         hidden_one[...] = hidden
         hidden_one_t[...] = hidden.T
+
+    def start_gradient():
         grad = (piece(5) * (live_ref[...] * cotangent[...].astype(jnp.float32))).astype(bfloat)
         grad_mlp[...] = grad
         grad_mlp_t[...] = grad.T
@@ -907,12 +963,6 @@
             part = span(index, chunk)
             grads[2][:, part] = dot_plain(grad_mlp_t[...], activated[:, part]).astype(bfloat)
 
-    hooks = {
-        0: start_modulation,
-        1: normalize_first,
-        2: finish_modulation,
-    }
-
     def after_part_zero():
         gather.finish_part(0)
         project()
@@ -921,19 +971,21 @@
         gather.finish_part(1)
         expand(0, 4)
 
-    hooks[depth + 2] = after_part_zero
-    hooks[depth + 3] = lambda: attend(0, 3)
-    hooks[depth + 4] = lambda: attend(3, 6)
-    hooks[depth + 5] = finish_attention
-    hooks[2 * depth + 2] = after_part_one
-    hooks[2 * depth + 3] = lambda: expand(4, 8)
-    hooks[2 * depth + 4] = lambda: fc2_weight_grad(0, 4)
-    hooks[2 * depth + 5] = lambda: fc2_weight_grad(4, 8)
-    for index in range(3 * depth + 2):
+    def send_fc2_grad():
+        fc2_weight_grad(4, 8)
+        scatter.start_pairs(2)
+
+    hooks = [
+        share_condition, normalize_first, start_modulation, None, sum_modulation, None,
+        finish_modulation, start_gradient, after_part_zero, lambda: attend(0, 3),
+        lambda: attend(3, 6), finish_attention, after_part_one, lambda: expand(4, 8),
+        lambda: fc2_weight_grad(0, 4), send_fc2_grad,
+    ]
+    for index, hook in enumerate(hooks):
         gather.turn(index)
-        if index in hooks:
-            hooks[index]()
-    scatter.start_pairs(2)
+        if hook is not None:
+            hook()
+    scatter.turn(0)
     gather.finish_part(2)
     third = 256
 
@@ -961,16 +1013,16 @@
         @pl.loop(0, D // third)
         def _(index):
             part = span(index, third)
-            middle[:, part] = against_weight(grad_pre[...], fc1[part, :])
+            grad_state[:, part] = against_weight(grad_pre[...], fc1[part, :])
 
     def middle_back():
-        grad_hidden = middle[...]
+        grad_hidden = grad_state[...]
         mod_grad[:, 3 * D : 4 * D] = columns_sum(grad_hidden)
         mod_grad[:, 4 * D : 5 * D] = columns_sum(grad_hidden * normed_two[...])
         grad_middle = live_ref[...] * cotangent[...].astype(jnp.float32) + norm_backward(
             grad_hidden * (1.0 + piece(4)), normed_two[...], inverse_two[...])
         mod_grad[:, 2 * D : 3 * D] = columns_sum(grad_middle * branch[...])
-        middle[...] = grad_middle
+        grad_state[...] = grad_middle
         grad_branch = (piece(2) * grad_middle).astype(bfloat)
         proj_sums[...] = columns_sum(grad_branch.astype(jnp.float32))
         for index in range(columns):
@@ -1007,7 +1059,7 @@
                     own_lanes(0), results[0][kind], results[1][kind]).astype(bfloat)
 
     def mixed_weight_grad():
-        qkv_sums[...] = columns_sum(grad_natural[:, : 3 * D].astype(jnp.float32))
+        qkv_sums[...] = columns_sum(grad_natural[...].astype(jnp.float32))
         for index in range(columns):
             grad_mixed[:, index * block : index * block + qkv_part] = (
                 grad_natural[:, index * qkv_part : (index + 1) * qkv_part])
@@ -1034,7 +1086,7 @@
         grad_hidden = branch[...]
         mod_grad[:, :D] = columns_sum(grad_hidden)
         mod_grad[:, D : 2 * D] = columns_sum(grad_hidden * normed_one[...])
-        latent_grad[...] = (middle[...] + norm_backward(
+        latent_grad[...] = (grad_state[...] + norm_backward(
             grad_hidden * (1.0 + piece(1)), normed_one[...], inverse_one[...])).astype(bfloat)
         pad = jnp.zeros((1, mod_pad - mod_width), jnp.float32)
         qv_sums = jnp.concatenate([qkv_sums[:, :D], qkv_sums[:, 2 * D :]], axis=1)
@@ -1046,60 +1098,66 @@
                 share = row.shape[1] // columns
                 pieces.append(row[:, index * share : (index + 1) * share])
             leaving[index] = jnp.concatenate(pieces, axis=1)
-        row_swap.start()
+        rows_first.start()
+
+    def share_rows():
+        rows_first.wait_arrivals()
+        rows_second.start()
 
     def own_sums():
-        row_swap.wait_arrivals()
-        arrived = all_rows[:, 0, :]
+        rows_second.wait_arrivals()
+        arrived = jnp.concatenate([rows_across[row, :, 0, :] for row in range(rows)], axis=0)
         sums = columns_sum(arrived)
         ada_bias_grad[...] = sums[:, :mod_width]
         low = mod_pad
         for out in (qv_bias_grad, proj_bias_grad, fc1_bias_grad, fc2_bias_grad):
             out[...] = sums[:, low : low + out.shape[1]]
             low += out.shape[1]
-        ada_grad[...] = contract_exact(cond_in[:, 0, :ada_rows], arrived[:, :mod_width])
-        back_out[:, 0, :ada_rows] = lax.dot_general(
+        ada_grad[...] = contract_exact(cond_in[:, :ada_rows], arrived[:, :mod_width])
+        back = lax.dot_general(
             arrived[:, :mod_width], ada_ref[...].astype(jnp.float32), (((1,), (1,)), ((), ())),
             precision=highest)
-        back_swap.start()
-
-    fc1_weight_grad(0, 4)
-    scatter.turn(0)
-    fc1_weight_grad(4, 8)
-    scatter.start_pairs(1)
-    scatter.turn(1)
-    finish_forward()
-    hidden_two_back()
-    scatter.turn(2)
-    middle_back()
-    scatter.turn(3)
-    attend_back(0, 2)
-    scatter.turn(4)
-    attend_back(2, 4)
-    scatter.turn(5)
-    attend_back(4, 6)
-    scatter.turn(6)
-    mixed_weight_grad()
-    scatter.start_pairs(0)
-    scatter.turn(7)
-    finish_backward()
-    fc2_grad[...] = scatter.finish_part(2).T
-    scatter.turn(8)
-    scatter.turn(9)
-    own_sums()
-    scatter.turn(10)
-    fc1_grad[...] = scatter.finish_part(1)
-    scatter.turn(11)
-    scatter.turn(12)
-    back_swap.wait_arrivals()
-    terms = []
-    for row in range(rows):
-        total = back_in[row * columns]
+        for row in range(rows):
+            back_out[row, :, :ada_rows] = back[row * columns : (row + 1) * columns]
+        back_first.start()
+
+    def share_back():
+        back_first.wait_arrivals()
+        for row in range(rows):
+            back_row[:, row, 0, :] = back_across[row]
+        back_second.start()
+
+    def finish_condition():
+        back_second.wait_arrivals()
+        total = back_along[0]
         for source in range(1, columns):
-            total = total + back_in[row * columns + source]
-        terms.append(total[:, :ada_rows])
-    cond_grad[...] = jnp.concatenate(terms, axis=1) * slope[...]
-    scatter.turn(13)
+            total = total + back_along[source]
+        cond_grad[...] = jnp.concatenate(
+            [total[row][:, :ada_rows] for row in range(rows)], axis=1) * slope[...]
+
+    def finish_fc2():
+        fc2_grad[...] = scatter.finish_part(2).T
+
+    def finish_fc1():
+        fc1_grad[...] = scatter.finish_part(1)
+
+    def send_fc1_grad():
+        fc1_weight_grad(4, 8)
+        scatter.start_pairs(1)
+
+    def send_mixed_grad():
+        mixed_weight_grad()
+        scatter.start_pairs(0)
+
+    hooks = [
+        lambda: fc1_weight_grad(0, 4), send_fc1_grad, hidden_two_back, middle_back,
+        lambda: attend_back(0, 3), lambda: attend_back(3, 6), send_mixed_grad,
+        finish_forward, finish_backward, finish_fc2, share_rows, own_sums, finish_fc1,
+        share_back, finish_condition,
+    ]
+    for index, hook in enumerate(hooks):
+        hook()
+        scatter.turn(index + 1)
     total = scatter.finish_part(0)
     qkv_grad[...] = total[:, :qkv_part]
     proj_grad[...] = total[:, qkv_part:]
@@ -1107,17 +1165,20 @@
     scatter.wait_pairs_sent(0)
     scatter.wait_sends()
     gather.wait_sends()
-    for swap in (cond_swap, part_swap, row_swap, back_swap):
+    for swap in swaps:
         swap.wait_sends()
 
 
 def run_layer(shards, cond_rows, slope, ada_weight, ada_bias, bias_row, latents, cotangent, live,
               widths, rows, columns):
     depth = columns // 2
+    cond_pad = cond_rows.shape[-1]
+    group = rows + bias_row.shape[-1] // cond_pad
     count = (depth - 1) + depth * rows + depth * (rows - 1) + 2 * depth
     total = rows * columns
     ada_rows, mod_width = ada_weight.shape
     mod_pad = round_up(mod_width)
+    bias_rows = bias_row.reshape(-1, 1, cond_rows.shape[-1])
     bias_width = bias_row.shape[-1]
     length = latents.shape[0]
     vmem = pl.BlockSpec(memory_space=pltpu.VMEM)
@@ -1160,24 +1221,30 @@
             dma((3, depth, 2)), dma((3, depth, 2)), dma((3, depth, 2)), dma((3, depth, 2)),
             dma((3, depth - 1)), dma((3, depth - 1)),
             dma((3,)), dma((3 * count,)), dma((2, 3, columns, rows)),
-            row_buffer(columns, bias_width), row_buffer(total, mod_pad), row_buffer(total, mod_pad),
-            dma((total,)), dma((total,)), dma((total,)), dma((total,)),
-            dma((columns,)), dma((columns,)),
-            row_buffer(columns, mod_pad + bias_width), row_buffer(total, cond_rows.shape[-1]),
-            row_buffer(total, mod_pad + bias_width),
-            row_buffer(total, round_up(ada_rows)), row_buffer(total, round_up(ada_rows)),
-            dma((total,)), dma((total,)), dma((total,)), dma((total,)),
+            dma((8, columns)), dma((8, columns)),
+            row_buffer(rows, cond_pad), row_buffer(group, cond_pad),
+            pltpu.VMEM((columns, group, 1, cond_pad), jnp.float32),
+            pltpu.VMEM((total, cond_pad), jnp.float32),
+            pltpu.VMEM((rows, columns, mod_pad), jnp.float32),
+            pltpu.VMEM((rows, columns, mod_pad), jnp.float32),
+            row_buffer(columns, mod_pad), row_buffer(columns, mod_pad),
+            row_buffer(columns, mod_pad + bias_width), row_buffer(columns, mod_pad + bias_width),
+            pltpu.VMEM((rows, columns, 1, mod_pad + bias_width), jnp.float32),
+            pltpu.VMEM((rows, columns, cond_pad), jnp.float32),
+            pltpu.VMEM((rows, columns, cond_pad), jnp.float32),
+            pltpu.VMEM((columns, rows, 1, cond_pad), jnp.float32),
+            pltpu.VMEM((columns, rows, 1, cond_pad), jnp.float32),
             wide_row(6 * D), wide_row(3 * D), wide_row(D), wide_row(FF), wide_row(D),
             wide_row(6 * D), wide_row(3 * D), wide_row(D), wide_row(FF), wide_row(D),
             single(1), single(1), single(D), single(D), single(D), single(D), single(FF),
             half(D), turned, half(D), turned, half(D), turned,
             half(D), turned, half(D), half(3 * D),
-            half(rest), half(FF), half(FF), pltpu.VMEM((HEADS, length, length), jnp.float32),
+            half(rest), half(FF), half(FF), half(3 * D), single(D), pltpu.VMEM((HEADS, length, length), jnp.float32),
         ],
         compiler_params=pltpu.CompilerParams(
             collective_id=2, has_side_effects=True, vmem_limit_bytes=62 * 2**20),
         name="run_layer",
-    )(*shards, cond_rows, slope, ada_weight, ada_bias, bias_row, latents, cotangent, live)
+    )(*shards, cond_rows, slope, ada_weight, ada_bias, bias_rows, latents, cotangent, live)
 
 
 def pick(mixed, columns, kind):

time: 203 us -> 169 us (0.83)
  Pallas kernels: 180 us -> 148 us
    pallas_call x1, Pallas kernels: 180 us -> 148 us  [run_layer(): pl.pallas_call(functools.partial(layer_kernel, rows, depth), out_shape=[j...]
where the time goes in v4:
time: 169 us; the launch traced here: 168 us
  Pallas kernels  148 us (88%)
  local copies, waits for them, and re-layouts  11.7 us (7%)
  other arithmetic  7.6 us (4%)
    pallas_call x1, Pallas kernels, run_layer(): pl.pallas_call(functools.partial(layer_kernel, rows, depth), out_shape=[j...  148 us
    unnamed x33, local copies, waits for them, and re-layouts  9.18 us

profile of v4, /device:TPU:0, one launch (start us, length us, event | category | flops | bytes accessed | tf_op | source)
XLA Modules:
  0.0 168.5 jit_solution(11492467751532360082)
XLA Ops:
  0.6 0.0 copy-start.6
  1.3 1.3 reshape.72.refs_6_
  2.6 0.6 broadcast_in_dim.10.refs_10_
  3.1 0.8 maximum_convert_fusion
  3.9 0.6 reshape.73.refs_7_
  4.5 1.3 fusion.1
  5.8 0.7 convert_reduce_fusion
  6.5 0.1 reshape.74
  6.6 0.6 pad_convert_fusion.refs_3_
  7.2 0.0 copy-done.6
  7.2 1.7 pad_maximum_fusion.refs_0_
  8.9 147.8 %run_layer.1 = (bf16[256,768]{1,0:T(8,128)(2,1)}, bf16[256,768]{1,0:T(8,128)(2,1)}, f32[1,768]{1,0:T(1,128)}, f32[192,576]{1,0:T(8,128)}, f32[1,576]{1,0:T(1,128...) custom-call(bf16[192,384]{1,0:T(8,128)(2,1)} %pad_maximum_fusion.ref, ...), custom_call_target="tpu_custom_call" | custom-call | tf_op jit(solution)/shard_map/run_layer/pallas_call | solution.py:1204
  156.7 0.0 copy-start.2
  156.7 1.3 reduce.2
  158.0 1.3 reduce.1
  159.3 1.9 %copy.28 = f32[768,96]{0,1:T(8,128)} copy(f32[768,96]{1,0:T(8,128)} %get-tuple-element.50) | data formatting | bytes 589824
  161.2 0.0 copy-done.2
  161.2 0.0 copy-start.1
  161.2 0.7 copy.40
  161.9 0.4 copy-done.1
  162.3 0.0 copy-start.7
  162.3 0.0 copy-start
  162.3 0.7 copy.41
  163.1 0.0 copy-done.7
  163.1 0.6 copy.42
  163.6 0.0 copy-done
  163.6 0.0 copy-start.4
  163.6 0.8 copy.43
  164.4 0.3 copy-done.4
  164.8 0.0 copy-start.8
  164.8 0.0 copy-start.5
  164.8 0.0 copy-start.3
  164.8 0.7 copy.44
  165.5 0.0 copy-done.8
  165.5 0.6 copy.45
  166.0 0.0 copy-done.5
  166.1 0.0 copy-start.10
  166.1 0.6 copy.46
  166.7 0.0 copy-done.10
  166.7 0.5 copy.47
  167.2 0.0 copy-done.3
  167.2 0.0 copy-start.9
  167.2 0.7 copy.48
  168.0 0.0 copy-done.9
  168.0 0.5 copy.49
Async XLA Ops:
  0.6 6.6 %copy-start.6 = (bf16[192,96]{1,0:T(8,128)(2,1)S(1)}, bf16[192,96]{1,0:T(8,128)(2,1)}, u32[]{:S(2)}) copy-start(bf16[192,96]{1,0:T(8,128)(2,1)} %param.22) | copy-start | bytes 110596
  156.7 4.5 %copy-start.2 = (bf16[256,768]{1,0:T(8,128)(2,1)S(1)}, bf16[256,768]{1,0:T(8,128)(2,1)}, u32[]{:S(2)}) copy-start(bf16[256,768]{1,0:T(8,128)(2,1)} %get-tuple-element.26) | copy-start | bytes 1179652
  161.2 1.1 copy-start.1
  162.3 0.8 copy-start.7
  162.3 1.3 copy-start
  163.6 1.1 copy-start.4
  164.8 0.7 copy-start.8
  164.8 1.3 copy-start.5
  164.8 2.5 %copy-start.3 = (f32[192,384]{1,0:T(8,128)S(1)}, f32[192,384]{1,0:T(8,128)}, u32[]{:S(2)}) copy-start(f32[192,384]{1,0:T(8,128)} %get-tuple-element.76) | copy-start | bytes 884740
  166.1 0.7 copy-start.10
  167.2 0.7 copy-start.9

commit v5 on v4

--- a/solution.py
+++ b/solution.py
@@ -748,13 +748,16 @@
 
 
 def layer_kernel(rows, depth, *refs):
-    shards = refs[:3]
-    cond_rows, slope, ada_ref, ada_bias, bias_rows, latents, cotangent, live_ref = refs[3:11]
+    sources, live_ref, outs = refs[2:13], refs[13], refs[14:22]
+    landed, results = refs[22:33], refs[33:41]
     (
-        block_out, latent_grad, cond_grad, ada_grad, ada_bias_grad, qkv_grad, qv_bias_grad,
-        proj_grad, proj_bias_grad, fc1_grad, fc1_bias_grad, fc2_grad, fc2_bias_grad,
-    ) = refs[11:24]
-    refs = refs[24:]
+        latents, cotangent, conditioning, ada_ref, ada_bias, qkv_shard, qv_shard, proj_shard,
+        proj_bias_shard, fc1_bias_shard, fc2_bias_shard,
+    ) = landed
+    block_out, latent_grad, ada_grad, qkv_grad, proj_grad, fc1_grad, fc2_grad, small = results
+    mixed_shard, cond_rows, slope, load_sems, store_sems = refs[41:46]
+    shards = (mixed_shard, refs[0], refs[1])
+    refs = refs[46:]
     weights, grads = refs[:3], (refs[3], refs[4], refs[3])
     scatter_buffers, scatter_sems = refs[5:17], refs[17:25]
     (
@@ -782,11 +785,31 @@
     scale_factor = HEAD ** (-0.5)
     ada_rows, mod_width = ada_ref.shape
     mod_pad = round_up(mod_width)
+    loads = [
+        pltpu.make_async_copy(source, target, load_sems.at[at])
+        for at, (source, target) in enumerate(zip(sources, landed))]
+    for at in (2, 5, 7, 6, 8, 9, 10, 0, 3, 4, 1):
+        loads[at].start()
+    stores = []
+
+    def store(at):
+        copy = pltpu.make_async_copy(results[at], outs[at], store_sems.at[at])
+        copy.start()
+        stores.append(copy)
+
     barrier = pltpu.get_barrier_semaphore()
     partners = [(lax.rem(dp + step, rows), column) for step in range(1, rows)]
     partners += [(dp, lax.rem(column + step, columns)) for step in range(1, columns)]
     for partner in partners:
         pl.semaphore_signal(barrier, inc=1, device_id=partner, device_id_type=MESH_IDS)
+    live = live_ref[0].astype(jnp.float32)
+    loads[2].wait()
+    cond_value = conditioning[...].astype(jnp.float32)
+    logistic = 1.0 / (1.0 + jnp.exp(-cond_value))
+    slope[...] = logistic * (1.0 + cond_value * (1.0 - logistic))
+    cond_act = (cond_value * logistic).astype(bfloat).astype(jnp.float32)
+    for row in range(rows):
+        cond_rows[row, :, :ada_rows] = cond_act[:, row * ada_rows : (row + 1) * ada_rows]
     pl.semaphore_wait(barrier, len(partners))
     gather = Gather(rows, depth, where, shards, weights, own_sems, send_sems, recv_sems)
     scatter = Scatter(
@@ -817,6 +840,10 @@
     back_first = swap_across(lambda other: back_out.at[other], back_across)
     back_second = swap_along(lambda other: back_row.at[other], back_along)
     cond_first.start()
+    loads[5].wait()
+    loads[7].wait()
+    mixed_shard[:, :qkv_part] = qkv_shard[...]
+    mixed_shard[:, qkv_part:] = proj_shard[...]
     for index in range(AHEAD):
         gather.send_deep(index)
     gather.send_own(0)
@@ -827,15 +854,25 @@
     def share_condition():
         cond_first.wait_arrivals()
         cond_own[:rows] = cond_across[...]
-        cond_own[rows:] = bias_rows[...]
+        bias_row = []
+        for at in (6, 8, 9, 10):
+            loads[at].wait()
+            bias_row.append(landed[at][...].astype(jnp.float32).reshape(1, -1))
+        bias_row = jnp.concatenate(bias_row, axis=1)
+        pad = cond_own.shape[-1]
+        for at in range(bias_row.shape[1] // pad):
+            cond_own[rows + at] = bias_row[:, at * pad : (at + 1) * pad]
         cond_second.start()
 
     def start_modulation():
         cond_second.wait_arrivals()
         cond_in[...] = jnp.concatenate(
             [cond_along[source, row] for row in range(rows) for source in range(columns)], axis=0)
+        loads[3].wait()
+        loads[4].wait()
         part = dot_plain(cond_in[:, :ada_rows].astype(bfloat), ada_ref[...])
-        part = part + jnp.where(dp == 0, ada_bias[...], 0.0)
+        own_bias = ada_bias[...].astype(jnp.float32).reshape(1, -1)
+        part = part + jnp.where(dp == 0, own_bias, 0.0)
         for row in range(rows):
             part_out[row, :, :mod_width] = part[row * columns : (row + 1) * columns]
         part_first.start()
@@ -849,6 +886,7 @@
         part_second.start()
 
     def normalize_first():
+        loads[0].wait()
         normed, inverse = normalize_rows(latents[...].astype(jnp.float32))
         normed_one[...] = normed
         inverse_one[...] = inverse
@@ -878,7 +916,8 @@
         hidden_one_t[...] = hidden.T
 
     def start_gradient():
-        grad = (piece(5) * (live_ref[...] * cotangent[...].astype(jnp.float32))).astype(bfloat)
+        loads[1].wait()
+        grad = (piece(5) * (live * cotangent[...].astype(jnp.float32))).astype(bfloat)
         grad_mlp[...] = grad
         grad_mlp_t[...] = grad.T
         fc2_sums[...] = columns_sum(grad.astype(jnp.float32))
@@ -994,11 +1033,13 @@
         def _(index):
             part = span(index, third)
             branch_part = against_weight(activated[...], fc2_turned[part, :]) + fc2_bias[:, part]
-            live_grad = live_ref[:, part] * cotangent[:, part].astype(jnp.float32)
+            live_grad = live * cotangent[:, part].astype(jnp.float32)
             last = pl.ds(pl.multiple_of(5 * D + index * third, third), third)
             block_out[:, part] = (
-                live_ref[:, part] * (middle[:, part] + mod[:, last] * branch_part)).astype(bfloat)
+                live * (middle[:, part] + mod[:, last] * branch_part)).astype(bfloat)
             mod_grad[:, last] = columns_sum(live_grad * branch_part)
+
+        store(0)
 
     def fc1_weight_grad(low, high):
         @pl.loop(low, high)
@@ -1019,7 +1060,7 @@
         grad_hidden = grad_state[...]
         mod_grad[:, 3 * D : 4 * D] = columns_sum(grad_hidden)
         mod_grad[:, 4 * D : 5 * D] = columns_sum(grad_hidden * normed_two[...])
-        grad_middle = live_ref[...] * cotangent[...].astype(jnp.float32) + norm_backward(
+        grad_middle = live * cotangent[...].astype(jnp.float32) + norm_backward(
             grad_hidden * (1.0 + piece(4)), normed_two[...], inverse_two[...])
         mod_grad[:, 2 * D : 3 * D] = columns_sum(grad_middle * branch[...])
         grad_state[...] = grad_middle
@@ -1088,6 +1129,7 @@
         mod_grad[:, D : 2 * D] = columns_sum(grad_hidden * normed_one[...])
         latent_grad[...] = (grad_state[...] + norm_backward(
             grad_hidden * (1.0 + piece(1)), normed_one[...], inverse_one[...])).astype(bfloat)
+        store(1)
         pad = jnp.zeros((1, mod_pad - mod_width), jnp.float32)
         qv_sums = jnp.concatenate([qkv_sums[:, :D], qkv_sums[:, 2 * D :]], axis=1)
         rows_of = (qv_sums, proj_sums[...], fc1_sums[...], fc2_sums[...])
@@ -1107,13 +1149,9 @@
     def own_sums():
         rows_second.wait_arrivals()
         arrived = jnp.concatenate([rows_across[row, :, 0, :] for row in range(rows)], axis=0)
-        sums = columns_sum(arrived)
-        ada_bias_grad[...] = sums[:, :mod_width]
-        low = mod_pad
-        for out in (qv_bias_grad, proj_bias_grad, fc1_bias_grad, fc2_bias_grad):
-            out[...] = sums[:, low : low + out.shape[1]]
-            low += out.shape[1]
+        small[:, D:] = columns_sum(arrived)
         ada_grad[...] = contract_exact(cond_in[:, :ada_rows], arrived[:, :mod_width])
+        store(2)
         back = lax.dot_general(
             arrived[:, :mod_width], ada_ref[...].astype(jnp.float32), (((1,), (1,)), ((), ())),
             precision=highest)
@@ -1132,14 +1170,17 @@
         total = back_along[0]
         for source in range(1, columns):
             total = total + back_along[source]
-        cond_grad[...] = jnp.concatenate(
+        small[:, :D] = jnp.concatenate(
             [total[row][:, :ada_rows] for row in range(rows)], axis=1) * slope[...]
+        store(7)
 
     def finish_fc2():
-        fc2_grad[...] = scatter.finish_part(2).T
+        fc2_grad[...] = scatter.finish_part(2)
+        store(6)
 
     def finish_fc1():
         fc1_grad[...] = scatter.finish_part(1)
+        store(5)
 
     def send_fc1_grad():
         fc1_weight_grad(4, 8)
@@ -1161,27 +1202,74 @@
     total = scatter.finish_part(0)
     qkv_grad[...] = total[:, :qkv_part]
     proj_grad[...] = total[:, qkv_part:]
+    store(3)
+    store(4)
     scatter.wait_pairs_sent(1)
     scatter.wait_pairs_sent(0)
     scatter.wait_sends()
     gather.wait_sends()
     for swap in swaps:
         swap.wait_sends()
-
-
-def run_layer(shards, cond_rows, slope, ada_weight, ada_bias, bias_row, latents, cotangent, live,
-              widths, rows, columns):
+    for copy in stores:
+        copy.wait()
+
+
+def emit_kernel(*refs):
+    small, wholes = refs[0], refs[1:8]
+    cond_grad, rows_out, outs, held, sems = refs[8], refs[9:14], refs[14:21], refs[21:28], refs[28]
+    loads = [
+        pltpu.make_async_copy(whole, hold, sems.at[0, at])
+        for at, (whole, hold) in enumerate(zip(wholes, held))]
+    stores = [
+        pltpu.make_async_copy(hold, out, sems.at[1, at])
+        for at, (hold, out) in enumerate(zip(held, outs))]
+    for load in loads:
+        load.start()
+    cond_grad[...] = small[:, :D]
+    low = D
+    for out in rows_out:
+        width = out.shape[0]
+        out[...] = small[0, low : low + width]
+        low += round_up(width) if low == D else width
+    for load, store in zip(loads, stores):
+        load.wait()
+        store.start()
+    for store in stores:
+        store.wait()
+
+
+def emit(small, wholes, widths):
+    vmem = pl.BlockSpec(memory_space=pltpu.VMEM)
+    anywhere = pl.BlockSpec(memory_space=pl.ANY)
+    count = len(wholes)
+    return pl.pallas_call(
+        emit_kernel,
+        out_shape=[jax.ShapeDtypeStruct((1, D), jnp.float32)]
+        + [jax.ShapeDtypeStruct((width,), jnp.float32) for width in widths]
+        + [jax.ShapeDtypeStruct(whole.shape, whole.dtype) for whole in wholes],
+        in_specs=[vmem] + [anywhere] * count,
+        out_specs=[vmem] * (1 + len(widths)) + [anywhere] * count,
+        scratch_shapes=[pltpu.VMEM(whole.shape, whole.dtype) for whole in wholes]
+        + [pltpu.SemaphoreType.DMA((2, count))],
+        name="emit",
+    )(small, *wholes)
+
+
+def run_layer(fc1_shard, fc2_turned_shard, sources, latent_count, rows, columns):
+    latents, _, conditioning, ada_weight, _, qkv_shard, _, proj_shard = sources[:8]
     depth = columns // 2
-    cond_pad = cond_rows.shape[-1]
-    group = rows + bias_row.shape[-1] // cond_pad
+    qkv_part, proj_part = qkv_shard.shape[1], proj_shard.shape[1]
+    shards = (
+        jax.ShapeDtypeStruct((qkv_shard.shape[0], qkv_part + proj_part), bfloat),
+        fc1_shard, fc2_turned_shard)
+    ada_rows, mod_width = ada_weight.shape
+    cond_pad = round_up(ada_rows)
+    bias_width = sum(sources[at].shape[0] for at in (6, 8, 9, 10))
+    group = rows + bias_width // cond_pad
     count = (depth - 1) + depth * rows + depth * (rows - 1) + 2 * depth
     total = rows * columns
-    ada_rows, mod_width = ada_weight.shape
     mod_pad = round_up(mod_width)
-    bias_rows = bias_row.reshape(-1, 1, cond_rows.shape[-1])
-    bias_width = bias_row.shape[-1]
     length = latents.shape[0]
-    vmem = pl.BlockSpec(memory_space=pltpu.VMEM)
     anywhere = pl.BlockSpec(memory_space=pl.ANY)
     dma = pltpu.SemaphoreType.DMA
     shapes = [
@@ -1199,23 +1287,28 @@
             height = height // 2 if 6 <= len(buffers) < 9 else height
             buffers.append(pltpu.VMEM(lead + (height, width), bfloat))
     float_out = lambda *shape: jax.ShapeDtypeStruct(shape, jnp.float32)
-    qkv_part, proj_part = 3 * D // columns, D // columns
-    height = shards[0].shape[0]
+    outs = [
+        jax.ShapeDtypeStruct((length, D), bfloat),
+        jax.ShapeDtypeStruct((length, D), bfloat),
+        float_out(ada_rows, mod_width),
+        float_out(qkv_shard.shape[0], qkv_part),
+        float_out(qkv_shard.shape[0], proj_part),
+        float_out(*fc1_shard.shape),
+        float_out(*fc2_turned_shard.shape),
+        float_out(1, D + mod_pad + bias_width),
+    ]
     return pl.pallas_call(
         functools.partial(layer_kernel, rows, depth),
-        out_shape=[
-            jax.ShapeDtypeStruct((length, D), bfloat),
-            jax.ShapeDtypeStruct((length, D), bfloat),
-            float_out(1, D),
-            float_out(ada_rows, mod_width), float_out(1, mod_width),
-            float_out(height, qkv_part), float_out(1, widths[0]),
-            float_out(height, proj_part), float_out(1, widths[1]),
-            float_out(*shards[1].shape), float_out(1, widths[2]),
-            float_out(*shards[2].shape[::-1]), float_out(1, widths[3]),
-        ],
-        in_specs=[anywhere] * 3 + [vmem] * 8,
-        out_specs=[vmem] * 13,
-        scratch_shapes=[pltpu.VMEM(shape, bfloat) for shape in shapes + shapes[:2]]
+        out_shape=outs,
+        in_specs=[anywhere] * 13 + [pl.BlockSpec(memory_space=pltpu.SMEM)],
+        out_specs=[anywhere] * 8,
+        scratch_shapes=[pltpu.VMEM(source.shape, source.dtype) for source in sources]
+        + [pltpu.VMEM(out.shape, out.dtype) for out in outs]
+        + [
+            pltpu.VMEM(shards[0].shape, bfloat), row_buffer(rows, cond_pad), wide_row(D),
+            dma((len(sources),)), dma((len(outs),)),
+        ]
+        + [pltpu.VMEM(shape, bfloat) for shape in shapes + shapes[:2]]
         + buffers + [
             dma((3, depth, rows)), dma((3, depth, rows)),
             dma((3, depth, 2)), dma((3, depth, 2)), dma((3, depth, 2)), dma((3, depth, 2)),
@@ -1244,7 +1337,7 @@
         compiler_params=pltpu.CompilerParams(
             collective_id=2, has_side_effects=True, vmem_limit_bytes=62 * 2**20),
         name="run_layer",
-    )(*shards, cond_rows, slope, ada_weight, ada_bias, bias_rows, latents, cotangent, live)
+    )(fc1_shard, fc2_turned_shard, *sources, latent_count)
 
 
 def pick(mixed, columns, kind):
@@ -1421,6 +1514,22 @@
     fc2_bias,
 ):
     rows, columns = lax.axis_size("dp"), lax.axis_size("fsdp")
+    if rows == 4 and columns == 8:
+        sources = (
+            latents[0], cotangent[0], conditioning, ada_weight, ada_bias, qkv_weight, qv_bias,
+            proj_weight, proj_bias, fc1_bias, fc2_bias)
+        *wholes, small = run_layer(
+            fc1_weight, fc2_weight.T, sources, latent_count, rows, columns)
+        widths = [bias.shape[0] for bias in (ada_bias, qv_bias, proj_bias, fc1_bias, fc2_bias)]
+        (
+            cond_grad, ada_bias_grad, qv_bias_grad, proj_bias_grad, fc1_bias_grad, fc2_bias_grad,
+            block_out, latent_grad, ada_grad, qkv_grad, proj_grad, fc1_grad, fc2_turned_grad,
+        ) = emit(small, wholes, widths)
+        return (
+            block_out[None], latent_grad[None], cond_grad, ada_grad, ada_bias_grad, qkv_grad,
+            qv_bias_grad, proj_grad, proj_bias_grad, fc1_grad, fc1_bias_grad, fc2_turned_grad.T,
+            fc2_bias_grad,
+        )
     live = latent_count[0].astype(jnp.float32)
     depth = ada_weight.shape[0]
     mod_width = ada_weight.shape[1]
@@ -1447,15 +1556,6 @@
     )
     shapes = [shard.shape for shard in shards]
     ada_row = ada_bias.astype(jnp.float32).reshape(1, -1)
-    fused = rows == 4 and columns == 8
-    if fused:
-        block_out, latent_grad, *param_grads = run_layer(
-            shards, cond_rows, slope, ada_weight, ada_row, bias_row, latents[0], cotangent[0],
-            jnp.full((1, D), live), widths, rows, columns)
-        param_grads = [
-            grad.reshape(-1) if 0 < place < 11 and place % 2 == 0 else grad
-            for place, grad in enumerate(param_grads)]
-        return (block_out[None], latent_grad[None], *param_grads)
     *blocks, mod_blocks, bias_blocks, cond_in = gather_shards(
         shards, cond_rows, ada_weight, ada_row, bias_row,
         rows, columns)

time: 169 us -> 151 us (0.89)
  local copies, waits for them, and re-layouts: 11.7 us -> 0 us
  other arithmetic: 7.6 us -> 0 us
    unnamed x33 -> x0, local copies, waits for them, and re-layouts: 9.18 us -> none
    pallas_call x2 -> x0, other arithmetic: 2.57 us -> none  [run_layer(): pl.pallas_call(functools.partial(layer_kernel, rows, depth), out_shape=[j...]
    pallas_call x1 -> x2, Pallas kernels: 148 us -> 149 us  [the longest x1 145 us: run_layer(): pl.pallas_call(functools.partial(layer_kernel, rows, depth), out_shape=ou...]
where the time goes in v5:
time: 151 us
  Pallas kernels  149 us (99%)
    pallas_call x1, Pallas kernels, run_layer(): pl.pallas_call(functools.partial(layer_kernel, rows, depth), out_shape=ou...  145 us
    pallas_call x1, Pallas kernels, emit(): pl.pallas_call(emit_kernel, out_shape=[jax.ShapeDtypeStruct((1, D), jnp.f...  3.79 us

profile of v5, /device:TPU:0, one launch (start us, length us, event | category | flops | bytes accessed | tf_op | source)
XLA Modules:
  0.0 150.6 jit_solution(4073160001641880519)
XLA Ops:
  1.3 145.3 %run_layer.1 = (bf16[256,768]{1,0:T(8,128)(2,1)}, bf16[256,768]{1,0:T(8,128)(2,1)}, f32[192,576]{1,0:T(8,128)}, f32[192,288]{1,0:T(8,128)}, f32[192,96]{1,0:T(8,...) custom-call(bf16[192,384]{1,0:T(8,128)(2,1)} %refs_0_.1, bf16[96,768]{1,0:T(8,128)(2,1)} %bitcast.8, ...), custom_call_target="tpu_custom_call" | custom-call | tf_op jit(solution)/shard_map/run_layer/pallas_call | solution.py:1300
  146.6 3.8 %emit.1 = (f32[1,768]{1,0:T(1,128)}, f32[576]{0:T(1024)}, f32[192]{0:T(256)}, f32[96]{0:T(128)}, f32[384]{0:T(512)}, /*index=5*/f32[96]{0:T(128)}, bf16[256,768]...) custom-call(f32[1,2176]{1,0:T(1,128)} %get-tuple-element.34.refs_0_,, ...), custom_call_target="tpu_custom_call" | custom-call | tf_op jit(solution)/shard_map/emit/pallas_call | solution.py:1245

commit v6 on v5

--- a/solution.py
+++ b/solution.py
@@ -542,8 +542,10 @@
         self.sends = []
         self.keeps = []
         self.own = self.z * 2 + self.core
-        self.lines = [(self.z ^ step) * 2 + self.core for step in range(depth)]
+        self.steps = [0] + list(range(2, depth)) + [1]
+        self.lines = [(self.z ^ step) * 2 + self.core for step in self.steps]
         self.units = [(part, turn) for part in range(3) for turn in range(depth)]
+        self.helped = depth - 1
 
     def slot_of(self, part, line, row):
         return block_of(self.outs[part], line, row, self.shards[part].shape, part == 2)
@@ -593,9 +595,9 @@
 
     def send_deep(self, index):
         if index < len(self.units):
-            part, step = self.units[index]
-            if step:
-                target = place(self.dp, self.z ^ step, self.core)
+            part, turn = self.units[index]
+            if turn:
+                target = place(self.dp, self.z ^ self.steps[turn], self.core)
                 self.send(part, self.own, self.dp, target, own=True)
 
     def turn(self, index):
@@ -609,22 +611,35 @@
             line = self.lines[turn]
             if turn:
                 self.arrive(part, line, dp)
+                which = 0 if turn == self.helped else None
                 for other in self.others:
-                    self.send(part, line, dp, place(other, z, core))
+                    self.send(part, line, dp, place(other, z, core), which=which)
                 self.send(part, line, dp, self.sibling)
         if LAG <= index < count + LAG:
             part, turn = self.units[index - LAG]
             line = self.lines[turn]
             for position, other in enumerate(self.others):
-                self.arrive(part, line, other)
-                self.send(
-                    part, line, other, place(self.others[1 - position], z, core), which=position)
+                if turn == self.helped:
+                    self.arrive(part, line, other, 0)
+                    self.arrive(part, line, other, 1)
+                else:
+                    self.arrive(part, line, other)
+                    self.send(
+                        part, line, other, place(self.others[1 - position], z, core),
+                        which=position)
+                if turn == 0:
+                    self.send(part, line, other, place(dp, z ^ 1, core), which=1)
                 self.send(part, line, other, self.sibling)
         if 2 * LAG <= index:
             part, turn = self.units[index - 2 * LAG]
             line = self.lines[turn]
-            self.arrive(part, line, dp ^ 3, 0)
-            self.arrive(part, line, dp ^ 3, 1)
+            if turn == self.helped:
+                self.arrive(part, line, dp ^ 3)
+            else:
+                self.arrive(part, line, dp ^ 3, 0)
+                self.arrive(part, line, dp ^ 3, 1)
+            if turn == 0:
+                self.send(part, line, dp ^ 3, place(dp, z ^ 1, core))
             self.send(part, line, dp ^ 3, self.sibling)
 
     def finish_part(self, part):
@@ -642,17 +657,19 @@
     def __init__(self, rows, depth, where, shapes, grads, buffers, sems):
         self.rows, self.depth, self.shapes, self.grads = rows, depth, shapes, grads
         self.dp, self.z, self.core, self.others = where
-        self.held, self.planes_in, self.crosses_in, self.alongs_in = (
-            buffers[3 * kind : 3 * kind + 3] for kind in range(4))
+        (
+            self.held, self.planes_in, self.crosses_in, self.alongs_in, self.help_in, self.half_in,
+        ) = (buffers[3 * kind : 3 * kind + 3] for kind in range(6))
         (
             self.pair_send, self.pair_recv, self.plane_send, self.plane_recv,
             self.cross_send, self.cross_recv, self.along_send, self.along_recv,
+            self.help_send, self.help_recv,
         ) = sems
         self.sibling = place(self.dp, self.z, 1 - self.core)
         self.targets = [self.dp ^ 3, self.dp ^ 1, self.dp ^ 2, self.dp]
-        self.lines = [self.z ^ step for step in reversed(range(depth))]
+        self.lines = [self.z ^ step for step in [1] + list(range(2, depth))[::-1] + [0]]
         self.units = [(part, turn) for part in (2, 1, 0) for turn in range(depth)]
-        self.pairs, self.planes, self.crosses, self.alongs = {}, {}, {}, {}
+        self.pairs, self.planes, self.crosses, self.alongs, self.helps = {}, {}, {}, {}, {}
 
     def remote(self, source, destination, send_sem, recv_sem, target):
         copy = pltpu.make_async_remote_copy(
@@ -674,6 +691,11 @@
             for other in others_in:
                 total = total + other[piece, :].astype(jnp.float32)
             target[piece, :] = total.astype(target.dtype)
+
+    def help(self, part, slot, source, destination):
+        self.helps[part, slot] = self.remote(
+            source, destination, self.help_send.at[part, slot], self.help_recv.at[part, slot],
+            place(self.dp, self.z ^ 1, self.core))
 
     def start_pairs(self, part):
         for turn, line in enumerate(self.lines):
@@ -700,8 +722,28 @@
                 self.pairs[part, turn, slot].wait_recv()
                 here = self.held[part].at[turn, slot]
                 own = self.block(part, self.lines[turn] * 2 + self.core, target)
-                self.add(own, [here], height, here)
-                if slot == 0:
+                arrived = [here]
+                if turn == self.depth - 1 and slot == 0:
+                    self.helps[part, 0].wait_recv()
+                    arrived.append(self.help_in[part])
+                self.add(own, arrived, height, here)
+                if turn == self.depth - 1 and slot in (1, 2):
+                    self.helps[part, slot].wait_recv()
+                    piece = self.held[part].at[turn, slot, pl.ds(half, half)]
+                    self.add(piece, [self.half_in[part].at[slot - 1]], half, piece)
+                if turn == 0 and slot == 0:
+                    self.help(part, 0, here, self.help_in[part])
+                elif turn == 0 and slot < 3:
+                    self.help(
+                        part, slot, self.held[part].at[turn, slot, pl.ds(half, half)],
+                        self.half_in[part].at[slot - 1])
+                    key = (part, turn, slot - 1)
+                    self.planes[key] = self.remote(
+                        self.held[part].at[turn, slot, pl.ds(0, half)],
+                        self.planes_in[part].at[turn, slot - 1, pl.ds(0, half)],
+                        self.plane_send.at[key], self.plane_recv.at[key],
+                        place(self.others[slot - 1], self.z, self.core))
+                elif slot == 0:
                     for position in range(2):
                         key = (part, turn, position)
                         self.crosses[key] = self.remote(
@@ -712,7 +754,7 @@
         if LAG <= index < count + LAG:
             part, turn = self.units[index - LAG]
             half = self.shapes[part][0] // 2
-            for position in range(2):
+            for position in range(2 if turn else 0):
                 self.crosses[part, turn, 1 - position].wait_recv()
                 piece = self.held[part].at[turn, 1 + position, pl.ds(position * half, half)]
                 self.add(piece, [self.crosses_in[part].at[turn, 1 - position]], half, piece)
@@ -725,9 +767,12 @@
             part, turn = self.units[index - 2 * LAG]
             for position in range(2):
                 self.planes[part, turn, position].wait_recv()
+            height = self.shapes[part][0] if turn else self.shapes[part][0] // 2
             here = self.held[part].at[turn, last]
-            arrived = [self.planes_in[part].at[turn, position] for position in range(2)]
-            self.add(here, arrived, self.shapes[part][0], here)
+            piece = self.held[part].at[turn, last, pl.ds(0, height)]
+            arrived = [
+                self.planes_in[part].at[turn, position, pl.ds(0, height)] for position in range(2)]
+            self.add(piece, arrived, height, piece)
             if turn < self.depth - 1:
                 key = (part, turn)
                 self.alongs[key] = self.remote(
@@ -742,24 +787,25 @@
         return total
 
     def wait_sends(self):
-        for copies in (self.planes, self.crosses, self.alongs):
+        for copies in (self.planes, self.crosses, self.alongs, self.helps):
             for copy in copies.values():
                 copy.wait_send()
 
 
 def layer_kernel(rows, depth, *refs):
     sources, live_ref, outs = refs[2:13], refs[13], refs[14:22]
-    landed, results = refs[22:33], refs[33:41]
+    landed = refs[22:33]
+    results = landed[:2] + refs[33:39]
     (
         latents, cotangent, conditioning, ada_ref, ada_bias, qkv_shard, qv_shard, proj_shard,
         proj_bias_shard, fc1_bias_shard, fc2_bias_shard,
     ) = landed
     block_out, latent_grad, ada_grad, qkv_grad, proj_grad, fc1_grad, fc2_grad, small = results
-    mixed_shard, cond_rows, slope, load_sems, store_sems = refs[41:46]
+    mixed_shard, cond_rows, slope, load_sems, store_sems = refs[39:44]
     shards = (mixed_shard, refs[0], refs[1])
-    refs = refs[46:]
+    refs = refs[44:]
     weights, grads = refs[:3], (refs[3], refs[4], refs[3])
-    scatter_buffers, scatter_sems = refs[5:17], refs[17:25]
+    scatter_buffers, scatter_sems = refs[5:23], refs[23:33]
     (
         own_sems, send_sems, recv_sems, swap_send, swap_recv,
         cond_across, cond_own, cond_along, cond_in, part_out, part_across, part_row, part_along,
@@ -767,10 +813,10 @@
         mod, qkv_bias, proj_bias, fc1_bias, fc2_bias, mod_grad, qkv_sums, proj_sums, fc1_sums,
         fc2_sums, inverse_one, inverse_two, normed_one, normed_two, middle, branch, wide,
         hidden_one, hidden_one_t, hidden_two, hidden_two_t, attended, attended_t,
-        grad_mlp, grad_mlp_t, grad_attended, projected,
+        grad_mlp, grad_mlp_t, projected,
         grad_proj_mixed, activated, grad_pre, grad_natural, grad_state, probability,
-    ) = refs[25:]
-    grad_mixed = grad_pre
+    ) = refs[33:]
+    grad_mixed, grad_attended = grad_pre, hidden_one
     mixed, fc1, fc2_turned = weights
     where = positions(rows, depth)
     dp = where[0]
@@ -1281,10 +1327,10 @@
     turned = pltpu.VMEM((D, length), bfloat)
     rest = 128 * columns
     buffers = []
-    for lead in ((depth, rows), (depth, 2), (depth, 2), (depth - 1,)):
+    for lead in ((depth, rows), (depth, 2), (depth, 2), (depth - 1,), (), (2,)):
         for shard in shards:
             height, width = shard.shape
-            height = height // 2 if 6 <= len(buffers) < 9 else height
+            height = height // 2 if len(buffers) // 3 in (2, 5) else height
             buffers.append(pltpu.VMEM(lead + (height, width), bfloat))
     float_out = lambda *shape: jax.ShapeDtypeStruct(shape, jnp.float32)
     outs = [
@@ -1303,7 +1349,7 @@
         in_specs=[anywhere] * 13 + [pl.BlockSpec(memory_space=pltpu.SMEM)],
         out_specs=[anywhere] * 8,
         scratch_shapes=[pltpu.VMEM(source.shape, source.dtype) for source in sources]
-        + [pltpu.VMEM(out.shape, out.dtype) for out in outs]
+        + [pltpu.VMEM(out.shape, out.dtype) for out in outs[2:]]
         + [
             pltpu.VMEM(shards[0].shape, bfloat), row_buffer(rows, cond_pad), wide_row(D),
             dma((len(sources),)), dma((len(outs),)),
@@ -1312,7 +1358,7 @@
         + buffers + [
             dma((3, depth, rows)), dma((3, depth, rows)),
             dma((3, depth, 2)), dma((3, depth, 2)), dma((3, depth, 2)), dma((3, depth, 2)),
-            dma((3, depth - 1)), dma((3, depth - 1)),
+            dma((3, depth - 1)), dma((3, depth - 1)), dma((3, 3)), dma((3, 3)),
             dma((3,)), dma((3 * count,)), dma((2, 3, columns, rows)),
             dma((8, columns)), dma((8, columns)),
             row_buffer(rows, cond_pad), row_buffer(group, cond_pad),
@@ -1331,7 +1377,7 @@
             wide_row(6 * D), wide_row(3 * D), wide_row(D), wide_row(FF), wide_row(D),
             single(1), single(1), single(D), single(D), single(D), single(D), single(FF),
             half(D), turned, half(D), turned, half(D), turned,
-            half(D), turned, half(D), half(3 * D),
+            half(D), turned, half(3 * D),
             half(rest), half(FF), half(FF), half(3 * D), single(D), pltpu.VMEM((HEADS, length, length), jnp.float32),
         ],
         compiler_params=pltpu.CompilerParams(

time: 151 us -> 146 us (0.967)
  Pallas kernels: 149 us -> 145 us
    pallas_call x1, Pallas kernels: 145 us -> 141 us  [run_layer(): pl.pallas_call(functools.partial(layer_kernel, rows, depth), out_shape=ou...]
where the time goes in v6:
time: 146 us
  Pallas kernels  145 us (99%)
  between operations  1.46 us (1%)
    pallas_call x1, Pallas kernels, run_layer(): pl.pallas_call(functools.partial(layer_kernel, rows, depth), out_shape=ou...  141 us
    pallas_call x1, Pallas kernels, emit(): pl.pallas_call(emit_kernel, out_shape=[jax.ShapeDtypeStruct((1, D), jnp.f...  3.79 us

profile of v6, /device:TPU:0, one launch (start us, length us, event | category | flops | bytes accessed | tf_op | source)
XLA Modules:
  0.0 146.2 jit_solution(16535861878887373407)
XLA Ops:
  1.3 140.9 %run_layer.1 = (bf16[256,768]{1,0:T(8,128)(2,1)}, bf16[256,768]{1,0:T(8,128)(2,1)}, f32[192,576]{1,0:T(8,128)}, f32[192,288]{1,0:T(8,128)}, f32[192,96]{1,0:T(8,...) custom-call(bf16[192,384]{1,0:T(8,128)(2,1)} %refs_0_.1, bf16[96,768]{1,0:T(8,128)(2,1)} %bitcast.8, ...), custom_call_target="tpu_custom_call" | custom-call | tf_op jit(solution)/shard_map/run_layer/pallas_call | solution.py:1346
  142.2 3.8 %emit.1 = (f32[1,768]{1,0:T(1,128)}, f32[576]{0:T(1024)}, f32[192]{0:T(256)}, f32[96]{0:T(128)}, f32[384]{0:T(512)}, /*index=5*/f32[96]{0:T(128)}, bf16[256,768]...) custom-call(f32[1,2176]{1,0:T(1,128)} %get-tuple-element.34.refs_0_,, ...), custom_call_target="tpu_custom_call" | custom-call | tf_op jit(solution)/shard_map/emit/pallas_call | solution.py:1291

commit v7 on v6

--- a/solution.py
+++ b/solution.py
@@ -1027,7 +1027,7 @@
         hidden_two[...] = hidden
         hidden_two_t[...] = hidden.T
 
-    chunk = 384
+    chunk = 1536
     chunks = FF // chunk
 
     def expand(low, high):
@@ -1054,17 +1054,17 @@
 
     def after_part_one():
         gather.finish_part(1)
-        expand(0, 4)
+        expand(0, 1)
 
     def send_fc2_grad():
-        fc2_weight_grad(4, 8)
+        fc2_weight_grad(1, 2)
         scatter.start_pairs(2)
 
     hooks = [
         share_condition, normalize_first, start_modulation, None, sum_modulation, None,
         finish_modulation, start_gradient, after_part_zero, lambda: attend(0, 3),
-        lambda: attend(3, 6), finish_attention, after_part_one, lambda: expand(4, 8),
-        lambda: fc2_weight_grad(0, 4), send_fc2_grad,
+        lambda: attend(3, 6), finish_attention, after_part_one, lambda: expand(1, 2),
+        lambda: fc2_weight_grad(0, 1), send_fc2_grad,
     ]
     for index, hook in enumerate(hooks):
         gather.turn(index)
@@ -1229,7 +1229,7 @@
         store(5)
 
     def send_fc1_grad():
-        fc1_weight_grad(4, 8)
+        fc1_weight_grad(1, 2)
         scatter.start_pairs(1)
 
     def send_mixed_grad():
@@ -1237,7 +1237,7 @@
         scatter.start_pairs(0)
 
     hooks = [
-        lambda: fc1_weight_grad(0, 4), send_fc1_grad, hidden_two_back, middle_back,
+        lambda: fc1_weight_grad(0, 1), send_fc1_grad, hidden_two_back, middle_back,
         lambda: attend_back(0, 3), lambda: attend_back(3, 6), send_mixed_grad,
         finish_forward, finish_backward, finish_fc2, share_rows, own_sums, finish_fc1,
         share_back, finish_condition,

time: 146 us -> 141 us (0.966)
  Pallas kernels: 145 us -> 139 us
    pallas_call x1, Pallas kernels: 141 us -> 135 us  [run_layer(): pl.pallas_call(functools.partial(layer_kernel, rows, depth), out_shape=ou...]
where the time goes in v7:
time: 141 us; the launch traced here: 140 us
  Pallas kernels  139 us (99%)
  between operations  1.46 us (1%)
    pallas_call x1, Pallas kernels, run_layer(): pl.pallas_call(functools.partial(layer_kernel, rows, depth), out_shape=ou...  135 us
    pallas_call x1, Pallas kernels, emit(): pl.pallas_call(emit_kernel, out_shape=[jax.ShapeDtypeStruct((1, D), jnp.f...  3.79 us

profile of v7, /device:TPU:0, one launch (start us, length us, event | category | flops | bytes accessed | tf_op | source)
XLA Modules:
  0.0 140.4 jit_solution(14943836842508955516)
XLA Ops:
  1.3 135.1 %run_layer.1 = (bf16[256,768]{1,0:T(8,128)(2,1)}, bf16[256,768]{1,0:T(8,128)(2,1)}, f32[192,576]{1,0:T(8,128)}, f32[192,288]{1,0:T(8,128)}, f32[192,96]{1,0:T(8,...) custom-call(bf16[192,384]{1,0:T(8,128)(2,1)} %refs_0_.1, bf16[96,768]{1,0:T(8,128)(2,1)} %bitcast.8, ...), custom_call_target="tpu_custom_call" | custom-call | tf_op jit(solution)/shard_map/run_layer/pallas_call | solution.py:1346
  136.5 3.8 %emit.1 = (f32[1,768]{1,0:T(1,128)}, f32[576]{0:T(1024)}, f32[192]{0:T(256)}, f32[96]{0:T(128)}, f32[384]{0:T(512)}, /*index=5*/f32[96]{0:T(128)}, bf16[256,768]...) custom-call(f32[1,2176]{1,0:T(1,128)} %get-tuple-element.34.refs_0_,, ...), custom_call_target="tpu_custom_call" | custom-call | tf_op jit(solution)/shard_map/emit/pallas_call | solution.py:1291

commit v8 on v7

--- a/solution.py
+++ b/solution.py
@@ -1261,23 +1261,26 @@
 
 
 def emit_kernel(*refs):
-    small, wholes = refs[0], refs[1:8]
-    cond_grad, rows_out, outs, held, sems = refs[8], refs[9:14], refs[14:21], refs[21:28], refs[28]
+    sources, outs, held, sems = refs[:8], refs[8:21], refs[21:35], refs[35]
     loads = [
-        pltpu.make_async_copy(whole, hold, sems.at[0, at])
-        for at, (whole, hold) in enumerate(zip(wholes, held))]
+        pltpu.make_async_copy(source, hold, sems.at[0, at])
+        for at, (source, hold) in enumerate(zip(sources, held[:1] + held[7:]))]
     stores = [
         pltpu.make_async_copy(hold, out, sems.at[1, at])
-        for at, (hold, out) in enumerate(zip(held, outs))]
+        for at, (hold, out) in enumerate(zip(held[1:], outs))]
     for load in loads:
         load.start()
+    loads[0].wait()
+    small, cond_grad, rows_out = held[0], held[1], held[2:7]
     cond_grad[...] = small[:, :D]
     low = D
     for out in rows_out:
         width = out.shape[0]
         out[...] = small[0, low : low + width]
         low += round_up(width) if low == D else width
-    for load, store in zip(loads, stores):
+    for store in stores[:6]:
+        store.start()
+    for load, store in zip(loads[1:], stores[6:]):
         load.wait()
         store.start()
     for store in stores:
@@ -1285,18 +1288,18 @@
 
 
 def emit(small, wholes, widths):
-    vmem = pl.BlockSpec(memory_space=pltpu.VMEM)
     anywhere = pl.BlockSpec(memory_space=pl.ANY)
-    count = len(wholes)
+    outs = [jax.ShapeDtypeStruct((1, D), jnp.float32)]
+    outs += [jax.ShapeDtypeStruct((width,), jnp.float32) for width in widths]
+    outs += [jax.ShapeDtypeStruct(whole.shape, whole.dtype) for whole in wholes]
     return pl.pallas_call(
         emit_kernel,
-        out_shape=[jax.ShapeDtypeStruct((1, D), jnp.float32)]
-        + [jax.ShapeDtypeStruct((width,), jnp.float32) for width in widths]
-        + [jax.ShapeDtypeStruct(whole.shape, whole.dtype) for whole in wholes],
-        in_specs=[vmem] + [anywhere] * count,
-        out_specs=[vmem] * (1 + len(widths)) + [anywhere] * count,
-        scratch_shapes=[pltpu.VMEM(whole.shape, whole.dtype) for whole in wholes]
-        + [pltpu.SemaphoreType.DMA((2, count))],
+        out_shape=outs,
+        in_specs=[anywhere] * (1 + len(wholes)),
+        out_specs=[anywhere] * len(outs),
+        scratch_shapes=[pltpu.VMEM(small.shape, small.dtype)]
+        + [pltpu.VMEM(out.shape, out.dtype) for out in outs]
+        + [pltpu.SemaphoreType.DMA((2, len(outs)))],
         name="emit",
     )(small, *wholes)
 

time: 141 us -> 140 us (level)
  no operation moved by 1% of the time
where the time goes in v8:
time: 140 us; the launch traced here: 139 us
  Pallas kernels  138 us (99%)
  between operations  1.46 us (1%)
    pallas_call x1, Pallas kernels, run_layer(): pl.pallas_call(functools.partial(layer_kernel, rows, depth), out_shape=ou...  135 us

profile of v8, /device:TPU:0, one launch (start us, length us, event | category | flops | bytes accessed | tf_op | source)
XLA Modules:
  0.0 139.2 jit_solution(2272937887914867549)
XLA Ops:
  1.3 135.1 %run_layer.1 = (bf16[256,768]{1,0:T(8,128)(2,1)}, bf16[256,768]{1,0:T(8,128)(2,1)}, f32[192,576]{1,0:T(8,128)}, f32[192,288]{1,0:T(8,128)}, f32[192,96]{1,0:T(8,...) custom-call(bf16[192,384]{1,0:T(8,128)(2,1)} %refs_0_.1, bf16[96,768]{1,0:T(8,128)(2,1)} %bitcast.8, ...), custom_call_target="tpu_custom_call" | custom-call | tf_op jit(solution)/shard_map/run_layer/pallas_call | solution.py:1349
  136.5 2.6 %emit.1 = (f32[1,768]{1,0:T(1,128)}, f32[576]{0:T(1024)}, f32[192]{0:T(256)}, f32[96]{0:T(128)}, f32[384]{0:T(512)}, /*index=5*/f32[96]{0:T(128)}, bf16[256,768]...) custom-call(f32[1,2176]{1,0:T(1,128)} %get-tuple-element.34.refs_0_,, ...), custom_call_target="tpu_custom_call" | custom-call | tf_op jit(solution)/shard_map/emit/pallas_call | solution.py:1295
